TPU v7x, 32 devices: a whole 2x2x4 slice. The times are simulated.
32 devices in a mesh: dp: 4 (over x, core), expert: 8 (over z, y).
Axes of the slice: x: 2, y: 2, z: 4, core: 2. Of those that a mesh axis runs over, the one named last changes fastest.
Arguments:
- hidden_states: bfloat16 [4096, 2880], P(('dp', 'expert')), may hold values from -12 to 12
- route_ids: int32 [4096, 4], P(('dp', 'expert')), may hold values from 0 to 7, all different within a row; in each aligned block of 128 rows (0 to 127, 128 to 255, ...) at most 68 rows name the same one
- route_weights: bfloat16 [4096, 4], P(('dp', 'expert')), may hold values from 0.099609375 to 0.59765625
- gate_up_proj: bfloat16 [8, 1440, 2, 2880], P('expert', 'dp'), may hold values from -0.109375 to 0.109375
- down_proj: bfloat16 [8, 1440, 2880], P('expert', 'dp'), may hold values from -0.15625 to 0.15625
Outputs:
- moe_output: bfloat16 [4096, 2880], P(('dp', 'expert'))
Inputs may be any that keep to these rules, and one draw needn't show every extreme that they name: `route_ids`: each token names 4 different experts. Among the tokens of one device (aligned blocks of 128 tokens) no expert is named more than 68 times, and in some block an expert is named exactly 68 times.
All inputs are finite; a program needn't handle non-finite values.
Results may differ from a plain program's by a relative error of at most 0.0057.
Values may be sent and summed in bfloat16 or wider, within the bound.
No kernel may reach another device: no remote copies, remote signals or barrier semaphores. Data moves between devices by JAX's collectives and lax.ppermute only.
A program may use at most 192 MiB of HBM per device.

v0:
```python
import jax
import jax.numpy as jnp
from jax import lax
from jax.sharding import PartitionSpec as P

clamp_limit = 7.0


def route_tables(ids, weights, slots_total, capacity):
    tok_rows, top_count = ids.shape
    flat_ids = ids.reshape(tok_rows * top_count)
    position = jnp.arange(tok_rows * top_count, dtype=jnp.int32)
    earlier = (flat_ids[:, None] == flat_ids[None, :]) & (position[None, :] < position[:, None])
    rank_in = jnp.sum(earlier.astype(jnp.int32), axis=1)
    slot_index = (flat_ids * capacity + rank_in).reshape(tok_rows, top_count)
    onehot = slot_index[:, :, None] == jnp.arange(slots_total, dtype=jnp.int32)[None, None, :]
    chosen = jnp.any(onehot, axis=1).astype(jnp.bfloat16)
    weighted = jnp.sum(jnp.where(onehot, weights[:, :, None].astype(jnp.float32), 0.0), axis=1)
    return (chosen, weighted)


def clamped_glu(rows, piece):
    gate_values = jnp.einsum(
        "secd,efd->secf", rows, piece[:, :, 0], preferred_element_type=jnp.float32
    )
    upper_values = jnp.einsum(
        "secd,efd->secf", rows, piece[:, :, 1], preferred_element_type=jnp.float32
    )
    gate_values = jnp.minimum(gate_values, clamp_limit)
    upper_values = jnp.clip(upper_values, -clamp_limit, clamp_limit)
    return ((upper_values + 1.0) * gate_values * jax.nn.sigmoid(1.702 * gate_values)).astype(
        jnp.bfloat16
    )


def local(hidden_states, route_ids, route_weights, gate_up_proj, down_proj):
    tok_rows = hidden_states.shape[0]
    top_count = route_ids.shape[1]
    local_experts = gate_up_proj.shape[0]
    owners = lax.axis_size("expert")
    experts_all = local_experts * owners
    capacity = max(2, 17 * tok_rows * top_count // (16 * experts_all))
    slots_total = experts_all * capacity
    chosen, weighted = route_tables(route_ids, route_weights, slots_total, capacity)
    selection = chosen.reshape(tok_rows, owners, local_experts, capacity)
    outgoing = jnp.einsum(
        "toec,td->oecd", selection, hidden_states, preferred_element_type=jnp.float32
    ).astype(jnp.bfloat16)
    arrived = lax.all_to_all(outgoing, "expert", split_axis=0, concat_axis=0, tiled=True)
    hidden = clamped_glu(arrived, lax.all_gather(gate_up_proj, "dp", axis=1, tiled=True))
    expert_out = jnp.einsum(
        "secf,efd->secd",
        hidden,
        lax.all_gather(down_proj, "dp", axis=1, tiled=True),
        preferred_element_type=jnp.float32,
    )
    returned = lax.all_to_all(
        expert_out.astype(jnp.bfloat16), "expert", split_axis=0, concat_axis=0, tiled=True
    )
    table = weighted.reshape(tok_rows, owners, local_experts, capacity).astype(jnp.bfloat16)
    result = jnp.einsum("toec,oecd->td", table, returned, preferred_element_type=jnp.float32)
    return result.astype(jnp.bfloat16)


def solution(mesh):
    placed = (
        P(("dp", "expert"), None),
        P(("dp", "expert"), None),
        P(("dp", "expert"), None),
        P("expert", "dp", None, None),
        P("expert", "dp", None),
    )
    return jax.shard_map(
        local, mesh=mesh, in_specs=placed, out_specs=P(("dp", "expert"), None), check_vma=False
    )
```

profile of v0, /device:TPU:0, one launch (start us, length us, event | category | flops | bytes accessed | tf_op | source)
XLA Modules:
  0.0 294.9 jit_solution(14371936626505706944)
XLA Ops:
  6.5 0.0 copy-start
  6.5 0.0 all-gather.3.cloned.1.call-start
  6.5 4.7 %copy.31 = bf16[1,360,2,2880]{3,1,2,0:T(8,128)(2,1)} copy(bf16[1,360,2,2880]{3,2,1,0:T(2,128)(2,1)} %param.8) | data formatting | bytes 8294400 | tf_op args[3]
  11.2 0.0 all-gather.3.cloned.1.call-update
  11.3 0.0 all-gather.5.cloned.1.call-start
  11.3 0.7 all-gather.5.cloned.1.call-update
  12.0 0.0 copy-done.1
  12.0 0.1 copy.28
  12.1 0.1 eq.28
  12.2 0.3 convert_reduce_fusion
  12.5 0.1 reduce_sum.21
  12.6 0.1 copy.29
  12.7 0.1 fusion.20
  12.9 0.0 copy-done
  12.9 1.0 fusion.10
  13.9 83.2 %all_to_all.10 = bf16[8,1,68,2880]{3,2,1,0:T(8,128)(2,1)} all-to-all(bf16[8,1,68,2880]{3,2,1,0:T(8,128)(2,1)S(1)} %fusion.10), channel_id=1, replica_groups=mesh['dp'=4,'expert'=8] {'expert'}, dimensions={0} | all-to-all | bytes 6266880 | tf_op jit(solution)/shard_map/all_to_all | solution.py:49
  97.1 24.1 %all-gather.3.cloned.1.call-done = bf16[1,1440,2,2880]{3,1,2,0:T(8,128)(2,1)} async-done(((bf16[1,360,2,2880]{3,1,2,0:T(8,128)(2,1)}), bf16[1,1440,2,2880]{3,1,2,0:T(8,128)(2,1)}) %all-gather.3.cloned.1.call-update) | async-done | bytes 16588816 | tf_op jit(solution)/shard_map/all_gather | solution.py:50
  121.2 11.1 %fusion.11 = f32[8,68,1440]{2,1,0:T(8,128)} fusion(bf16[1,1440,2,2880]{3,1,2,0:T(8,128)(2,1)} %all-gather.3.cloned.1.call-done, bf16[8,1,68,2880]{3,2,1,0:T(8,128)(2,1)} %all_to_all.10), kind=kOutput, calls=%fused_computation.11 | convolution fusion | flops 4512936960 | bytes 15003648 | tf_op jit(solution)/shard_map/secd,efd->secf/dot_general | solution.py:26
  132.3 49.3 %all-gather.5.cloned.1.call-done = bf16[1,1440,2880]{2,1,0:T(8,128)(2,1)} async-done(((bf16[1,360,2880]{2,1,0:T(8,128)(2,1)}), bf16[1,1440,2880]{2,1,0:T(8,128)(2,1)}) %all-gather.5.cloned.1.call-update) | async-done | bytes 8294416 | tf_op jit(solution)/shard_map/all_gather | solution.py:54
  181.6 20.0 %fusion.7 = bf16[8,1,68,2880]{3,2,1,0:T(8,128)(2,1)} fusion(bf16[1,1440,2880]{2,1,0:T(8,128)(2,1)} %all-gather.5.cloned.1.call-done, f32[8,68,1440]{2,1,0:T(8,128)} %fusion.11, bf16[1,1440,2,2880]{3,1,2,0:T(8,128)(2,1)} %all-gather.3.cloned.1.call-done, bf16[8,1,68,2880]{3,2,1,0:T(8,128)(2,1)} %all_to_all.10), kind=kOutput, calls=%fused_computation.8 | convolution fusion | flops 9032924160 | bytes 27021312 | tf_op jit(solution)/shard_map/secf,efd->secd/dot_general | solution.py:51
  201.6 5.6 %all-to-all-start.1 = ((bf16[8,1,68,2880]{3,2,1,0:T(8,128)(2,1)}), bf16[8,1,68,2880]{3,2,1,0:T(8,128)(2,1)}, u32[]{:S(2)}, u32[]{:S(2)}) async-start(bf16[8,1,68,2880]{3,2,1,0:T(8,128)(2,1)} %fusion.7), calls=%async_computation.1 | async-start | bytes 6782976 | tf_op jit(solution)/shard_map/all_to_all | solution.py:57
  207.2 0.1 select_reduce_fusion
  207.4 76.3 %all-to-all-done.1 = bf16[8,1,68,2880]{3,2,1,0:T(8,128)(2,1)} async-done(((bf16[8,1,68,2880]{3,2,1,0:T(8,128)(2,1)}), bf16[8,1,68,2880]{3,2,1,0:T(8,128)(2,1)}, u32[]{:S(2)}, u32[]{:S(2)}) %all-to-all-start.1) | async-done | bytes 3133472 | tf_op jit(solution)/shard_map/all_to_all | solution.py:57
  283.7 4.3 %fusion.12 = bf16[128,2880]{0,1:T(8,128)(2,1)} fusion(bf16[128,8,68]{0,2,1:T(8,128)(2,1)S(1)} %convert_element_type.44, bf16[8,1,68,2880]{3,2,1,0:T(8,128)(2,1)} %all-to-all-done.1), kind=kOutput, calls=%fused_computation.12 | convolution fusion | flops 401448960 | bytes 4009984 | tf_op jit(solution)/shard_map/toec,oecd->td/dot_general | solution.py:61
  (7 shorter events, 0.1 us)
Async XLA Ops:
  6.5 6.3 %copy-start = (bf16[128,2880]{0,1:T(8,128)(2,1)S(1)}, bf16[128,2880]{0,1:T(8,128)(2,1)}, u32[]{:S(2)}) copy-start(bf16[128,2880]{0,1:T(8,128)(2,1)} %param.5) | copy-start | bytes 2211844
  6.5 114.7 %all-gather.3.cloned.1.call-start = ((), (), s32[]{:S(2)}) async-start(), calls=%async_computation.2 | async-start | bytes 21196800 | tf_op jit(solution)/shard_map/all_gather | solution.py:50
  11.2 0.8 copy-start.1
  11.3 170.4 %all-gather.5.cloned.1.call-start = ((), (), s32[]{:S(2)}) async-start(), calls=%async_computation.3 | async-start | bytes 10598400 | tf_op jit(solution)/shard_map/all_gather | solution.py:54
  201.6 5.7 %copy-start.2 = (bf16[128,4]{0,1:T(4,128)(2,1)S(1)}, bf16[128,4]{0,1:T(4,128)(2,1)}, u32[]{:S(2)}) copy-start(bf16[128,4]{0,1:T(4,128)(2,1)} %param.7) | copy-start | bytes 3076
  201.6 82.2 %all-to-all-start.1 = ((bf16[8,1,68,2880]{3,2,1,0:T(8,128)(2,1)}), bf16[8,1,68,2880]{3,2,1,0:T(8,128)(2,1)}, u32[]{:S(2)}, u32[]{:S(2)}) async-start(bf16[8,1,68,2880]{3,2,1,0:T(8,128)(2,1)} %fusion.7), calls=%async_computation.1 | async-start | bytes 6782976 | tf_op jit(solution)/shard_map/all_to_all | solution.py:57
Sparse Core Ops, SparseCore 0:
  11.4 109.8 all-gather.2
  122.8 58.7 all-gather.4
where the time goes:
time: 295 us
  waiting for transfers between devices  150 us (51%)
  blocking collectives  83.2 us (28%)
  matrix products  36.4 us (12%)
  between operations  13.5 us (5%)
  starting transfers between devices  5.69 us (2%)
  local copies, waits for them, and re-layouts  5.15 us (2%)
    all_to_all x1, blocking collectives, local(): lax.all_to_all(outgoing, 'expert', split_axis=0, concat_axis=0, tiled=True)  83.2 us
    all_to_all x1, waiting for transfers between devices, local(): lax.all_to_all(expert_out.astype(jnp.bfloat16), 'expert', split_axis=0, c...  76.3 us
    all_gather x1, waiting for transfers between devices, local(): lax.all_gather(down_proj, 'dp', axis=1, tiled=True)  49.3 us
    all_gather x1, waiting for transfers between devices, local(): lax.all_gather(gate_up_proj, 'dp', axis=1, tiled=True)  24.1 us
    dot_general x1, matrix products, local(): jnp.einsum('secf,efd->secd', hidden, lax.all_gather(down_proj, 'dp', axis...  20 us
    dot_general x1, matrix products, clamped_glu(): jnp.einsum('secd,efd->secf', rows, piece[:, :, 1], preferred_element_type...  11.1 us
  transfers between devices with their start and end apart: 3, of which 3 were waited for; matrix products, arithmetic and copies ran while one was open for 4% of the time, Pallas kernels for 0%

commit v1 on v0

v1 whole, which is shorter than its diff:
```python
import functools

import jax
import jax.numpy as jnp
from jax import lax
from jax.experimental import pallas as pl
from jax.experimental.pallas import tpu as pltpu
from jax.sharding import PartitionSpec as P

clamp_limit = 7.0
AXES = ("dp", "expert")
VMEM_LIMIT = 40 * 1024 * 1024


def chunk_bounds(total, parts, unit):
    step = -(-total // (parts * unit)) * unit
    return [(low, min(low + step, total)) for low in range(0, total, step)]


def sent_to(array, target):
    dp_size, expert_size = lax.axis_size("dp"), lax.axis_size("expert")
    pairs = []
    for d in range(dp_size):
        for e in range(expert_size):
            td, te = target(d, e)
            pairs.append((d * expert_size + e, td * expert_size + te))
    return lax.ppermute(array, AXES, pairs)


def to_other_core(array):
    return sent_to(array, lambda d, e: (d ^ 1, e))


def to_chip(array, step):
    dp_size = lax.axis_size("dp")
    return sent_to(array, lambda d, e: ((d + 2 * step) % dp_size, e))


def to_expert(array, offset):
    return sent_to(array, lambda d, e: (d, e ^ offset))


def call_kernel(body, out_shapes, args, flops):
    moved = sum(a.size * a.dtype.itemsize for a in args) + sum(s.size * s.dtype.itemsize for s in out_shapes)
    return pl.pallas_call(
        body,
        out_shape=out_shapes,
        in_specs=[pl.BlockSpec(memory_space=pltpu.VMEM)] * len(args),
        out_specs=[pl.BlockSpec(memory_space=pltpu.VMEM)] * len(out_shapes),
        compiler_params=pltpu.CompilerParams(vmem_limit_bytes=VMEM_LIMIT),
        cost_estimate=pl.CostEstimate(flops=flops, bytes_accessed=moved, transcendentals=0),
    )(*args)


def pick_kernel(groups, sel_ref, hid_ref, *out_refs):
    hid = hid_ref[...]
    for k in range(groups):
        out_refs[k][...] = jnp.dot(sel_ref[k], hid, preferred_element_type=jnp.float32).astype(jnp.bfloat16)


def down_kernel(shards, *refs):
    hidden_refs, weight_refs, out_refs = refs[:shards], refs[shards : 2 * shards], refs[2 * shards :]
    total = jnp.dot(hidden_refs[0][...], weight_refs[0][...], preferred_element_type=jnp.float32)
    for s in range(1, shards):
        total += jnp.dot(hidden_refs[s][...], weight_refs[s][...], preferred_element_type=jnp.float32)
    rows = total.shape[0] // len(out_refs)
    for k, out_ref in enumerate(out_refs):
        out_ref[...] = total[k * rows : (k + 1) * rows].astype(jnp.bfloat16)


def combine_kernel(groups, table_ref, *refs):
    total = jnp.dot(table_ref[0], refs[0][...], preferred_element_type=jnp.float32)
    for k in range(1, groups):
        total += jnp.dot(table_ref[k], refs[k][...], preferred_element_type=jnp.float32)
    refs[groups][...] = total.astype(jnp.bfloat16)


def glu(rows, weights):
    gate = lax.dot_general(rows, weights[0], (((1,), (1,)), ((), ())), preferred_element_type=jnp.float32)
    upper = lax.dot_general(rows, weights[1], (((1,), (1,)), ((), ())), preferred_element_type=jnp.float32)
    gate = jnp.minimum(gate, clamp_limit)
    upper = jnp.clip(upper, -clamp_limit, clamp_limit)
    return ((upper + 1.0) * gate * jax.nn.sigmoid(1.702 * gate)).astype(jnp.bfloat16)


def local(hidden_states, route_ids, route_weights, gate_up_proj, down_proj):
    tok_rows, width = hidden_states.shape
    top_count = route_ids.shape[1]
    units = gate_up_proj.shape[1]
    groups = lax.axis_size("expert")
    chips = lax.axis_size("dp") // 2
    capacity = max(2, 17 * tok_rows * top_count // (16 * groups))
    slots = -(-capacity // 8) * 8
    me = lax.axis_index("expert")

    pieces = [(0, 2 * units // 3 // 8 * 8), (2 * units // 3 // 8 * 8, units)]
    own_gu = [jnp.transpose(gate_up_proj[0, a:b], (1, 0, 2)) for a, b in pieces]
    chunks = chunk_bounds(width, 4, 128)
    own_dn = [down_proj[0, :, a:b] for a, b in chunks]
    far_gu = [[to_chip(p, s) for p in own_gu] for s in range(1, chips)]
    far_dn = [[to_chip(c, s) for c in own_dn] for s in range(1, chips)]
    gu = [own_gu, [to_other_core(p) for p in own_gu]]
    dn = [own_dn, [to_other_core(c) for c in own_dn]]
    for s in range(chips - 1):
        gu += [far_gu[s], [to_other_core(p) for p in far_gu[s]]]
        dn += [far_dn[s], [to_other_core(c) for c in far_dn[s]]]

    near = (route_ids ^ me)[:, :, None] == jnp.arange(groups, dtype=jnp.int32)
    member = jnp.any(near, axis=1)
    weight = jnp.sum(jnp.where(near, route_weights[:, :, None].astype(jnp.float32), 0.0), axis=1)
    before = jnp.tril(jnp.ones((tok_rows, tok_rows), jnp.bfloat16), -1)
    rank = jnp.dot(before, member.astype(jnp.bfloat16), preferred_element_type=jnp.float32).astype(jnp.int32)
    rank = jnp.where(member, rank, -1)
    chosen = rank.T[:, None, :] == jnp.arange(slots, dtype=jnp.int32)[None, :, None]
    table = jnp.where(rank.T[:, :, None] == jnp.arange(slots, dtype=jnp.int32), weight.T[:, :, None], 0.0)
    table = table.astype(jnp.bfloat16)

    outgoing = call_kernel(
        functools.partial(pick_kernel, groups),
        [jax.ShapeDtypeStruct((slots, width), jnp.bfloat16)] * groups,
        (chosen.astype(jnp.bfloat16), hidden_states),
        2 * groups * slots * tok_rows * width,
    )
    arrived = [outgoing[0]] + [to_expert(outgoing[k], k) for k in range(1, groups)]
    rows = jnp.concatenate(arrived, axis=0)

    hidden = [jnp.concatenate([glu(rows, p) for p in shard], axis=1) for shard in gu]
    results = []
    for j, (a, b) in enumerate(chunks):
        outs = call_kernel(
            functools.partial(down_kernel, len(dn)),
            [jax.ShapeDtypeStruct((slots, b - a), jnp.bfloat16)] * groups,
            (*hidden, *[shard[j] for shard in dn]),
            2 * groups * slots * units * len(dn) * (b - a),
        )
        returned = [outs[0]] + [to_expert(outs[k], k) for k in range(1, groups)]
        results += call_kernel(
            functools.partial(combine_kernel, groups),
            [jax.ShapeDtypeStruct((tok_rows, b - a), jnp.bfloat16)],
            (table, *returned),
            2 * groups * slots * tok_rows * (b - a),
        )
    return jnp.concatenate(results, axis=1)


def solution(mesh):
    placed = (
        P(("dp", "expert"), None),
        P(("dp", "expert"), None),
        P(("dp", "expert"), None),
        P("expert", "dp", None, None),
        P("expert", "dp", None),
    )
    return jax.shard_map(
        local, mesh=mesh, in_specs=placed, out_specs=P(("dp", "expert"), None), check_vma=False
    )
```

time: 295 us -> 285 us (0.966)
  blocking collectives: 83.2 us -> 0 us
  starting transfers between devices: 5.69 us -> 80.6 us
  between operations: 13.5 us -> 0.45 us
  matrix products: 36.4 us -> 24.4 us
  Pallas kernels: 0 us -> 11.1 us
  waiting for transfers between devices: 150 us -> 158 us
    ppermute x0 -> x53, waiting for transfers between devices: none -> 158 us  [sent_to(): return lax.ppermute(array, AXES, pairs)]
    all_to_all x1 -> x0, blocking collectives: 83.2 us -> none  [local(): lax.all_to_all(outgoing, 'expert', split_axis=0, concat_axis=0, tiled=True)]
    ppermute x0 -> x53, starting transfers between devices: none -> 80.6 us  [sent_to(): return lax.ppermute(array, AXES, pairs)]
    all_to_all x1 -> x0, waiting for transfers between devices: 76.3 us -> none  [local(): lax.all_to_all(expert_out.astype(jnp.bfloat16), 'expert', split_axis=0, c...]
    all_gather x2 -> x0, waiting for transfers between devices: 73.4 us -> none  [the longest x1 49.3 us: local(): lax.all_gather(down_proj, 'dp', axis=1, tiled=True)]
    dot_general x4 -> x17, matrix products: 36.4 us -> 24.4 us  [the longest x8 12.2 us: glu(): lax.dot_general(rows, weights[0], (((1,), (1,)), ((), ())), preferred_ele...]
    pallas_call x0 -> x9, Pallas kernels: none -> 11.1 us  [call_kernel(): pl.pallas_call(body, out_shape=out_shapes, in_specs=[pl.BlockSpec(memory_...]
    all_to_all x1 -> x0, starting transfers between devices: 5.65 us -> none  [local(): lax.all_to_all(expert_out.astype(jnp.bfloat16), 'expert', split_axis=0, c...]
  transfers between devices with their start and end apart: 3 -> 53, of which waited for: 3 -> 16; matrix products, arithmetic and copies ran while one was open for 4% -> 10% of each run, Pallas kernels for 0% -> 4%
where the time goes in v1:
time: 285 us; the launch traced here: 283 us
  waiting for transfers between devices  158 us (55%)
  starting transfers between devices  80.6 us (28%)
  matrix products  24.4 us (9%)
  Pallas kernels  11.1 us (4%)
  local copies, waits for them, and re-layouts  7.69 us (3%)
    ppermute x53, waiting for transfers between devices, sent_to(): return lax.ppermute(array, AXES, pairs)  158 us
    ppermute x53, starting transfers between devices, sent_to(): return lax.ppermute(array, AXES, pairs)  80.6 us
    dot_general x8, matrix products, glu(): lax.dot_general(rows, weights[0], (((1,), (1,)), ((), ())), preferred_ele...  12.2 us
    dot_general x8, matrix products, glu(): lax.dot_general(rows, weights[1], (((1,), (1,)), ((), ())), preferred_ele...  12.1 us
    pallas_call x9, Pallas kernels, call_kernel(): pl.pallas_call(body, out_shape=out_shapes, in_specs=[pl.BlockSpec(memory_...  11.1 us
  transfers between devices with their start and end apart: 53, of which 16 were waited for; matrix products, arithmetic and copies ran while one was open for 10% of the time, Pallas kernels for 4%

profile of v1, /device:TPU:0, one launch (start us, length us, event | category | flops | bytes accessed | tf_op | source)
XLA Modules:
  0.0 283.3 jit_solution(8366957514327039564)
XLA Ops:
  14.3 6.2 %collective-permute-done = bf16[72,2880]{1,0:T(8,128)(2,1)S(1)} collective-permute-done((bf16[72,2880]{1,0:T(8,128)(2,1)S(1)}, bf16[72,2880]{1,0:T(8,128)(2,1)S(1)}, u32[]{:S(2)}, u32[]{:S(2)}) %collective-permute-start) | collective-permute-done | bytes 414752 | tf_op jit(solution)/shard_map/ppermute | solution.py:27
  20.5 2.6 collective-permute-start.3
  25.3 13.8 %collective-permute-done.2 = bf16[72,2880]{1,0:T(8,128)(2,1)S(1)} collective-permute-done((bf16[72,2880]{1,0:T(8,128)(2,1)S(1)}, bf16[72,2880]{1,0:T(8,128)(2,1)S(1)}, u32[]{:S(2)}, u32[]{:S(2)}) %collective-permute-start.2) | collective-permute-done | bytes 414752 | tf_op jit(solution)/shard_map/ppermute | solution.py:27
  40.5 20.8 %collective-permute-done.3 = bf16[72,2880]{1,0:T(8,128)(2,1)S(1)} collective-permute-done((bf16[72,2880]{1,0:T(8,128)(2,1)S(1)}, bf16[72,2880]{1,0:T(8,128)(2,1)S(1)}, u32[]{:S(2)}, u32[]{:S(2)}) %collective-permute-start.3) | collective-permute-done | bytes 414752 | tf_op jit(solution)/shard_map/ppermute | solution.py:27
  61.3 4.6 %collective-permute-start.6 = (bf16[72,2880]{1,0:T(8,128)(2,1)S(1)}, bf16[72,2880]{1,0:T(8,128)(2,1)S(1)}, u32[]{:S(2)}, u32[]{:S(2)}) collective-permute-start(bf16[72,2880]{1,0:T(8,128)(2,1)S(1)} %get-tuple-element.52), channel_id=1, source_target_pairs={{0,7},{1,6},{2,5},{3,4},{4,3},{5,2},{6,1},{7,0},{8,15},{9,14},{10,... | collective-permute-start | bytes 1244168 | tf_op jit(solution)/shard_map/ppermute | solution.py:27
  65.9 14.5 %collective-permute-done.4 = bf16[72,2880]{1,0:T(8,128)(2,1)S(1)} collective-permute-done((bf16[72,2880]{1,0:T(8,128)(2,1)S(1)}, bf16[72,2880]{1,0:T(8,128)(2,1)S(1)}, u32[]{:S(2)}, u32[]{:S(2)}) %collective-permute-start.4) | collective-permute-done | bytes 414752 | tf_op jit(solution)/shard_map/ppermute | solution.py:27
  96.4 48.2 %collective-permute-done.9 = bf16[2,240,2880]{2,1,0:T(8,128)(2,1)S(1)} collective-permute-done((bf16[2,240,2880]{2,1,0:T(8,128)(2,1)S(1)}, bf16[2,240,2880]{2,1,0:T(8,128)(2,1)S(1)}, u32[]{:S(2)}, u32[]{:S(2)}) %collective-permute-start.9) | collective-permute-done | bytes 2764832 | tf_op jit(solution)/shard_map/ppermute | solution.py:27
  159.0 8.5 %collective-permute-done.34.refs_6_ = bf16[360,768]{1,0:T(8,128)(2,1)S(1)} collective-permute-done((bf16[360,768]{1,0:T(8,128)(2,1)S(1)}, bf16[360,768]{1,0:T(8,128)(2,1)S(1)}, u32[]{:S(2)}, u32[]{:S(2)}) %collective-permute-start.34) | collective-permute-done | bytes 552992 | tf_op jit(solution)/shard_map/ppermute | solution.py:27
  167.6 11.8 %collective-permute-done.24.refs_6_ = bf16[360,768]{1,0:T(8,128)(2,1)S(1)} collective-permute-done((bf16[360,768]{1,0:T(8,128)(2,1)S(1)}, bf16[360,768]{1,0:T(8,128)(2,1)S(1)}, u32[]{:S(2)}, u32[]{:S(2)}) %collective-permute-start.24) | collective-permute-done | bytes 552992 | tf_op jit(solution)/shard_map/ppermute | solution.py:27
  179.4 10.9 %collective-permute-done.14.refs_6_ = bf16[360,768]{1,0:T(8,128)(2,1)S(1)} collective-permute-done((bf16[360,768]{1,0:T(8,128)(2,1)S(1)}, bf16[360,768]{1,0:T(8,128)(2,1)S(1)}, u32[]{:S(2)}, u32[]{:S(2)}) %collective-permute-start.14) | collective-permute-done | bytes 552992 | tf_op jit(solution)/shard_map/ppermute | solution.py:27
  194.6 10.0 %collective-permute-start.47 = (bf16[72,576]{1,0:T(8,128)(2,1)S(1)}, bf16[72,576]{1,0:T(8,128)(2,1)S(1)}, u32[]{:S(2)}, u32[]{:S(2)}) collective-permute-start(bf16[72,576]{1,0:T(8,128)(2,1)S(1)} %get-tuple-element.79), channel_id=1, source_target_pairs={{0,2},{1,3},{2,0},{3,1},{4,6},{5,7},{6,4},{7,5},{8,10},{9,11},{10,... | collective-permute-start | bytes 248840 | tf_op jit(solution)/shard_map/ppermute | solution.py:27
  208.2 3.9 %collective-permute-start.49 = (bf16[72,576]{1,0:T(8,128)(2,1)S(1)}, bf16[72,576]{1,0:T(8,128)(2,1)S(1)}, u32[]{:S(2)}, u32[]{:S(2)}) collective-permute-start(bf16[72,576]{1,0:T(8,128)(2,1)S(1)} %get-tuple-element.81), channel_id=1, source_target_pairs={{0,4},{1,5},{2,6},{3,7},{4,0},{5,1},{6,2},{7,3},{8,12},{9,13},{10,... | collective-permute-start | bytes 248840 | tf_op jit(solution)/shard_map/ppermute | solution.py:27
  216.9 5.7 %collective-permute-done.49.refs_4_ = bf16[72,576]{1,0:T(8,128)(2,1)S(1)} collective-permute-done((bf16[72,576]{1,0:T(8,128)(2,1)S(1)}, bf16[72,576]{1,0:T(8,128)(2,1)S(1)}, u32[]{:S(2)}, u32[]{:S(2)}) %collective-permute-start.49) | collective-permute-done | bytes 82976 | tf_op jit(solution)/shard_map/ppermute | solution.py:27
  224.4 4.5 %collective-permute-start.39 = (bf16[72,768]{1,0:T(8,128)(2,1)S(1)}, bf16[72,768]{1,0:T(8,128)(2,1)S(1)}, u32[]{:S(2)}, u32[]{:S(2)}) collective-permute-start(bf16[72,768]{1,0:T(8,128)(2,1)S(1)} %get-tuple-element.73), channel_id=1, source_target_pairs={{0,4},{1,5},{2,6},{3,7},{4,0},{5,1},{6,2},{7,3},{8,12},{9,13},{10,... | collective-permute-start | bytes 331784 | tf_op jit(solution)/shard_map/ppermute | solution.py:27
  228.9 3.1 %collective-permute-start.40 = (bf16[72,768]{1,0:T(8,128)(2,1)S(1)}, bf16[72,768]{1,0:T(8,128)(2,1)S(1)}, u32[]{:S(2)}, u32[]{:S(2)}) collective-permute-start(bf16[72,768]{1,0:T(8,128)(2,1)S(1)} %get-tuple-element.74), channel_id=1, source_target_pairs={{0,5},{1,4},{2,7},{3,6},{4,1},{5,0},{6,3},{7,2},{8,13},{9,12},{10,... | collective-permute-start | bytes 331784 | tf_op jit(solution)/shard_map/ppermute | solution.py:27
  234.5 3.2 %collective-permute-start.42 = (bf16[72,768]{1,0:T(8,128)(2,1)S(1)}, bf16[72,768]{1,0:T(8,128)(2,1)S(1)}, u32[]{:S(2)}, u32[]{:S(2)}) collective-permute-start(bf16[72,768]{1,0:T(8,128)(2,1)S(1)} %get-tuple-element.76), channel_id=1, source_target_pairs={{0,7},{1,6},{2,5},{3,4},{4,3},{5,2},{6,1},{7,0},{8,15},{9,14},{10,... | collective-permute-start | bytes 331784 | tf_op jit(solution)/shard_map/ppermute | solution.py:27
  240.0 3.3 %collective-permute-done.40.refs_5_ = bf16[72,768]{1,0:T(8,128)(2,1)S(1)} collective-permute-done((bf16[72,768]{1,0:T(8,128)(2,1)S(1)}, bf16[72,768]{1,0:T(8,128)(2,1)S(1)}, u32[]{:S(2)}, u32[]{:S(2)}) %collective-permute-start.40) | collective-permute-done | bytes 110624 | tf_op jit(solution)/shard_map/ppermute | solution.py:27
  243.3 3.6 %collective-permute-start.29 = (bf16[72,768]{1,0:T(8,128)(2,1)S(1)}, bf16[72,768]{1,0:T(8,128)(2,1)S(1)}, u32[]{:S(2)}, u32[]{:S(2)}) collective-permute-start(bf16[72,768]{1,0:T(8,128)(2,1)S(1)} %get-tuple-element.65), channel_id=1, source_target_pairs={{0,4},{1,5},{2,6},{3,7},{4,0},{5,1},{6,2},{7,3},{8,12},{9,13},{10,... | collective-permute-start | bytes 331784 | tf_op jit(solution)/shard_map/ppermute | solution.py:27
  252.7 2.9 %collective-permute-start.32 = (bf16[72,768]{1,0:T(8,128)(2,1)S(1)}, bf16[72,768]{1,0:T(8,128)(2,1)S(1)}, u32[]{:S(2)}, u32[]{:S(2)}) collective-permute-start(bf16[72,768]{1,0:T(8,128)(2,1)S(1)} %get-tuple-element.68), channel_id=1, source_target_pairs={{0,7},{1,6},{2,5},{3,4},{4,3},{5,2},{6,1},{7,0},{8,15},{9,14},{10,... | collective-permute-start | bytes 331784 | tf_op jit(solution)/shard_map/ppermute | solution.py:27
  258.4 4.2 %collective-permute-done.30.refs_5_ = bf16[72,768]{1,0:T(8,128)(2,1)S(1)} collective-permute-done((bf16[72,768]{1,0:T(8,128)(2,1)S(1)}, bf16[72,768]{1,0:T(8,128)(2,1)S(1)}, u32[]{:S(2)}, u32[]{:S(2)}) %collective-permute-start.30) | collective-permute-done | bytes 110624 | tf_op jit(solution)/shard_map/ppermute | solution.py:27
  262.6 3.3 %collective-permute-start.19 = (bf16[72,768]{1,0:T(8,128)(2,1)S(1)}, bf16[72,768]{1,0:T(8,128)(2,1)S(1)}, u32[]{:S(2)}, u32[]{:S(2)}) collective-permute-start(bf16[72,768]{1,0:T(8,128)(2,1)S(1)} %get-tuple-element.57), channel_id=1, source_target_pairs={{0,4},{1,5},{2,6},{3,7},{4,0},{5,1},{6,2},{7,3},{8,12},{9,13},{10,... | collective-permute-start | bytes 331784 | tf_op jit(solution)/shard_map/ppermute | solution.py:27
  265.9 4.2 %collective-permute-start.20 = (bf16[72,768]{1,0:T(8,128)(2,1)S(1)}, bf16[72,768]{1,0:T(8,128)(2,1)S(1)}, u32[]{:S(2)}, u32[]{:S(2)}) collective-permute-start(bf16[72,768]{1,0:T(8,128)(2,1)S(1)} %get-tuple-element.58), channel_id=1, source_target_pairs={{0,5},{1,4},{2,7},{3,6},{4,1},{5,0},{6,3},{7,2},{8,13},{9,12},{10,... | collective-permute-start | bytes 331784 | tf_op jit(solution)/shard_map/ppermute | solution.py:27
  271.2 2.6 collective-permute-start.22
  277.4 4.1 %collective-permute-done.20.refs_5_ = bf16[72,768]{1,0:T(8,128)(2,1)S(1)} collective-permute-done((bf16[72,768]{1,0:T(8,128)(2,1)S(1)}, bf16[72,768]{1,0:T(8,128)(2,1)S(1)}, u32[]{:S(2)}, u32[]{:S(2)}) %collective-permute-start.20) | collective-permute-done | bytes 110624 | tf_op jit(solution)/shard_map/ppermute | solution.py:27
  (144 shorter events, 82.4 us)
Async XLA Ops:
  2.6 89.4 %collective-permute-start.8 = (bf16[2,120,2880]{2,1,0:T(8,128)(2,1)}, bf16[2,120,2880]{2,1,0:T(8,128)(2,1)}, u32[]{:S(2)}, u32[]{:S(2)}) collective-permute-start(bf16[2,120,2880]{2,1,0:T(8,128)(2,1)} %bitcast.133), channel_id=1, source_target_pairs={{0,8},{1,9},{2,10},{3,11},{4,12},{5,13},{6,14},{7,15},{8,0},{9,1},... | collective-permute-start | bytes 4147208 | tf_op jit(solution)/shard_map/ppermute | solution.py:27
  3.1 85.2 %collective-permute-start.10 = (bf16[2,120,2880]{2,1,0:T(8,128)(2,1)}, bf16[2,120,2880]{2,1,0:T(8,128)(2,1)}, u32[]{:S(2)}, u32[]{:S(2)}) collective-permute-start(bf16[2,120,2880]{2,1,0:T(8,128)(2,1)} %bitcast.133), channel_id=1, source_target_pairs={{0,16},{1,17},{2,18},{3,19},{4,20},{5,21},{6,22},{7,23},{8,24},{9,... | collective-permute-start | bytes 4147208 | tf_op jit(solution)/shard_map/ppermute | solution.py:27
  11.7 27.5 %collective-permute-start.2 = (bf16[72,2880]{1,0:T(8,128)(2,1)S(1)}, bf16[72,2880]{1,0:T(8,128)(2,1)S(1)}, u32[]{:S(2)}, u32[]{:S(2)}) collective-permute-start(bf16[72,2880]{1,0:T(8,128)(2,1)S(1)} %get-tuple-element.48), channel_id=1, source_target_pairs={{0,3},{1,2},{2,1},{3,0},{4,7},{5,6},{6,5},{7,4},{8,11},{9,10},{10,... | collective-permute-start | bytes 1244168 | tf_op jit(solution)/shard_map/ppermute | solution.py:27
  20.5 40.9 %collective-permute-start.3 = (bf16[72,2880]{1,0:T(8,128)(2,1)S(1)}, bf16[72,2880]{1,0:T(8,128)(2,1)S(1)}, u32[]{:S(2)}, u32[]{:S(2)}) collective-permute-start(bf16[72,2880]{1,0:T(8,128)(2,1)S(1)} %get-tuple-element.49), channel_id=1, source_target_pairs={{0,4},{1,5},{2,6},{3,7},{4,0},{5,1},{6,2},{7,3},{8,12},{9,13},{10,... | collective-permute-start | bytes 1244168 | tf_op jit(solution)/shard_map/ppermute | solution.py:27
  23.1 57.4 %collective-permute-start.4 = (bf16[72,2880]{1,0:T(8,128)(2,1)S(1)}, bf16[72,2880]{1,0:T(8,128)(2,1)S(1)}, u32[]{:S(2)}, u32[]{:S(2)}) collective-permute-start(bf16[72,2880]{1,0:T(8,128)(2,1)S(1)} %get-tuple-element.50), channel_id=1, source_target_pairs={{0,5},{1,4},{2,7},{3,6},{4,1},{5,0},{6,3},{7,2},{8,13},{9,12},{10,... | collective-permute-start | bytes 1244168 | tf_op jit(solution)/shard_map/ppermute | solution.py:27
  39.1 41.4 %collective-permute-start.5 = (bf16[72,2880]{1,0:T(8,128)(2,1)S(1)}, bf16[72,2880]{1,0:T(8,128)(2,1)S(1)}, u32[]{:S(2)}, u32[]{:S(2)}) collective-permute-start(bf16[72,2880]{1,0:T(8,128)(2,1)S(1)} %get-tuple-element.51), channel_id=1, source_target_pairs={{0,6},{1,7},{2,4},{3,5},{4,2},{5,3},{6,0},{7,1},{8,14},{9,15},{10,... | collective-permute-start | bytes 1244168 | tf_op jit(solution)/shard_map/ppermute | solution.py:27
  61.3 19.8 %collective-permute-start.6 = (bf16[72,2880]{1,0:T(8,128)(2,1)S(1)}, bf16[72,2880]{1,0:T(8,128)(2,1)S(1)}, u32[]{:S(2)}, u32[]{:S(2)}) collective-permute-start(bf16[72,2880]{1,0:T(8,128)(2,1)S(1)} %get-tuple-element.52), channel_id=1, source_target_pairs={{0,7},{1,6},{2,5},{3,4},{4,3},{5,2},{6,1},{7,0},{8,15},{9,14},{10,... | collective-permute-start | bytes 1244168 | tf_op jit(solution)/shard_map/ppermute | solution.py:27
  80.5 67.5 %collective-permute-start.7 = (bf16[2,240,2880]{2,1,0:T(8,128)(2,1)S(1)}, bf16[2,240,2880]{2,1,0:T(8,128)(2,1)S(1)}, u32[]{:S(2)}, u32[]{:S(2)}) collective-permute-start(bf16[2,240,2880]{2,1,0:T(8,128)(2,1)S(1)} %bitcast.134), channel_id=1, source_target_pairs={{0,8},{1,9},{2,10},{3,11},{4,12},{5,13},{6,14},{7,15},{8,0},{9,1},... | collective-permute-start | bytes 8294408 | tf_op jit(solution)/shard_map/ppermute | solution.py:27
  80.5 64.1 %collective-permute-start.9 = (bf16[2,240,2880]{2,1,0:T(8,128)(2,1)S(1)}, bf16[2,240,2880]{2,1,0:T(8,128)(2,1)S(1)}, u32[]{:S(2)}, u32[]{:S(2)}) collective-permute-start(bf16[2,240,2880]{2,1,0:T(8,128)(2,1)S(1)} %bitcast.135), channel_id=1, source_target_pairs={{0,16},{1,17},{2,18},{3,19},{4,20},{5,21},{6,22},{7,23},{8,24},{9,... | collective-permute-start | bytes 8294408 | tf_op jit(solution)/shard_map/ppermute | solution.py:27
  81.2 73.7 %collective-permute-start.43 = (bf16[360,576]{1,0:T(8,128)(2,1)S(1)}, bf16[360,576]{1,0:T(8,128)(2,1)S(1)}, u32[]{:S(2)}, u32[]{:S(2)}) collective-permute-start(bf16[360,576]{1,0:T(8,128)(2,1)S(1)} %slice_bitcast_fusion.83.refs_4_), channel_id=1, source_target_pairs={{0,8},{1,9},{2,10},{3,11},{4,12},{5,13},{6,14},{7,15},{8,0},{9,1},... | collective-permute-start | bytes 1244168 | tf_op jit(solution)/shard_map/ppermute | solution.py:27
  88.3 68.1 %collective-permute-start.44 = (bf16[360,576]{1,0:T(8,128)(2,1)S(1)}, bf16[360,576]{1,0:T(8,128)(2,1)S(1)}, u32[]{:S(2)}, u32[]{:S(2)}) collective-permute-start(bf16[360,576]{1,0:T(8,128)(2,1)S(1)} %slice_bitcast_fusion.83.refs_4_), channel_id=1, source_target_pairs={{0,16},{1,17},{2,18},{3,19},{4,20},{5,21},{6,22},{7,23},{8,24},{9,... | collective-permute-start | bytes 1244168 | tf_op jit(solution)/shard_map/ppermute | solution.py:27
  92.0 60.1 %collective-permute-start.12 = (bf16[2,120,2880]{2,1,0:T(8,128)(2,1)}, bf16[2,120,2880]{2,1,0:T(8,128)(2,1)S(1)}, u32[]{:S(2)}, u32[]{:S(2)}) collective-permute-start(bf16[2,120,2880]{2,1,0:T(8,128)(2,1)} %collective-permute-done.10), channel_id=1, source_target_pairs={{0,8},{1,9},{2,10},{3,11},{4,12},{5,13},{6,14},{7,15},{8,0},{9,1},... | collective-permute-start | bytes 4147208 | tf_op jit(solution)/shard_map/ppermute | solution.py:27
  154.8 24.6 %collective-permute-start.24 = (bf16[360,768]{1,0:T(8,128)(2,1)S(1)}, bf16[360,768]{1,0:T(8,128)(2,1)S(1)}, u32[]{:S(2)}, u32[]{:S(2)}) collective-permute-start(bf16[360,768]{1,0:T(8,128)(2,1)S(1)} %get-tuple-element.86.refs_4_), channel_id=1, source_target_pairs={{0,16},{1,17},{2,18},{3,19},{4,20},{5,21},{6,22},{7,23},{8,24},{9,... | collective-permute-start | bytes 1658888 | tf_op jit(solution)/shard_map/ppermute | solution.py:27
  156.4 33.9 %collective-permute-start.14 = (bf16[360,768]{1,0:T(8,128)(2,1)S(1)}, bf16[360,768]{1,0:T(8,128)(2,1)S(1)}, u32[]{:S(2)}, u32[]{:S(2)}) collective-permute-start(bf16[360,768]{1,0:T(8,128)(2,1)S(1)} %get-tuple-element.85.refs_4_), channel_id=1, source_target_pairs={{0,16},{1,17},{2,18},{3,19},{4,20},{5,21},{6,22},{7,23},{8,24},{9,... | collective-permute-start | bytes 1658888 | tf_op jit(solution)/shard_map/ppermute | solution.py:27
  157.1 33.2 %collective-permute-start.45 = (bf16[360,576]{1,0:T(8,128)(2,1)S(1)}, bf16[360,576]{1,0:T(8,128)(2,1)S(1)}, u32[]{:S(2)}, u32[]{:S(2)}) collective-permute-start(bf16[360,576]{1,0:T(8,128)(2,1)S(1)} %collective-permute-done.44.refs_6_), channel_id=1, source_target_pairs={{0,8},{1,9},{2,10},{3,11},{4,12},{5,13},{6,14},{7,15},{8,0},{9,1},... | collective-permute-start | bytes 1244168 | tf_op jit(solution)/shard_map/ppermute | solution.py:27
  158.5 35.6 %collective-permute-start.23 = (bf16[360,768]{1,0:T(8,128)(2,1)S(1)}, bf16[360,768]{1,0:T(8,128)(2,1)S(1)}, u32[]{:S(2)}, u32[]{:S(2)}) collective-permute-start(bf16[360,768]{1,0:T(8,128)(2,1)S(1)} %get-tuple-element.86.refs_4_), channel_id=1, source_target_pairs={{0,8},{1,9},{2,10},{3,11},{4,12},{5,13},{6,14},{7,15},{8,0},{9,1},... | collective-permute-start | bytes 1658888 | tf_op jit(solution)/shard_map/ppermute | solution.py:27
  167.6 27.0 %collective-permute-start.13 = (bf16[360,768]{1,0:T(8,128)(2,1)S(1)}, bf16[360,768]{1,0:T(8,128)(2,1)S(1)}, u32[]{:S(2)}, u32[]{:S(2)}) collective-permute-start(bf16[360,768]{1,0:T(8,128)(2,1)S(1)} %get-tuple-element.85.refs_4_), channel_id=1, source_target_pairs={{0,8},{1,9},{2,10},{3,11},{4,12},{5,13},{6,14},{7,15},{8,0},{9,1},... | collective-permute-start | bytes 1658888 | tf_op jit(solution)/shard_map/ppermute | solution.py:27
  179.4 25.2 %collective-permute-start.35 = (bf16[360,768]{1,0:T(8,128)(2,1)S(1)}, bf16[360,768]{1,0:T(8,128)(2,1)S(1)}, u32[]{:S(2)}, u32[]{:S(2)}) collective-permute-start(bf16[360,768]{1,0:T(8,128)(2,1)S(1)} %collective-permute-done.34.refs_6_), channel_id=1, source_target_pairs={{0,8},{1,9},{2,10},{3,11},{4,12},{5,13},{6,14},{7,15},{8,0},{9,1},... | collective-permute-start | bytes 1658888 | tf_op jit(solution)/shard_map/ppermute | solution.py:27
  190.3 16.3 %collective-permute-start.25 = (bf16[360,768]{1,0:T(8,128)(2,1)S(1)}, bf16[360,768]{1,0:T(8,128)(2,1)S(1)}, u32[]{:S(2)}, u32[]{:S(2)}) collective-permute-start(bf16[360,768]{1,0:T(8,128)(2,1)S(1)} %collective-permute-done.24.refs_6_), channel_id=1, source_target_pairs={{0,8},{1,9},{2,10},{3,11},{4,12},{5,13},{6,14},{7,15},{8,0},{9,1},... | collective-permute-start | bytes 1658888 | tf_op jit(solution)/shard_map/ppermute | solution.py:27
  190.3 17.9 %collective-permute-start.15 = (bf16[360,768]{1,0:T(8,128)(2,1)S(1)}, bf16[360,768]{1,0:T(8,128)(2,1)S(1)}, u32[]{:S(2)}, u32[]{:S(2)}) collective-permute-start(bf16[360,768]{1,0:T(8,128)(2,1)S(1)} %collective-permute-done.14.refs_6_), channel_id=1, source_target_pairs={{0,8},{1,9},{2,10},{3,11},{4,12},{5,13},{6,14},{7,15},{8,0},{9,1},... | collective-permute-start | bytes 1658888 | tf_op jit(solution)/shard_map/ppermute | solution.py:27
  194.0 18.0 %collective-permute-start.46 = (bf16[72,576]{1,0:T(8,128)(2,1)S(1)}, bf16[72,576]{1,0:T(8,128)(2,1)S(1)}, u32[]{:S(2)}, u32[]{:S(2)}) collective-permute-start(bf16[72,576]{1,0:T(8,128)(2,1)S(1)} %get-tuple-element.78), channel_id=1, source_target_pairs={{0,1},{1,0},{2,3},{3,2},{4,5},{5,4},{6,7},{7,6},{8,9},{9,8},{10,11... | collective-permute-start | bytes 248840 | tf_op jit(solution)/shard_map/ppermute | solution.py:27
  194.6 17.5 %collective-permute-start.47 = (bf16[72,576]{1,0:T(8,128)(2,1)S(1)}, bf16[72,576]{1,0:T(8,128)(2,1)S(1)}, u32[]{:S(2)}, u32[]{:S(2)}) collective-permute-start(bf16[72,576]{1,0:T(8,128)(2,1)S(1)} %get-tuple-element.79), channel_id=1, source_target_pairs={{0,2},{1,3},{2,0},{3,1},{4,6},{5,7},{6,4},{7,5},{8,10},{9,11},{10,... | collective-permute-start | bytes 248840 | tf_op jit(solution)/shard_map/ppermute | solution.py:27
  206.6 25.4 %collective-permute-start.36 = (bf16[72,768]{1,0:T(8,128)(2,1)S(1)}, bf16[72,768]{1,0:T(8,128)(2,1)S(1)}, u32[]{:S(2)}, u32[]{:S(2)}) collective-permute-start(bf16[72,768]{1,0:T(8,128)(2,1)S(1)} %get-tuple-element.70), channel_id=1, source_target_pairs={{0,1},{1,0},{2,3},{3,2},{4,5},{5,4},{6,7},{7,6},{8,9},{9,8},{10,11... | collective-permute-start | bytes 331784 | tf_op jit(solution)/shard_map/ppermute | solution.py:27
  224.4 15.7 %collective-permute-start.39 = (bf16[72,768]{1,0:T(8,128)(2,1)S(1)}, bf16[72,768]{1,0:T(8,128)(2,1)S(1)}, u32[]{:S(2)}, u32[]{:S(2)}) collective-permute-start(bf16[72,768]{1,0:T(8,128)(2,1)S(1)} %get-tuple-element.73), channel_id=1, source_target_pairs={{0,4},{1,5},{2,6},{3,7},{4,0},{5,1},{6,2},{7,3},{8,12},{9,13},{10,... | collective-permute-start | bytes 331784 | tf_op jit(solution)/shard_map/ppermute | solution.py:27
  (34 other events, 419.5 us)

commit v2 on v1

v2 whole, which is shorter than its diff:
```python
import functools

import jax
import jax.numpy as jnp
from jax import lax
from jax.experimental import pallas as pl
from jax.experimental.pallas import tpu as pltpu
from jax.sharding import PartitionSpec as P

clamp_limit = 7.0
AXES = ("dp", "expert")
VMEM_LIMIT = 12 * 1024 * 1024
FAR_IN = 3
TIES = {11: (7,), 13: (6,), 14: (5,), 15: (4,)}
F32, BF16 = jnp.float32, jnp.bfloat16


def sent_to(array, target):
    dp_size, expert_size = lax.axis_size("dp"), lax.axis_size("expert")
    pairs = []
    for d in range(dp_size):
        for e in range(expert_size):
            td, te = target(d, e)
            pairs.append((d * expert_size + e, td * expert_size + te))
    return lax.ppermute(array, AXES, pairs)


def to_other_core(array):
    return sent_to(array, lambda d, e: (d ^ 1, e))


def to_chip(step):
    dp_size = lax.axis_size("dp")
    return lambda array: sent_to(array, lambda d, e: ((d + 2 * step) % dp_size, e))


def to_expert(offset):
    return lambda array: sent_to(array, lambda d, e: (d, e ^ offset))


def after(array, *others):
    return lax.optimization_barrier((array, others))[0]


class Line:
    def __init__(self, depth):
        self.depth = depth
        self.done = []

    def send(self, array, move, ties=()):
        if len(self.done) >= self.depth:
            ties = [*ties, self.done[-self.depth]]
        if ties:
            array = after(array, *ties)
        moved = move(array)
        self.done.append(moved)
        return moved


def call_kernel(body, out_shapes, args, flops):
    moved = sum(a.size * a.dtype.itemsize for a in args) + sum(s.size * s.dtype.itemsize for s in out_shapes)
    return pl.pallas_call(
        body,
        out_shape=out_shapes,
        in_specs=[pl.BlockSpec(memory_space=pltpu.VMEM)] * len(args),
        out_specs=[pl.BlockSpec(memory_space=pltpu.VMEM)] * len(out_shapes),
        compiler_params=pltpu.CompilerParams(vmem_limit_bytes=VMEM_LIMIT),
        cost_estimate=pl.CostEstimate(flops=flops, bytes_accessed=moved, transcendentals=0),
    )(*args)


def pick_kernel(sel_ref, hid_ref, *out_refs):
    hid = hid_ref[...]
    for k, out_ref in enumerate(out_refs):
        out_ref[...] = jnp.dot(sel_ref[k], hid, preferred_element_type=F32).astype(BF16)


def expert_kernel(blocks, shards, *refs):
    row_refs, up_refs, down_refs = refs[:blocks], refs[blocks : blocks + shards], refs[blocks + shards : blocks + 2 * shards]
    out_refs = refs[blocks + 2 * shards :]
    rows = jnp.concatenate([ref[...].astype(F32) for ref in row_refs], axis=0).astype(BF16)
    dims = (((1,), (1,)), ((), ()))
    total = None
    for up_ref, down_ref in zip(up_refs, down_refs):
        gate = lax.dot_general(rows, up_ref[0], dims, preferred_element_type=F32)
        upper = lax.dot_general(rows, up_ref[1], dims, preferred_element_type=F32)
        gate = jnp.minimum(gate, clamp_limit)
        upper = jnp.clip(upper, -clamp_limit, clamp_limit)
        hidden = ((upper + 1.0) * gate * jax.nn.sigmoid(1.702 * gate)).astype(BF16)
        part = jnp.dot(hidden, down_ref[...], preferred_element_type=F32)
        total = part if total is None else total + part
    slots = total.shape[0] // blocks
    for s, out_ref in enumerate(out_refs):
        out_ref[...] = total[s * slots : (s + 1) * slots].astype(out_ref.dtype)


def add_kernel(*refs):
    total = refs[0][...]
    for ref in refs[1:-1]:
        total += ref[...].astype(F32)
    refs[-1][...] = total.astype(BF16)


def combine_kernel(table_ref, *refs):
    total = jnp.dot(table_ref[0], refs[0][...], preferred_element_type=F32)
    for k in range(1, len(refs) - 1):
        total += jnp.dot(table_ref[k], refs[k][...], preferred_element_type=F32)
    refs[-1][...] = total.astype(BF16)


def plan(groups):
    half = groups // 2
    far, near = list(range(groups - 1, half - 1, -1)), list(range(2, half))
    steps = [("out", 0), ("out", 1), ("out", far[0]), ("back", 1)]
    for last, k in zip(far, far[1:]):
        steps += [("out", k), ("back", last)]
    steps += [("back", far[-1])]
    steps += [("out", k) for k in near] + [("back", k) for k in near] + [("back", 0)]
    return steps


def local(hidden_states, route_ids, route_weights, gate_up_proj, down_proj):
    tok_rows, width = hidden_states.shape
    top_count = route_ids.shape[1]
    units = gate_up_proj.shape[1]
    groups = lax.axis_size("expert")
    chips = lax.axis_size("dp") // 2
    capacity = max(2, 17 * tok_rows * top_count // (16 * groups))
    slots = -(-capacity // 8) * 8
    half = groups // 2
    me = lax.axis_index("expert")

    near = (route_ids ^ me)[:, :, None] == jnp.arange(groups, dtype=jnp.int32)
    member = jnp.any(near, axis=1)
    weight = jnp.sum(jnp.where(near, route_weights[:, :, None].astype(F32), 0.0), axis=1)
    before = jnp.tril(jnp.ones((tok_rows, tok_rows), BF16), -1)
    rank = jnp.dot(before, member.astype(BF16), preferred_element_type=F32).astype(jnp.int32)
    rank = jnp.where(member, rank, -1)
    slot_range = jnp.arange(slots, dtype=jnp.int32)
    chosen = rank.T[:, None, :] == slot_range[None, :, None]
    table = jnp.where(rank.T[:, :, None] == slot_range, weight.T[:, :, None], 0.0).astype(BF16)
    outgoing = call_kernel(
        pick_kernel,
        [jax.ShapeDtypeStruct((slots, width), BF16)] * groups,
        (chosen.astype(BF16), hidden_states),
        2 * groups * slots * tok_rows * width,
    )

    between_chips = Line(2 * (chips - 1))
    far_in, near_in, far_out, near_out = Line(FAR_IN), Line(1), Line(2), Line(1)
    rows = [outgoing[0]] + [None] * (groups - 1)
    for k in range(groups - 1, half - 1, -1):
        rows[k] = far_in.send(outgoing[k], to_expert(k))
    rows[1] = near_in.send(outgoing[1], to_expert(1))

    weights, partial, results = [], {}, [None] * groups
    steps = plan(groups)
    for number, (what, k) in enumerate(steps):
        ties = [results[t] for t in TIES.get(number, ()) if t < groups and results[t] is not None]
        if what == "out":
            if k >= 2 and k < half:
                rows[k] = near_in.send(rows[k], to_expert(k))
            others = [between_chips.send(rows[k], to_chip(s), ties) for s in range(1, chips)]
            if k == 0:
                own_gu = jnp.transpose(after(gate_up_proj[0], *others), (1, 0, 2))
                core_gu = to_other_core(own_gu)
                core_dn = to_other_core(after(down_proj[0], *others))
                weights = [own_gu, core_gu, down_proj[0], core_dn]
                near_in.done.append(core_dn)
                for t in range(2, half):
                    rows[t] = outgoing[t]
            partial[k] = call_kernel(
                functools.partial(expert_kernel, chips, 2),
                [jax.ShapeDtypeStruct((slots, width), F32)] + [jax.ShapeDtypeStruct((slots, width), BF16)] * (chips - 1),
                (rows[k], *others, *weights),
                6 * chips * slots * width * 2 * units,
            )
            continue
        mine, *foreign = partial[k]
        back = [between_chips.send(v, to_chip(-s), ties) for s, v in enumerate(foreign, 1)]
        out, = call_kernel(add_kernel, [jax.ShapeDtypeStruct((slots, width), BF16)], (mine, *back), 0)
        line = far_out if k >= half else near_out
        results[k] = line.send(out, to_expert(k)) if k else out
    combined, = call_kernel(
        combine_kernel,
        [jax.ShapeDtypeStruct((tok_rows, width), BF16)],
        (table, *results),
        2 * groups * slots * tok_rows * width,
    )
    return combined


def solution(mesh):
    placed = (
        P(("dp", "expert"), None),
        P(("dp", "expert"), None),
        P(("dp", "expert"), None),
        P("expert", "dp", None, None),
        P("expert", "dp", None),
    )
    return jax.shard_map(
        local, mesh=mesh, in_specs=placed, out_specs=P(("dp", "expert"), None), check_vma=False
    )
```

time: 285 us -> 198 us (0.69)
  waiting for transfers between devices: 158 us -> 101 us
  starting transfers between devices: 80.6 us -> 55.3 us
  matrix products: 24.4 us -> 0.2 us
  Pallas kernels: 11.1 us -> 34.9 us
    ppermute x53 -> x32, waiting for transfers between devices: 158 us -> 101 us  [sent_to(): return lax.ppermute(array, AXES, pairs)]
    ppermute x53 -> x32, starting transfers between devices: 80.6 us -> 55.3 us  [sent_to(): return lax.ppermute(array, AXES, pairs)]
    dot_general x17 -> x1, matrix products: 24.4 us -> 0.2 us  [local(): jnp.dot(before, member.astype(BF16), preferred_element_type=F32)]
    pallas_call x9 -> x18, Pallas kernels: 11.1 us -> 34.9 us  [call_kernel(): pl.pallas_call(body, out_shape=out_shapes, in_specs=[pl.BlockSpec(memory_...]
    slice x4 -> x0, local copies, waits for them, and re-layouts: 3.09 us -> none  [local(): own_gu = [jnp.transpose(gate_up_proj[0, a:b], (1, 0, 2)) for a, b in pieces]]
  transfers between devices with their start and end apart: 53 -> 32, of which waited for: 16 -> 19; matrix products, arithmetic and copies ran while one was open for 10% -> 2% of each run, Pallas kernels for 4% -> 16%
where the time goes in v2:
time: 198 us
  waiting for transfers between devices  101 us (51%)
  starting transfers between devices  55.3 us (28%)
  Pallas kernels  34.9 us (18%)
  local copies, waits for them, and re-layouts  5.26 us (3%)
    ppermute x32, waiting for transfers between devices, sent_to(): return lax.ppermute(array, AXES, pairs)  101 us
    ppermute x32, starting transfers between devices, sent_to(): return lax.ppermute(array, AXES, pairs)  55.3 us
    pallas_call x18, Pallas kernels, call_kernel(): pl.pallas_call(body, out_shape=out_shapes, in_specs=[pl.BlockSpec(memory_...  34.9 us
    unnamed x6, local copies, waits for them, and re-layouts  4.11 us
  transfers between devices with their start and end apart: 32, of which 19 were waited for; matrix products, arithmetic and copies ran while one was open for 2% of the time, Pallas kernels for 16%

profile of v2, /device:TPU:0, one launch (start us, length us, event | category | flops | bytes accessed | tf_op | source)
XLA Modules:
  0.0 198.2 jit_solution(1201752767149633993)
XLA Ops:
  9.3 7.1 %collective-permute-done.refs_1_ = bf16[72,2880]{1,0:T(8,128)(2,1)S(1)} collective-permute-done((bf16[72,2880]{1,0:T(8,128)(2,1)S(1)}, bf16[72,2880]{1,0:T(8,128)(2,1)S(1)}, u32[]{:S(2)}, u32[]{:S(2)}) %collective-permute-start) | collective-permute-done | bytes 414752 | tf_op jit(solution)/shard_map/ppermute | solution.py:25
  18.7 3.5 %collective-permute-start.3 = (bf16[72,2880]{1,0:T(8,128)(2,1)S(1)}, bf16[72,2880]{1,0:T(8,128)(2,1)S(1)}, u32[]{:S(2)}, u32[]{:S(2)}) collective-permute-start(bf16[72,2880]{1,0:T(8,128)(2,1)S(1)} %get-tuple-element.58), channel_id=1, source_target_pairs={{0,7},{1,6},{2,5},{3,4},{4,3},{5,2},{6,1},{7,0},{8,15},{9,14},{10,... | collective-permute-start | bytes 1244168 | tf_op jit(solution)/shard_map/ppermute | solution.py:25
  22.2 15.5 %collective-permute-done.12.refs_0_ = bf16[72,2880]{1,0:T(8,128)(2,1)S(1)} collective-permute-done((bf16[72,2880]{1,0:T(8,128)(2,1)S(1)}, bf16[72,2880]{1,0:T(8,128)(2,1)S(1)}, u32[]{:S(2)}, u32[]{:S(2)}) %collective-permute-start.12) | collective-permute-done | bytes 414752 | tf_op jit(solution)/shard_map/ppermute | solution.py:25
  39.4 3.6 %collective-permute-start.6 = (bf16[72,2880]{1,0:T(8,128)(2,1)S(1)}, bf16[72,2880]{1,0:T(8,128)(2,1)S(1)}, u32[]{:S(2)}, u32[]{:S(2)}) collective-permute-start(bf16[72,2880]{1,0:T(8,128)(2,1)S(1)} %get-tuple-element.61), channel_id=1, source_target_pairs={{0,6},{1,7},{2,4},{3,5},{4,2},{5,3},{6,0},{7,1},{8,14},{9,15},{10,... | collective-permute-start | bytes 1244168 | tf_op jit(solution)/shard_map/ppermute | solution.py:25
  43.6 6.8 %collective-permute-done.13.refs_1_ = bf16[72,2880]{1,0:T(8,128)(2,1)S(1)} collective-permute-done((bf16[72,2880]{1,0:T(8,128)(2,1)S(1)}, bf16[72,2880]{1,0:T(8,128)(2,1)S(1)}, u32[]{:S(2)}, u32[]{:S(2)}) %collective-permute-start.13) | collective-permute-done | bytes 414752 | tf_op jit(solution)/shard_map/ppermute | solution.py:25
  50.4 3.8 %shard_map.61 = (f32[72,2880]{1,0:T(8,128)S(1)}, bf16[72,2880]{1,0:T(8,128)(2,1)S(1)}) custom-call(bf16[72,2880]{1,0:T(8,128)(2,1)S(1)} %collective-permute-done.12.refs_0_, bf16[72,2880]{1,0:T(8,128)(2,1)S(1)} %collective-permute-done.13.refs_1_, bf16[2,360,2880]{2,1,0:T(8,128)(2,1)S(1)} %bitcast.10, ...), custom_call_target="tpu_custom_call" | custom-call | flops 1791590400 | bytes 14515200 | tf_op jit(solution)/shard_map/pallas_call | solution.py:62
  61.2 3.9 %shard_map.60 = (f32[72,2880]{1,0:T(8,128)S(1)}, bf16[72,2880]{1,0:T(8,128)(2,1)S(1)}) custom-call(bf16[72,2880]{1,0:T(8,128)(2,1)S(1)} %collective-permute-done.3.refs_0_, bf16[72,2880]{1,0:T(8,128)(2,1)S(1)} %collective-permute-done.7.refs_1_, bf16[2,360,2880]{2,1,0:T(8,128)(2,1)S(1)} %bitcast.11, ...), custom_call_target="tpu_custom_call" | custom-call | flops 1791590400 | bytes 14515200 | tf_op jit(solution)/shard_map/pallas_call | solution.py:62
  70.3 5.9 %collective-permute-start.4 = (bf16[72,2880]{1,0:T(8,128)(2,1)S(1)}, bf16[72,2880]{1,0:T(8,128)(2,1)S(1)}, u32[]{:S(2)}, u32[]{:S(2)}) collective-permute-start(bf16[72,2880]{1,0:T(8,128)(2,1)S(1)} %get-tuple-element.59), channel_id=1, source_target_pairs={{0,4},{1,5},{2,6},{3,7},{4,0},{5,1},{6,2},{7,3},{8,12},{9,13},{10,... | collective-permute-start | bytes 1244168 | tf_op jit(solution)/shard_map/ppermute | solution.py:25
  76.2 11.2 %collective-permute-done.5.refs_0_ = bf16[72,2880]{1,0:T(8,128)(2,1)S(1)} collective-permute-done((bf16[72,2880]{1,0:T(8,128)(2,1)S(1)}, bf16[72,2880]{1,0:T(8,128)(2,1)S(1)}, u32[]{:S(2)}, u32[]{:S(2)}) %collective-permute-start.5) | collective-permute-done | bytes 414752 | tf_op jit(solution)/shard_map/ppermute | solution.py:25
  88.9 3.8 %shard_map.59 = (f32[72,2880]{1,0:T(8,128)S(1)}, bf16[72,2880]{1,0:T(8,128)(2,1)S(1)}) custom-call(bf16[72,2880]{1,0:T(8,128)(2,1)S(1)} %collective-permute-done.6.refs_0_, bf16[72,2880]{1,0:T(8,128)(2,1)S(1)} %collective-permute-done.8.refs_1_, bf16[2,360,2880]{2,1,0:T(8,128)(2,1)S(1)} %bitcast.12, ...), custom_call_target="tpu_custom_call" | custom-call | flops 1791590400 | bytes 14515200 | tf_op jit(solution)/shard_map/pallas_call | solution.py:62
  94.7 5.4 %collective-permute-done.9.refs_1_ = bf16[72,2880]{1,0:T(8,128)(2,1)S(1)} collective-permute-done((bf16[72,2880]{1,0:T(8,128)(2,1)S(1)}, bf16[72,2880]{1,0:T(8,128)(2,1)S(1)}, u32[]{:S(2)}, u32[]{:S(2)}) %collective-permute-start.9) | collective-permute-done | bytes 414752 | tf_op jit(solution)/shard_map/ppermute | solution.py:25
  101.6 4.0 %shard_map.64 = (f32[72,2880]{1,0:T(8,128)S(1)}, bf16[72,2880]{1,0:T(8,128)(2,1)S(1)}) custom-call(bf16[72,2880]{1,0:T(8,128)(2,1)S(1)} %collective-permute-done.5.refs_0_, bf16[72,2880]{1,0:T(8,128)(2,1)S(1)} %collective-permute-done.9.refs_1_, bf16[2,360,2880]{2,1,0:T(8,128)(2,1)S(1)} %bitcast.13, ...), custom_call_target="tpu_custom_call" | custom-call | flops 1791590400 | bytes 14515200 | tf_op jit(solution)/shard_map/pallas_call | solution.py:62
  111.3 7.0 %collective-permute-done.10.refs_1_ = bf16[72,2880]{1,0:T(8,128)(2,1)S(1)} collective-permute-done((bf16[72,2880]{1,0:T(8,128)(2,1)S(1)}, bf16[72,2880]{1,0:T(8,128)(2,1)S(1)}, u32[]{:S(2)}, u32[]{:S(2)}) %collective-permute-start.10) | collective-permute-done | bytes 414752 | tf_op jit(solution)/shard_map/ppermute | solution.py:25
  118.3 3.8 %shard_map.57 = (f32[72,2880]{1,0:T(8,128)S(1)}, bf16[72,2880]{1,0:T(8,128)(2,1)S(1)}) custom-call(bf16[72,2880]{1,0:T(8,128)(2,1)S(1)} %collective-permute-done.4.refs_0_, bf16[72,2880]{1,0:T(8,128)(2,1)S(1)} %collective-permute-done.10.refs_1_, bf16[2,360,2880]{2,1,0:T(8,128)(2,1)S(1)} %bitcast.14, ...), custom_call_target="tpu_custom_call" | custom-call | flops 1791590400 | bytes 14515200 | tf_op jit(solution)/shard_map/pallas_call | solution.py:62
  123.7 3.7 %collective-permute-done.21.refs_1_ = bf16[72,2880]{1,0:T(8,128)(2,1)S(1)} collective-permute-done((bf16[72,2880]{1,0:T(8,128)(2,1)S(1)}, bf16[72,2880]{1,0:T(8,128)(2,1)S(1)}, u32[]{:S(2)}, u32[]{:S(2)}) %collective-permute-start.21) | collective-permute-done | bytes 414752 | tf_op jit(solution)/shard_map/ppermute | solution.py:25
  131.9 4.6 %collective-permute-done.11.refs_1_ = bf16[72,2880]{1,0:T(8,128)(2,1)S(1)} collective-permute-done((bf16[72,2880]{1,0:T(8,128)(2,1)S(1)}, bf16[72,2880]{1,0:T(8,128)(2,1)S(1)}, u32[]{:S(2)}, u32[]{:S(2)}) %collective-permute-start.11) | collective-permute-done | bytes 414752 | tf_op jit(solution)/shard_map/ppermute | solution.py:25
  140.1 5.5 %collective-permute-done.22.refs_1_ = bf16[72,2880]{1,0:T(8,128)(2,1)S(1)} collective-permute-done((bf16[72,2880]{1,0:T(8,128)(2,1)S(1)}, bf16[72,2880]{1,0:T(8,128)(2,1)S(1)}, u32[]{:S(2)}, u32[]{:S(2)}) %collective-permute-start.22) | collective-permute-done | bytes 414752 | tf_op jit(solution)/shard_map/ppermute | solution.py:25
  145.6 3.9 %shard_map.65 = (f32[72,2880]{1,0:T(8,128)S(1)}, bf16[72,2880]{1,0:T(8,128)(2,1)S(1)}) custom-call(bf16[72,2880]{1,0:T(8,128)(2,1)S(1)} %collective-permute-done.19.refs_0_, bf16[72,2880]{1,0:T(8,128)(2,1)S(1)} %collective-permute-done.22.refs_1_, bf16[2,360,2880]{2,1,0:T(8,128)(2,1)S(1)} %bitcast.15, ...), custom_call_target="tpu_custom_call" | custom-call | flops 1791590400 | bytes 14515200 | tf_op jit(solution)/shard_map/pallas_call | solution.py:62
  153.0 3.8 %shard_map.69 = (f32[72,2880]{1,0:T(8,128)S(1)}, bf16[72,2880]{1,0:T(8,128)(2,1)S(1)}) custom-call(bf16[72,2880]{1,0:T(8,128)(2,1)S(1)} %collective-permute-done.27.refs_0_, bf16[72,2880]{1,0:T(8,128)(2,1)S(1)} %collective-permute-done.28.refs_1_, bf16[2,360,2880]{2,1,0:T(8,128)(2,1)S(1)} %bitcast.16, ...), custom_call_target="tpu_custom_call" | custom-call | flops 1791590400 | bytes 14515200 | tf_op jit(solution)/shard_map/pallas_call | solution.py:62
  156.9 5.7 %collective-permute-start.18 = (bf16[72,2880]{1,0:T(8,128)(2,1)S(1)}, bf16[72,2880]{1,0:T(8,128)(2,1)S(1)}, u32[]{:S(2)}, u32[]{:S(2)}) collective-permute-start(bf16[72,2880]{1,0:T(8,128)(2,1)S(1)} %shard_map.58), channel_id=1, source_target_pairs={{0,4},{1,5},{2,6},{3,7},{4,0},{5,1},{6,2},{7,3},{8,12},{9,13},{10,... | collective-permute-start | bytes 1244168 | tf_op jit(solution)/shard_map/ppermute | solution.py:25
  162.6 11.0 %collective-permute-done.29.refs_5_ = bf16[72,2880]{1,0:T(8,128)(2,1)S(1)} collective-permute-done((bf16[72,2880]{1,0:T(8,128)(2,1)S(1)}, bf16[72,2880]{1,0:T(8,128)(2,1)S(1)}, u32[]{:S(2)}, u32[]{:S(2)}) %collective-permute-start.29) | collective-permute-done | bytes 414752 | tf_op jit(solution)/shard_map/ppermute | solution.py:25
  173.8 4.1 %shard_map.56 = (f32[72,2880]{1,0:T(8,128)S(1)}, bf16[72,2880]{1,0:T(8,128)(2,1)S(1)}) custom-call(bf16[72,2880]{1,0:T(8,128)(2,1)S(1)} %get-tuple-element.52.refs_0_, bf16[72,2880]{1,0:T(8,128)(2,1)S(1)} %collective-permute-done.refs_1_, bf16[2,360,2880]{2,1,0:T(8,128)(2,1)S(1)} %bitcast.17, bf16[2,360,2880]{2,1,0:T(8,128)(2,1)S(1)} %collective-permute-done.1.refs_3_, ...), custom_call_target="tpu_custom_call" | custom-call | flops 1791590400 | bytes 14515200 | tf_op jit(solution)/shard_map/pallas_call | solution.py:62
  180.0 6.2 %collective-permute-done.30.refs_1_ = bf16[72,2880]{1,0:T(8,128)(2,1)S(1)} collective-permute-done((bf16[72,2880]{1,0:T(8,128)(2,1)S(1)}, bf16[72,2880]{1,0:T(8,128)(2,1)S(1)}, u32[]{:S(2)}, u32[]{:S(2)}) %collective-permute-start.30) | collective-permute-done | bytes 414752 | tf_op jit(solution)/shard_map/ppermute | solution.py:25
  190.9 4.5 %collective-permute-done.31.refs_3_ = bf16[72,2880]{1,0:T(8,128)(2,1)S(1)} collective-permute-done((bf16[72,2880]{1,0:T(8,128)(2,1)S(1)}, bf16[72,2880]{1,0:T(8,128)(2,1)S(1)}, u32[]{:S(2)}, u32[]{:S(2)}) %collective-permute-start.31) | collective-permute-done | bytes 414752 | tf_op jit(solution)/shard_map/ppermute | solution.py:25
  (73 shorter events, 59.5 us)
Async XLA Ops:
  16.4 34.0 %collective-permute-start.1 = (bf16[2,360,2880]{2,1,0:T(8,128)(2,1)S(1)}, bf16[2,360,2880]{2,1,0:T(8,128)(2,1)S(1)}, u32[]{:S(2)}, u32[]{:S(2)}) collective-permute-start(bf16[2,360,2880]{2,1,0:T(8,128)(2,1)S(1)} %bitcast.9), channel_id=1, source_target_pairs={{0,8},{1,9},{2,10},{3,11},{4,12},{5,13},{6,14},{7,15},{8,0},{9,1},... | collective-permute-start | bytes 12441608 | tf_op jit(solution)/shard_map/ppermute | solution.py:25
  16.4 34.0 %collective-permute-start.2 = (bf16[360,2880]{1,0:T(8,128)(2,1)S(1)}, bf16[360,2880]{1,0:T(8,128)(2,1)S(1)}, u32[]{:S(2)}, u32[]{:S(2)}) collective-permute-start(bf16[360,2880]{1,0:T(8,128)(2,1)S(1)} %bitcast.18), channel_id=1, source_target_pairs={{0,8},{1,9},{2,10},{3,11},{4,12},{5,13},{6,14},{7,15},{8,0},{9,1},... | collective-permute-start | bytes 6220808 | tf_op jit(solution)/shard_map/ppermute | solution.py:25
  16.9 20.8 %collective-permute-start.12 = (bf16[72,2880]{1,0:T(8,128)(2,1)S(1)}, bf16[72,2880]{1,0:T(8,128)(2,1)S(1)}, u32[]{:S(2)}, u32[]{:S(2)}) collective-permute-start(bf16[72,2880]{1,0:T(8,128)(2,1)S(1)} %get-tuple-element.72), channel_id=1, source_target_pairs={{0,1},{1,0},{2,3},{3,2},{4,5},{5,4},{6,7},{7,6},{8,9},{9,8},{10,11... | collective-permute-start | bytes 1244168 | tf_op jit(solution)/shard_map/ppermute | solution.py:25
  18.7 24.3 %collective-permute-start.3 = (bf16[72,2880]{1,0:T(8,128)(2,1)S(1)}, bf16[72,2880]{1,0:T(8,128)(2,1)S(1)}, u32[]{:S(2)}, u32[]{:S(2)}) collective-permute-start(bf16[72,2880]{1,0:T(8,128)(2,1)S(1)} %get-tuple-element.58), channel_id=1, source_target_pairs={{0,7},{1,6},{2,5},{3,4},{4,3},{5,2},{6,1},{7,0},{8,15},{9,14},{10,... | collective-permute-start | bytes 1244168 | tf_op jit(solution)/shard_map/ppermute | solution.py:25
  39.4 16.6 %collective-permute-start.6 = (bf16[72,2880]{1,0:T(8,128)(2,1)S(1)}, bf16[72,2880]{1,0:T(8,128)(2,1)S(1)}, u32[]{:S(2)}, u32[]{:S(2)}) collective-permute-start(bf16[72,2880]{1,0:T(8,128)(2,1)S(1)} %get-tuple-element.61), channel_id=1, source_target_pairs={{0,6},{1,7},{2,4},{3,5},{4,2},{5,3},{6,0},{7,1},{8,14},{9,15},{10,... | collective-permute-start | bytes 1244168 | tf_op jit(solution)/shard_map/ppermute | solution.py:25
  43.0 16.5 %collective-permute-start.7 = (bf16[72,2880]{1,0:T(8,128)(2,1)S(1)}, bf16[72,2880]{1,0:T(8,128)(2,1)S(1)}, u32[]{:S(2)}, u32[]{:S(2)}) collective-permute-start(bf16[72,2880]{1,0:T(8,128)(2,1)S(1)} %collective-permute-done.3.refs_0_), channel_id=1, source_target_pairs={{0,16},{1,17},{2,18},{3,19},{4,20},{5,21},{6,22},{7,23},{8,24},{9,... | collective-permute-start | bytes 1244168 | tf_op jit(solution)/shard_map/ppermute | solution.py:25
  54.3 14.3 %collective-permute-start.14 = (bf16[72,2880]{1,0:T(8,128)(2,1)S(1)}, bf16[72,2880]{1,0:T(8,128)(2,1)S(1)}, u32[]{:S(2)}, u32[]{:S(2)}) collective-permute-start(bf16[72,2880]{1,0:T(8,128)(2,1)S(1)} %get-tuple-element.74), channel_id=1, source_target_pairs={{0,16},{1,17},{2,18},{3,19},{4,20},{5,21},{6,22},{7,23},{8,24},{9,... | collective-permute-start | bytes 1244168 | tf_op jit(solution)/shard_map/ppermute | solution.py:25
  56.0 31.4 %collective-permute-start.5 = (bf16[72,2880]{1,0:T(8,128)(2,1)S(1)}, bf16[72,2880]{1,0:T(8,128)(2,1)S(1)}, u32[]{:S(2)}, u32[]{:S(2)}) collective-permute-start(bf16[72,2880]{1,0:T(8,128)(2,1)S(1)} %get-tuple-element.60), channel_id=1, source_target_pairs={{0,5},{1,4},{2,7},{3,6},{4,1},{5,0},{6,3},{7,2},{8,13},{9,12},{10,... | collective-permute-start | bytes 1244168 | tf_op jit(solution)/shard_map/ppermute | solution.py:25
  59.5 27.9 %collective-permute-start.8 = (bf16[72,2880]{1,0:T(8,128)(2,1)S(1)}, bf16[72,2880]{1,0:T(8,128)(2,1)S(1)}, u32[]{:S(2)}, u32[]{:S(2)}) collective-permute-start(bf16[72,2880]{1,0:T(8,128)(2,1)S(1)} %collective-permute-done.6.refs_0_), channel_id=1, source_target_pairs={{0,16},{1,17},{2,18},{3,19},{4,20},{5,21},{6,22},{7,23},{8,24},{9,... | collective-permute-start | bytes 1244168 | tf_op jit(solution)/shard_map/ppermute | solution.py:25
  68.6 24.2 %collective-permute-start.15 = (bf16[72,2880]{1,0:T(8,128)(2,1)S(1)}, bf16[72,2880]{1,0:T(8,128)(2,1)S(1)}, u32[]{:S(2)}, u32[]{:S(2)}) collective-permute-start(bf16[72,2880]{1,0:T(8,128)(2,1)S(1)} %get-tuple-element.75), channel_id=1, source_target_pairs={{0,16},{1,17},{2,18},{3,19},{4,20},{5,21},{6,22},{7,23},{8,24},{9,... | collective-permute-start | bytes 1244168 | tf_op jit(solution)/shard_map/ppermute | solution.py:25
  70.3 24.4 %collective-permute-start.4 = (bf16[72,2880]{1,0:T(8,128)(2,1)S(1)}, bf16[72,2880]{1,0:T(8,128)(2,1)S(1)}, u32[]{:S(2)}, u32[]{:S(2)}) collective-permute-start(bf16[72,2880]{1,0:T(8,128)(2,1)S(1)} %get-tuple-element.59), channel_id=1, source_target_pairs={{0,4},{1,5},{2,6},{3,7},{4,0},{5,1},{6,2},{7,3},{8,12},{9,13},{10,... | collective-permute-start | bytes 1244168 | tf_op jit(solution)/shard_map/ppermute | solution.py:25
  92.8 16.4 %collective-permute-start.16 = (bf16[72,2880]{1,0:T(8,128)(2,1)S(1)}, bf16[72,2880]{1,0:T(8,128)(2,1)S(1)}, u32[]{:S(2)}, u32[]{:S(2)}) collective-permute-start(bf16[72,2880]{1,0:T(8,128)(2,1)S(1)} %get-tuple-element.76), channel_id=1, source_target_pairs={{0,16},{1,17},{2,18},{3,19},{4,20},{5,21},{6,22},{7,23},{8,24},{9,... | collective-permute-start | bytes 1244168 | tf_op jit(solution)/shard_map/ppermute | solution.py:25
  93.4 17.3 %collective-permute-start.19 = (bf16[72,2880]{1,0:T(8,128)(2,1)S(1)}, bf16[72,2880]{1,0:T(8,128)(2,1)S(1)}, u32[]{:S(2)}, u32[]{:S(2)}) collective-permute-start(bf16[72,2880]{1,0:T(8,128)(2,1)S(1)} %get-tuple-element.79), channel_id=1, source_target_pairs={{0,2},{1,3},{2,0},{3,1},{4,6},{5,7},{6,4},{7,5},{8,10},{9,11},{10,... | collective-permute-start | bytes 1244168 | tf_op jit(solution)/shard_map/ppermute | solution.py:25
  100.1 18.2 %collective-permute-start.10 = (bf16[72,2880]{1,0:T(8,128)(2,1)S(1)}, bf16[72,2880]{1,0:T(8,128)(2,1)S(1)}, u32[]{:S(2)}, u32[]{:S(2)}) collective-permute-start(bf16[72,2880]{1,0:T(8,128)(2,1)S(1)} %collective-permute-done.4.refs_0_), channel_id=1, source_target_pairs={{0,16},{1,17},{2,18},{3,19},{4,20},{5,21},{6,22},{7,23},{8,24},{9,... | collective-permute-start | bytes 1244168 | tf_op jit(solution)/shard_map/ppermute | solution.py:25
  105.8 18.0 %collective-permute-start.20 = (bf16[72,2880]{1,0:T(8,128)(2,1)S(1)}, bf16[72,2880]{1,0:T(8,128)(2,1)S(1)}, u32[]{:S(2)}, u32[]{:S(2)}) collective-permute-start(bf16[72,2880]{1,0:T(8,128)(2,1)S(1)} %shard_map.63), channel_id=1, source_target_pairs={{0,7},{1,6},{2,5},{3,4},{4,3},{5,2},{6,1},{7,0},{8,15},{9,14},{10,... | collective-permute-start | bytes 1244168 | tf_op jit(solution)/shard_map/ppermute | solution.py:25
  109.2 18.2 %collective-permute-start.21 = (bf16[72,2880]{1,0:T(8,128)(2,1)S(1)}, bf16[72,2880]{1,0:T(8,128)(2,1)S(1)}, u32[]{:S(2)}, u32[]{:S(2)}) collective-permute-start(bf16[72,2880]{1,0:T(8,128)(2,1)S(1)} %get-tuple-element.82), channel_id=1, source_target_pairs={{0,16},{1,17},{2,18},{3,19},{4,20},{5,21},{6,22},{7,23},{8,24},{9,... | collective-permute-start | bytes 1244168 | tf_op jit(solution)/shard_map/ppermute | solution.py:25
  110.7 21.2 %collective-permute-start.27 = (bf16[72,2880]{1,0:T(8,128)(2,1)S(1)}, bf16[72,2880]{1,0:T(8,128)(2,1)S(1)}, u32[]{:S(2)}, u32[]{:S(2)}) collective-permute-start(bf16[72,2880]{1,0:T(8,128)(2,1)S(1)} %get-tuple-element.91), channel_id=1, source_target_pairs={{0,3},{1,2},{2,1},{3,0},{4,7},{5,6},{6,5},{7,4},{8,11},{9,10},{10,... | collective-permute-start | bytes 1244168 | tf_op jit(solution)/shard_map/ppermute | solution.py:25
  127.4 18.2 %collective-permute-start.22 = (bf16[72,2880]{1,0:T(8,128)(2,1)S(1)}, bf16[72,2880]{1,0:T(8,128)(2,1)S(1)}, u32[]{:S(2)}, u32[]{:S(2)}) collective-permute-start(bf16[72,2880]{1,0:T(8,128)(2,1)S(1)} %collective-permute-done.19.refs_0_), channel_id=1, source_target_pairs={{0,16},{1,17},{2,18},{3,19},{4,20},{5,21},{6,22},{7,23},{8,24},{9,... | collective-permute-start | bytes 1244168 | tf_op jit(solution)/shard_map/ppermute | solution.py:25
  129.0 20.4 %collective-permute-start.17 = (bf16[72,2880]{1,0:T(8,128)(2,1)S(1)}, bf16[72,2880]{1,0:T(8,128)(2,1)S(1)}, u32[]{:S(2)}, u32[]{:S(2)}) collective-permute-start(bf16[72,2880]{1,0:T(8,128)(2,1)S(1)} %shard_map.62), channel_id=1, source_target_pairs={{0,6},{1,7},{2,4},{3,5},{4,2},{5,3},{6,0},{7,1},{8,14},{9,15},{10,... | collective-permute-start | bytes 1244168 | tf_op jit(solution)/shard_map/ppermute | solution.py:25
  136.5 16.6 %collective-permute-start.28 = (bf16[72,2880]{1,0:T(8,128)(2,1)S(1)}, bf16[72,2880]{1,0:T(8,128)(2,1)S(1)}, u32[]{:S(2)}, u32[]{:S(2)}) collective-permute-start(bf16[72,2880]{1,0:T(8,128)(2,1)S(1)} %collective-permute-done.27.refs_0_), channel_id=1, source_target_pairs={{0,16},{1,17},{2,18},{3,19},{4,20},{5,21},{6,22},{7,23},{8,24},{9,... | collective-permute-start | bytes 1244168 | tf_op jit(solution)/shard_map/ppermute | solution.py:25
  138.1 35.5 %collective-permute-start.29 = (bf16[72,2880]{1,0:T(8,128)(2,1)S(1)}, bf16[72,2880]{1,0:T(8,128)(2,1)S(1)}, u32[]{:S(2)}, u32[]{:S(2)}) collective-permute-start(bf16[72,2880]{1,0:T(8,128)(2,1)S(1)} %shard_map.70), channel_id=1, source_target_pairs={{0,5},{1,4},{2,7},{3,6},{4,1},{5,0},{6,3},{7,2},{8,13},{9,12},{10,... | collective-permute-start | bytes 1244168 | tf_op jit(solution)/shard_map/ppermute | solution.py:25
  149.4 24.2 %collective-permute-start.23 = (bf16[72,2880]{1,0:T(8,128)(2,1)S(1)}, bf16[72,2880]{1,0:T(8,128)(2,1)S(1)}, u32[]{:S(2)}, u32[]{:S(2)}) collective-permute-start(bf16[72,2880]{1,0:T(8,128)(2,1)S(1)} %get-tuple-element.85), channel_id=1, source_target_pairs={{0,16},{1,17},{2,18},{3,19},{4,20},{5,21},{6,22},{7,23},{8,24},{9,... | collective-permute-start | bytes 1244168 | tf_op jit(solution)/shard_map/ppermute | solution.py:25
  151.1 22.6 %collective-permute-start.25 = (bf16[72,2880]{1,0:T(8,128)(2,1)S(1)}, bf16[72,2880]{1,0:T(8,128)(2,1)S(1)}, u32[]{:S(2)}, u32[]{:S(2)}) collective-permute-start(bf16[72,2880]{1,0:T(8,128)(2,1)S(1)} %shard_map.67), channel_id=1, source_target_pairs={{0,1},{1,0},{2,3},{3,2},{4,5},{5,4},{6,7},{7,6},{8,9},{9,8},{10,11... | collective-permute-start | bytes 1244168 | tf_op jit(solution)/shard_map/ppermute | solution.py:25
  156.9 21.2 %collective-permute-start.18 = (bf16[72,2880]{1,0:T(8,128)(2,1)S(1)}, bf16[72,2880]{1,0:T(8,128)(2,1)S(1)}, u32[]{:S(2)}, u32[]{:S(2)}) collective-permute-start(bf16[72,2880]{1,0:T(8,128)(2,1)S(1)} %shard_map.58), channel_id=1, source_target_pairs={{0,4},{1,5},{2,6},{3,7},{4,0},{5,1},{6,2},{7,3},{8,12},{9,13},{10,... | collective-permute-start | bytes 1244168 | tf_op jit(solution)/shard_map/ppermute | solution.py:25
  (10 other events, 126.4 us)

commit v3 on v2

v3 whole, which is shorter than its diff:
```python
import functools

import jax
import jax.numpy as jnp
from jax import lax
from jax.experimental import pallas as pl
from jax.experimental.pallas import tpu as pltpu
from jax.sharding import PartitionSpec as P

clamp_limit = 7.0
AXES = ("dp", "expert")
VMEM_LIMIT = 12 * 1024 * 1024
F32, BF16 = jnp.float32, jnp.bfloat16
PARAMS = {'far': [4, 2, 5, 6, 3, 7],
 'far_in': 3,
 'far_out': 2,
 'kcost': 6,
 'late': 2,
 'near_in': 1,
 'plan': [('out', 0),
          ('out', 1),
          ('out', 4),
          ('out', 2),
          ('back', 4),
          ('out', 6),
          ('back', 2),
          ('out', 5),
          ('back', 5),
          ('out', 3),
          ('back', 6),
          ('out', 7),
          ('back', 3),
          ('back', 7),
          ('back', 1),
          ('back', 0)],
 'ties': {'dn': (('out', 0), ('z', 1), ('z', 4)),
          'gu': (('out', 0), ('z', 1), ('z', 4)),
          ('back', 0): (('r', 3),),
          ('back', 1): (('r', 6),),
          ('back', 3): (('r', 5),),
          ('back', 7): (('r', 2),),
          ('out', 3): (('r', 4),),
          ('z', 3): (('r', 7),)},
 'xdepth': 3}


def sent_to(array, target):
    dp_size, expert_size = lax.axis_size("dp"), lax.axis_size("expert")
    pairs = []
    for d in range(dp_size):
        for e in range(expert_size):
            td, te = target(d, e)
            pairs.append((d * expert_size + e, td * expert_size + te))
    return lax.ppermute(array, AXES, pairs)


def to_other_core(array):
    return sent_to(array, lambda d, e: (d ^ 1, e))


def to_chip(step):
    dp_size = lax.axis_size("dp")
    return lambda array: sent_to(array, lambda d, e: ((d + 2 * step) % dp_size, e))


def moved(e, k, groups, sign):
    return (e // 2 + sign * (k // 2)) % (groups // 2) * 2 + (e % 2 ^ k % 2)


def to_expert(k):
    return lambda array: sent_to(array, lambda d, e: (d, moved(e, k, lax.axis_size("expert"), 1)))


def from_expert(k):
    return lambda array: sent_to(array, lambda d, e: (d, moved(e, k, lax.axis_size("expert"), -1)))


def after(array, *others):
    return lax.optimization_barrier((array, others))[0] if others else array


class Line:
    def __init__(self, depth):
        self.depth = depth
        self.done = []

    def send(self, array, move, ties=()):
        if len(self.done) >= self.depth:
            ties = [*ties, self.done[-self.depth]]
        moved = move(after(array, *ties))
        self.done.append(moved)
        return moved


def call_kernel(body, out_shapes, args, flops, scratch=()):
    moved = sum(a.size * a.dtype.itemsize for a in args) + sum(s.size * s.dtype.itemsize for s in out_shapes)
    return pl.pallas_call(
        body,
        out_shape=out_shapes,
        in_specs=[pl.BlockSpec(memory_space=pltpu.VMEM)] * len(args),
        out_specs=[pl.BlockSpec(memory_space=pltpu.VMEM)] * len(out_shapes),
        scratch_shapes=[pltpu.VMEM(shape, F32) for shape in scratch],
        compiler_params=pltpu.CompilerParams(vmem_limit_bytes=VMEM_LIMIT),
        cost_estimate=pl.CostEstimate(flops=flops, bytes_accessed=moved, transcendentals=0),
    )(*args)


def packed_rows(capacity, width):
    tiles, rest = divmod(width, 128)
    assert rest * 2 <= 128
    first = -(-(-(-capacity // 2)) // 8) * 8
    return -(-(tiles * capacity + (first if rest else 0)) // 16) * 16, first


def pack(block, capacity, out_ref):
    rows, width = block.shape
    tiles, rest = divmod(width, 128)
    for t in range(tiles):
        out_ref[pl.ds(t * capacity, rows)] = block[:, t * 128 : (t + 1) * 128]
    if rest:
        first = packed_rows(capacity, width)[1]
        left, right = block[:first, tiles * 128 :], block[first:, tiles * 128 :]
        if rows - first < first:
            right = jnp.concatenate([right, jnp.zeros((2 * first - rows, rest), F32)], axis=0)
        parts = [left, right[:first]]
        if rest < 64:
            parts = [jnp.pad(p, ((0, 0), (0, 64 - rest))) for p in parts]
        out_ref[pl.ds(tiles * capacity, first)] = jnp.concatenate(parts, axis=1)


def unpack(packed_ref, capacity, rows, low, out_ref):
    width = out_ref.shape[1]
    tiles, rest = divmod(width, 128)
    for t in range(tiles):
        out_ref[low : low + rows, t * 128 : (t + 1) * 128] = packed_ref[pl.ds(t * capacity, rows)]
    if rest:
        first = packed_rows(capacity, width)[1]
        tail = packed_ref[pl.ds(tiles * capacity, first)]
        out_ref[low : low + first, tiles * 128 :] = tail[:, :rest]
        out_ref[low + first : low + rows, tiles * 128 :] = tail[: rows - first, 64 : 64 + rest]


def pick_kernel(capacity, sel_ref, hid_ref, *refs):
    hid, scratch = hid_ref[...].T, refs[-1]
    for k, out_ref in enumerate(refs[:-1]):
        pack(jnp.dot(sel_ref[k], hid, preferred_element_type=F32), capacity, scratch)
        out_ref[...] = scratch[: out_ref.shape[0]].astype(BF16)


def expert_kernel(capacity, blocks, shards, *refs):
    row_refs, up_refs, down_refs = refs[:blocks], refs[blocks : blocks + shards], refs[blocks + shards : blocks + 2 * shards]
    out_refs, packed, spread = refs[blocks + 2 * shards : -2], refs[-2], refs[-1]
    slots = spread.shape[0] // blocks
    for s, ref in enumerate(row_refs):
        packed[: ref.shape[0]] = ref[...].astype(F32)
        unpack(packed, capacity, slots, s * slots, spread)
    rows = spread[...].astype(BF16)
    dims = (((1,), (1,)), ((), ()))
    total = None
    for up_ref, down_ref in zip(up_refs, down_refs):
        gate = lax.dot_general(rows, up_ref[0], dims, preferred_element_type=F32)
        upper = lax.dot_general(rows, up_ref[1], dims, preferred_element_type=F32)
        gate = jnp.minimum(gate, clamp_limit)
        upper = jnp.clip(upper, -clamp_limit, clamp_limit)
        hidden = ((upper + 1.0) * gate * jax.nn.sigmoid(1.702 * gate)).astype(BF16)
        part = jnp.dot(hidden, down_ref[...], preferred_element_type=F32)
        total = part if total is None else total + part
    for s, out_ref in enumerate(out_refs):
        pack(total[s * slots : (s + 1) * slots], capacity, packed)
        out_ref[...] = packed[: out_ref.shape[0]].astype(out_ref.dtype)


def add_kernel(*refs):
    total = refs[0][...]
    for ref in refs[1:-1]:
        total += ref[...].astype(F32)
    refs[-1][...] = total.astype(BF16)


def combine_kernel(capacity, final, blocks, table_ref, *refs):
    out_ref, packed, spread = refs[-3:]
    total = None
    for k in range(blocks):
        packed[: refs[k].shape[0]] = refs[k][...].astype(F32)
        unpack(packed, capacity, spread.shape[0], 0, spread)
        part = jnp.dot(table_ref[k], spread[...].astype(BF16), preferred_element_type=F32)
        total = part if total is None else total + part
    for ref in refs[blocks:-3]:
        total += ref[...]
    out_ref[...] = total.T.astype(BF16) if final else total


def general_plan(groups):
    return [step for k in range(groups) for step in (("out", k), ("back", k))]


def local(hidden_states, route_ids, route_weights, gate_up_proj, down_proj):
    tok_rows, width = hidden_states.shape
    top_count = route_ids.shape[1]
    units = gate_up_proj.shape[1]
    groups = lax.axis_size("expert")
    chips = lax.axis_size("dp") // 2
    capacity = max(2, 17 * tok_rows * top_count // (16 * groups))
    slots = -(-capacity // 8) * 8
    packed = (packed_rows(capacity, width)[0], 128)
    packed_scratch = (packed[0] + slots, 128)
    half = groups // 2
    me = lax.axis_index("expert")
    known = groups == 8 and chips == 2
    steps = PARAMS["plan"] if known else general_plan(groups)
    tied = PARAMS["ties"] if known else {}
    far_order = PARAMS["far"] if known else list(range(2, groups))

    relative = lax.rem(route_ids // 2 - me // 2 + half, half) * 2 + ((route_ids ^ me) & 1)
    near = relative[:, :, None] == jnp.arange(groups, dtype=jnp.int32)
    member = jnp.any(near, axis=1)
    weight = jnp.sum(jnp.where(near, route_weights[:, :, None].astype(F32), 0.0), axis=1)
    before = jnp.tril(jnp.ones((tok_rows, tok_rows), BF16), -1)
    rank = jnp.dot(before, member.astype(BF16), preferred_element_type=F32).astype(jnp.int32)
    rank = jnp.where(member, rank, -1)
    slot_range = jnp.arange(slots, dtype=jnp.int32)
    chosen = rank.T[:, None, :] == slot_range[None, :, None]
    table = jnp.where(rank.T[:, :, None] == slot_range, weight.T[:, :, None], 0.0).astype(BF16)
    outgoing = call_kernel(
        functools.partial(pick_kernel, capacity),
        [jax.ShapeDtypeStruct(packed, BF16)] * groups,
        (chosen.astype(BF16), hidden_states.T),
        2 * groups * slots * tok_rows * width,
        [packed_scratch],
    )

    between_chips, far_in = Line(PARAMS["xdepth"] * (chips - 1)), Line(PARAMS["far_in"])
    near_in, far_out, near_out = Line(PARAMS["near_in"]), Line(PARAMS["far_out"]), Line(1)
    done, rows = {}, [outgoing[0]] + [None] * (groups - 1)

    def ties_of(name):
        return [done[t] for t in tied.get(name, ()) if t in done]

    for k in far_order:
        rows[k] = done["z", k] = far_in.send(outgoing[k], to_expert(k), ties_of(("z", k)))
    rows[1] = done["z", 1] = near_in.send(outgoing[1], to_expert(1), ties_of(("z", 1)))
    partial, results, weights = {}, [None] * groups, None
    for what, k in steps:
        name = (what, k)
        if what == "out":
            if rows[k] is None:
                rows[k] = done["z", k] = near_in.send(outgoing[k], to_expert(k), ties_of(("z", k)))
            others = [between_chips.send(rows[k], to_chip(s), ties_of(name)) for s in range(1, chips)]
            done[name] = others[0]
            if weights is None:
                own_gu = jnp.transpose(after(gate_up_proj[0], *ties_of("copy")), (1, 0, 2))
                core_gu = done["gu"] = to_other_core(after(own_gu, *ties_of("gu")))
                core_dn = done["dn"] = to_other_core(after(down_proj[0], *ties_of("dn")))
                weights = [own_gu, core_gu, down_proj[0], core_dn]
            partial[k] = call_kernel(
                functools.partial(expert_kernel, capacity, chips, 2),
                [jax.ShapeDtypeStruct(packed, F32)] + [jax.ShapeDtypeStruct(packed, BF16)] * (chips - 1),
                (rows[k], *others, *weights),
                PARAMS["kcost"] * chips * slots * width * 2 * units,
                [packed_scratch, (chips * slots, width)],
            )
            continue
        mine, *foreign = partial[k]
        back = [between_chips.send(v, to_chip(-s), ties_of(name)) for s, v in enumerate(foreign, 1)]
        done[name] = back[0]
        out, = call_kernel(add_kernel, [jax.ShapeDtypeStruct(packed, BF16)], (mine, *back), 0)
        line = far_out if k >= 2 else near_out
        results[k] = done["r", k] = line.send(out, from_expert(k), ties_of(("r", k))) if k else out
    order, sums = [k for what, k in steps if what == "back"], ()
    late = min(PARAMS["late"], groups)
    for first, last in ((0, groups - late), (groups - late, groups)):
        blocks, final = order[first:last], last == groups
        if blocks:
            shape = jax.ShapeDtypeStruct((width, tok_rows), BF16) if final else jax.ShapeDtypeStruct((tok_rows, width), F32)
            sums = call_kernel(
                functools.partial(combine_kernel, capacity, final, len(blocks)),
                [shape],
                (jnp.stack([table[k] for k in blocks]), *[results[k] for k in blocks], *sums),
                2 * len(blocks) * slots * tok_rows * width,
                [packed_scratch, (slots, width)],
            )
    return sums[0].T


def solution(mesh):
    placed = (
        P(("dp", "expert"), None),
        P(("dp", "expert"), None),
        P(("dp", "expert"), None),
        P("expert", "dp", None, None),
        P("expert", "dp", None),
    )
    return jax.shard_map(
        local, mesh=mesh, in_specs=placed, out_specs=P(("dp", "expert"), None), check_vma=False
    )
```

time: 198 us -> 187 us (0.944)
  waiting for transfers between devices: 101 us -> 66.5 us
  starting transfers between devices: 55.3 us -> 75 us
  Pallas kernels: 34.9 us -> 39.1 us
    ppermute x32, waiting for transfers between devices: 101 us -> 66.5 us  [sent_to(): return lax.ppermute(array, AXES, pairs)]
    ppermute x32, starting transfers between devices: 55.3 us -> 75 us  [sent_to(): return lax.ppermute(array, AXES, pairs)]
    pallas_call x18 -> x19, Pallas kernels: 34.9 us -> 39.1 us  [call_kernel(): pl.pallas_call(body, out_shape=out_shapes, in_specs=[pl.BlockSpec(memory_...]
    unnamed x6 -> x11, local copies, waits for them, and re-layouts: 4.11 us -> 3.8 us
  transfers between devices with their start and end apart: 32 -> 32, of which waited for: 19 -> 13; matrix products, arithmetic and copies ran while one was open for 2% -> 2% of each run, Pallas kernels for 16% -> 19%
where the time goes in v3:
time: 187 us; the launch traced here: 186 us
  starting transfers between devices  75 us (40%)
  waiting for transfers between devices  66.5 us (36%)
  Pallas kernels  39.1 us (21%)
  local copies, waits for them, and re-layouts  3.81 us (2%)
    ppermute x32, starting transfers between devices, sent_to(): return lax.ppermute(array, AXES, pairs)  75 us
    ppermute x32, waiting for transfers between devices, sent_to(): return lax.ppermute(array, AXES, pairs)  66.5 us
    pallas_call x19, Pallas kernels, call_kernel(): pl.pallas_call(body, out_shape=out_shapes, in_specs=[pl.BlockSpec(memory_...  39.1 us
    unnamed x11, local copies, waits for them, and re-layouts  3.8 us
  transfers between devices with their start and end apart: 32, of which 13 were waited for; matrix products, arithmetic and copies ran while one was open for 2% of the time, Pallas kernels for 19%

profile of v3, /device:TPU:0, one launch (start us, length us, event | category | flops | bytes accessed | tf_op | source)
XLA Modules:
  0.0 185.9 jit_solution(13056227798223716499)
XLA Ops:
  4.6 3.0 %collective-permute-start = (bf16[1536,128]{1,0:T(8,128)(2,1)S(1)}, bf16[1536,128]{1,0:T(8,128)(2,1)S(1)}, u32[]{:S(2)}, u32[]{:S(2)}) collective-permute-start(bf16[1536,128]{1,0:T(8,128)(2,1)S(1)} %get-tuple-element.51), channel_id=1, source_target_pairs={{0,1},{1,0},{2,3},{3,2},{4,5},{5,4},{6,7},{7,6},{8,9},{9,8},{10,11... | collective-permute-start | bytes 1179656 | tf_op jit(solution)/shard_map/ppermute | solution.py:54
  11.7 2.6 %copy.11 = bf16[1,360,2,2880]{3,1,2,0:T(8,128)(2,1)S(1)} copy(bf16[1,360,2,2880]{3,2,1,0:T(2,128)(2,1)} %param.8) | data formatting | bytes 8294400 | tf_op args[3]
  16.7 10.8 %collective-permute-done.3.refs_0_ = bf16[1536,128]{1,0:T(8,128)(2,1)S(1)} collective-permute-done((bf16[1536,128]{1,0:T(8,128)(2,1)S(1)}, bf16[1536,128]{1,0:T(8,128)(2,1)S(1)}, u32[]{:S(2)}, u32[]{:S(2)}) %collective-permute-start.3) | collective-permute-done | bytes 393248 | tf_op jit(solution)/shard_map/ppermute | solution.py:54
  30.7 9.3 %collective-permute-done.7.refs_1_ = bf16[1536,128]{1,0:T(8,128)(2,1)S(1)} collective-permute-done((bf16[1536,128]{1,0:T(8,128)(2,1)S(1)}, bf16[1536,128]{1,0:T(8,128)(2,1)S(1)}, u32[]{:S(2)}, u32[]{:S(2)}) %collective-permute-start.7) | collective-permute-done | bytes 393248 | tf_op jit(solution)/shard_map/ppermute | solution.py:54
  40.0 4.1 %shard_map.58 = (f32[1536,128]{1,0:T(8,128)S(1)}, bf16[1536,128]{1,0:T(8,128)(2,1)S(1)}) custom-call(bf16[1536,128]{1,0:T(8,128)(2,1)S(1)} %collective-permute-done.3.refs_0_, bf16[1536,128]{1,0:T(8,128)(2,1)S(1)} %collective-permute-done.7.refs_1_, bf16[2,360,2880]{2,1,0:T(8,128)(2,1)S(1)} %bitcast.13, ...), custom_call_target="tpu_custom_call" | custom-call | flops 1791590400 | bytes 14407680 | tf_op jit(solution)/shard_map/pallas_call | solution.py:97
  44.1 3.4 %collective-permute-done.1.refs_1_ = bf16[1536,128]{1,0:T(8,128)(2,1)S(1)} collective-permute-done((bf16[1536,128]{1,0:T(8,128)(2,1)S(1)}, bf16[1536,128]{1,0:T(8,128)(2,1)S(1)}, u32[]{:S(2)}, u32[]{:S(2)}) %collective-permute-start.1) | collective-permute-done | bytes 393248 | tf_op jit(solution)/shard_map/ppermute | solution.py:54
  49.0 3.5 %collective-permute-start.6 = (bf16[1536,128]{1,0:T(8,128)(2,1)S(1)}, bf16[1536,128]{1,0:T(8,128)(2,1)S(1)}, u32[]{:S(2)}, u32[]{:S(2)}) collective-permute-start(bf16[1536,128]{1,0:T(8,128)(2,1)S(1)} %get-tuple-element.59), channel_id=1, source_target_pairs={{0,6},{1,7},{2,0},{3,1},{4,2},{5,3},{6,4},{7,5},{8,14},{9,15},{10,... | collective-permute-start | bytes 1179656 | tf_op jit(solution)/shard_map/ppermute | solution.py:54
  53.1 6.8 %collective-permute-done.9.refs_0_ = bf16[1536,128]{1,0:T(8,128)(2,1)S(1)} collective-permute-done((bf16[1536,128]{1,0:T(8,128)(2,1)S(1)}, bf16[1536,128]{1,0:T(8,128)(2,1)S(1)}, u32[]{:S(2)}, u32[]{:S(2)}) %collective-permute-start.9) | collective-permute-done | bytes 393248 | tf_op jit(solution)/shard_map/ppermute | solution.py:54
  61.4 5.8 %collective-permute-start.23 = (bf16[1536,128]{1,0:T(8,128)(2,1)S(1)}, bf16[1536,128]{1,0:T(8,128)(2,1)S(1)}, u32[]{:S(2)}, u32[]{:S(2)}) collective-permute-start(bf16[1536,128]{1,0:T(8,128)(2,1)S(1)} %get-tuple-element.83), channel_id=1, source_target_pairs={{0,3},{1,2},{2,5},{3,4},{4,7},{5,6},{6,1},{7,0},{8,11},{9,10},{10,... | collective-permute-start | bytes 1179656 | tf_op jit(solution)/shard_map/ppermute | solution.py:54
  68.0 4.1 %shard_map.60 = (f32[1536,128]{1,0:T(8,128)S(1)}, bf16[1536,128]{1,0:T(8,128)(2,1)S(1)}) custom-call(bf16[1536,128]{1,0:T(8,128)(2,1)S(1)} %collective-permute-done.13.refs_0_, bf16[1536,128]{1,0:T(8,128)(2,1)S(1)} %collective-permute-done.14.refs_1_, bf16[2,360,2880]{2,1,0:T(8,128)(2,1)S(1)} %bitcast.14, ...), custom_call_target="tpu_custom_call" | custom-call | flops 1791590400 | bytes 14407680 | tf_op jit(solution)/shard_map/pallas_call | solution.py:97
  73.7 3.9 %collective-permute-start.24 = (bf16[1536,128]{1,0:T(8,128)(2,1)S(1)}, bf16[1536,128]{1,0:T(8,128)(2,1)S(1)}, u32[]{:S(2)}, u32[]{:S(2)}) collective-permute-start(bf16[1536,128]{1,0:T(8,128)(2,1)S(1)} %shard_map.65), channel_id=1, source_target_pairs={{0,4},{1,5},{2,6},{3,7},{4,0},{5,1},{6,2},{7,3},{8,12},{9,13},{10,... | collective-permute-start | bytes 1179656 | tf_op jit(solution)/shard_map/ppermute | solution.py:54
  77.6 3.6 %collective-permute-start.18 = (bf16[1536,128]{1,0:T(8,128)(2,1)S(1)}, bf16[1536,128]{1,0:T(8,128)(2,1)S(1)}, u32[]{:S(2)}, u32[]{:S(2)}) collective-permute-start(bf16[1536,128]{1,0:T(8,128)(2,1)S(1)} %get-tuple-element.75), channel_id=1, source_target_pairs={{0,7},{1,6},{2,1},{3,0},{4,3},{5,2},{6,5},{7,4},{8,15},{9,14},{10,... | collective-permute-start | bytes 1179656 | tf_op jit(solution)/shard_map/ppermute | solution.py:54
  81.2 4.1 %shard_map.62 = (f32[1536,128]{1,0:T(8,128)S(1)}, bf16[1536,128]{1,0:T(8,128)(2,1)S(1)}) custom-call(bf16[1536,128]{1,0:T(8,128)(2,1)S(1)} %collective-permute-done.9.refs_0_, bf16[1536,128]{1,0:T(8,128)(2,1)S(1)} %collective-permute-done.11.refs_1_, bf16[2,360,2880]{2,1,0:T(8,128)(2,1)S(1)} %bitcast.15, ...), custom_call_target="tpu_custom_call" | custom-call | flops 1791590400 | bytes 14407680 | tf_op jit(solution)/shard_map/pallas_call | solution.py:97
  86.9 4.1 %shard_map.57 = (f32[1536,128]{1,0:T(8,128)S(1)}, bf16[1536,128]{1,0:T(8,128)(2,1)S(1)}) custom-call(bf16[1536,128]{1,0:T(8,128)(2,1)S(1)} %collective-permute-done.6.refs_0_, bf16[1536,128]{1,0:T(8,128)(2,1)S(1)} %collective-permute-done.8.refs_1_, bf16[2,360,2880]{2,1,0:T(8,128)(2,1)S(1)} %bitcast.16, ...), custom_call_target="tpu_custom_call" | custom-call | flops 1791590400 | bytes 14407680 | tf_op jit(solution)/shard_map/pallas_call | solution.py:97
  93.4 4.0 %collective-permute-start.16 = (bf16[1536,128]{1,0:T(8,128)(2,1)S(1)}, bf16[1536,128]{1,0:T(8,128)(2,1)S(1)}, u32[]{:S(2)}, u32[]{:S(2)}) collective-permute-start(bf16[1536,128]{1,0:T(8,128)(2,1)S(1)} %shard_map.61), channel_id=1, source_target_pairs={{0,6},{1,7},{2,0},{3,1},{4,2},{5,3},{6,4},{7,5},{8,14},{9,15},{10,... | collective-permute-start | bytes 1179656 | tf_op jit(solution)/shard_map/ppermute | solution.py:54
  103.5 14.7 %collective-permute-done.12.refs_1_ = bf16[1536,128]{1,0:T(8,128)(2,1)S(1)} collective-permute-done((bf16[1536,128]{1,0:T(8,128)(2,1)S(1)}, bf16[1536,128]{1,0:T(8,128)(2,1)S(1)}, u32[]{:S(2)}, u32[]{:S(2)}) %collective-permute-start.12) | collective-permute-done | bytes 393248 | tf_op jit(solution)/shard_map/ppermute | solution.py:54
  118.3 21.0 %collective-permute-start.17 = (bf16[1536,128]{1,0:T(8,128)(2,1)S(1)}, bf16[1536,128]{1,0:T(8,128)(2,1)S(1)}, u32[]{:S(2)}, u32[]{:S(2)}) collective-permute-start(bf16[1536,128]{1,0:T(8,128)(2,1)S(1)} %shard_map.59), channel_id=1, source_target_pairs={{0,2},{1,3},{2,4},{3,5},{4,6},{5,7},{6,0},{7,1},{8,10},{9,11},{10,... | collective-permute-start | bytes 1179656 | tf_op jit(solution)/shard_map/ppermute | solution.py:54
  139.3 4.1 %shard_map.66 = (f32[1536,128]{1,0:T(8,128)S(1)}, bf16[1536,128]{1,0:T(8,128)(2,1)S(1)}) custom-call(bf16[1536,128]{1,0:T(8,128)(2,1)S(1)} %collective-permute-done.23.refs_0_, bf16[1536,128]{1,0:T(8,128)(2,1)S(1)} %collective-permute-done.25.refs_1_, bf16[2,360,2880]{2,1,0:T(8,128)(2,1)S(1)} %bitcast.17, ...), custom_call_target="tpu_custom_call" | custom-call | flops 1791590400 | bytes 14407680 | tf_op jit(solution)/shard_map/pallas_call | solution.py:97
  143.9 4.1 %shard_map.56 = (f32[1536,128]{1,0:T(8,128)S(1)}, bf16[1536,128]{1,0:T(8,128)(2,1)S(1)}) custom-call(bf16[1536,128]{1,0:T(8,128)(2,1)S(1)} %collective-permute-done.refs_0_, bf16[1536,128]{1,0:T(8,128)(2,1)S(1)} %collective-permute-done.1.refs_1_, bf16[2,360,2880]{2,1,0:T(8,128)(2,1)S(1)} %bitcast.18, ...), custom_call_target="tpu_custom_call" | custom-call | flops 1791590400 | bytes 14407680 | tf_op jit(solution)/shard_map/pallas_call | solution.py:97
  148.0 4.1 %shard_map.70 = (f32[1536,128]{1,0:T(8,128)S(1)}, bf16[1536,128]{1,0:T(8,128)(2,1)S(1)}) custom-call(bf16[1536,128]{1,0:T(8,128)(2,1)S(1)} %collective-permute-done.18.refs_0_, bf16[1536,128]{1,0:T(8,128)(2,1)S(1)} %collective-permute-done.20.refs_1_, bf16[2,360,2880]{2,1,0:T(8,128)(2,1)S(1)} %bitcast.19, ...), custom_call_target="tpu_custom_call" | custom-call | flops 1791590400 | bytes 14407680 | tf_op jit(solution)/shard_map/pallas_call | solution.py:97
  154.3 5.2 %collective-permute-start.28 = (bf16[1536,128]{1,0:T(8,128)(2,1)S(1)}, bf16[1536,128]{1,0:T(8,128)(2,1)S(1)}, u32[]{:S(2)}, u32[]{:S(2)}) collective-permute-start(bf16[1536,128]{1,0:T(8,128)(2,1)S(1)} %shard_map.68), channel_id=1, source_target_pairs={{0,7},{1,6},{2,1},{3,0},{4,3},{5,2},{6,5},{7,4},{8,15},{9,14},{10,... | collective-permute-start | bytes 1179656 | tf_op jit(solution)/shard_map/ppermute | solution.py:54
  159.5 4.1 %shard_map.64 = (f32[1536,128]{1,0:T(8,128)S(1)}, bf16[1536,128]{1,0:T(8,128)(2,1)S(1)}) custom-call(bf16[1536,128]{1,0:T(8,128)(2,1)S(1)} %get-tuple-element.52.refs_0_, bf16[1536,128]{1,0:T(8,128)(2,1)S(1)} %collective-permute-done.2.refs_1_, bf16[2,360,2880]{2,1,0:T(8,128)(2,1)S(1)} %bitcast.20, bf16[2,360,2880]{2,1,0:T(8,128)(2,1)S(1)} %collective-permute-done.4.refs_3_, ...), custom_call_target="tpu_custom_call" | custom-call | flops 1791590400 | bytes 14407680 | tf_op jit(solution)/shard_map/pallas_call | solution.py:97
  163.9 4.1 %collective-permute-done.21.refs_1_ = bf16[1536,128]{1,0:T(8,128)(2,1)S(1)} collective-permute-done((bf16[1536,128]{1,0:T(8,128)(2,1)S(1)}, bf16[1536,128]{1,0:T(8,128)(2,1)S(1)}, u32[]{:S(2)}, u32[]{:S(2)}) %collective-permute-start.21) | collective-permute-done | bytes 393248 | tf_op jit(solution)/shard_map/ppermute | solution.py:54
  172.1 9.3 %collective-permute-done.31.refs_5_ = bf16[1536,128]{1,0:T(8,128)(2,1)S(1)} collective-permute-done((bf16[1536,128]{1,0:T(8,128)(2,1)S(1)}, bf16[1536,128]{1,0:T(8,128)(2,1)S(1)}, u32[]{:S(2)}, u32[]{:S(2)}) %collective-permute-start.31) | collective-permute-done | bytes 393248 | tf_op jit(solution)/shard_map/ppermute | solution.py:54
  (80 shorter events, 42.2 us)
Async XLA Ops:
  7.6 19.9 %collective-permute-start.3 = (bf16[1536,128]{1,0:T(8,128)(2,1)S(1)}, bf16[1536,128]{1,0:T(8,128)(2,1)S(1)}, u32[]{:S(2)}, u32[]{:S(2)}) collective-permute-start(bf16[1536,128]{1,0:T(8,128)(2,1)S(1)} %get-tuple-element.53), channel_id=1, source_target_pairs={{0,4},{1,5},{2,6},{3,7},{4,0},{5,1},{6,2},{7,3},{8,12},{9,13},{10,... | collective-permute-start | bytes 1179656 | tf_op jit(solution)/shard_map/ppermute | solution.py:54
  10.2 17.3 %collective-permute-start.2 = (bf16[1536,128]{1,0:T(8,128)(2,1)S(1)}, bf16[1536,128]{1,0:T(8,128)(2,1)S(1)}, u32[]{:S(2)}, u32[]{:S(2)}) collective-permute-start(bf16[1536,128]{1,0:T(8,128)(2,1)S(1)} %get-tuple-element.52.refs_0_), channel_id=1, source_target_pairs={{0,16},{1,17},{2,18},{3,19},{4,20},{5,21},{6,22},{7,23},{8,24},{9,... | collective-permute-start | bytes 1179656 | tf_op jit(solution)/shard_map/ppermute | solution.py:54
  27.5 12.5 %collective-permute-start.4 = (bf16[2,360,2880]{2,1,0:T(8,128)(2,1)S(1)}, bf16[2,360,2880]{2,1,0:T(8,128)(2,1)S(1)}, u32[]{:S(2)}, u32[]{:S(2)}) collective-permute-start(bf16[2,360,2880]{2,1,0:T(8,128)(2,1)S(1)} %bitcast.12), channel_id=1, source_target_pairs={{0,8},{1,9},{2,10},{3,11},{4,12},{5,13},{6,14},{7,15},{8,0},{9,1},... | collective-permute-start | bytes 12441608 | tf_op jit(solution)/shard_map/ppermute | solution.py:54
  29.5 18.0 %collective-permute-start.1 = (bf16[1536,128]{1,0:T(8,128)(2,1)S(1)}, bf16[1536,128]{1,0:T(8,128)(2,1)S(1)}, u32[]{:S(2)}, u32[]{:S(2)}) collective-permute-start(bf16[1536,128]{1,0:T(8,128)(2,1)S(1)} %collective-permute-done.refs_0_), channel_id=1, source_target_pairs={{0,16},{1,17},{2,18},{3,19},{4,20},{5,21},{6,22},{7,23},{8,24},{9,... | collective-permute-start | bytes 1179656 | tf_op jit(solution)/shard_map/ppermute | solution.py:54
  30.1 22.5 %collective-permute-start.13 = (bf16[1536,128]{1,0:T(8,128)(2,1)S(1)}, bf16[1536,128]{1,0:T(8,128)(2,1)S(1)}, u32[]{:S(2)}, u32[]{:S(2)}) collective-permute-start(bf16[1536,128]{1,0:T(8,128)(2,1)S(1)} %get-tuple-element.68), channel_id=1, source_target_pairs={{0,2},{1,3},{2,4},{3,5},{4,6},{5,7},{6,0},{7,1},{8,10},{9,11},{10,... | collective-permute-start | bytes 1179656 | tf_op jit(solution)/shard_map/ppermute | solution.py:54
  40.0 19.8 %collective-permute-start.9 = (bf16[1536,128]{1,0:T(8,128)(2,1)S(1)}, bf16[1536,128]{1,0:T(8,128)(2,1)S(1)}, u32[]{:S(2)}, u32[]{:S(2)}) collective-permute-start(bf16[1536,128]{1,0:T(8,128)(2,1)S(1)} %get-tuple-element.63), channel_id=1, source_target_pairs={{0,5},{1,4},{2,7},{3,6},{4,1},{5,0},{6,3},{7,2},{8,13},{9,12},{10,... | collective-permute-start | bytes 1179656 | tf_op jit(solution)/shard_map/ppermute | solution.py:54
  49.0 18.1 %collective-permute-start.6 = (bf16[1536,128]{1,0:T(8,128)(2,1)S(1)}, bf16[1536,128]{1,0:T(8,128)(2,1)S(1)}, u32[]{:S(2)}, u32[]{:S(2)}) collective-permute-start(bf16[1536,128]{1,0:T(8,128)(2,1)S(1)} %get-tuple-element.59), channel_id=1, source_target_pairs={{0,6},{1,7},{2,0},{3,1},{4,2},{5,3},{6,4},{7,5},{8,14},{9,15},{10,... | collective-permute-start | bytes 1179656 | tf_op jit(solution)/shard_map/ppermute | solution.py:54
  52.5 15.5 %collective-permute-start.14 = (bf16[1536,128]{1,0:T(8,128)(2,1)S(1)}, bf16[1536,128]{1,0:T(8,128)(2,1)S(1)}, u32[]{:S(2)}, u32[]{:S(2)}) collective-permute-start(bf16[1536,128]{1,0:T(8,128)(2,1)S(1)} %collective-permute-done.13.refs_0_), channel_id=1, source_target_pairs={{0,16},{1,17},{2,18},{3,19},{4,20},{5,21},{6,22},{7,23},{8,24},{9,... | collective-permute-start | bytes 1179656 | tf_op jit(solution)/shard_map/ppermute | solution.py:54
  59.9 17.8 %collective-permute-start.11 = (bf16[1536,128]{1,0:T(8,128)(2,1)S(1)}, bf16[1536,128]{1,0:T(8,128)(2,1)S(1)}, u32[]{:S(2)}, u32[]{:S(2)}) collective-permute-start(bf16[1536,128]{1,0:T(8,128)(2,1)S(1)} %collective-permute-done.9.refs_0_), channel_id=1, source_target_pairs={{0,16},{1,17},{2,18},{3,19},{4,20},{5,21},{6,22},{7,23},{8,24},{9,... | collective-permute-start | bytes 1179656 | tf_op jit(solution)/shard_map/ppermute | solution.py:54
  61.4 36.1 %collective-permute-start.23 = (bf16[1536,128]{1,0:T(8,128)(2,1)S(1)}, bf16[1536,128]{1,0:T(8,128)(2,1)S(1)}, u32[]{:S(2)}, u32[]{:S(2)}) collective-permute-start(bf16[1536,128]{1,0:T(8,128)(2,1)S(1)} %get-tuple-element.83), channel_id=1, source_target_pairs={{0,3},{1,2},{2,5},{3,4},{4,7},{5,6},{6,1},{7,0},{8,11},{9,10},{10,... | collective-permute-start | bytes 1179656 | tf_op jit(solution)/shard_map/ppermute | solution.py:54
  67.2 18.1 %collective-permute-start.8 = (bf16[1536,128]{1,0:T(8,128)(2,1)S(1)}, bf16[1536,128]{1,0:T(8,128)(2,1)S(1)}, u32[]{:S(2)}, u32[]{:S(2)}) collective-permute-start(bf16[1536,128]{1,0:T(8,128)(2,1)S(1)} %collective-permute-done.6.refs_0_), channel_id=1, source_target_pairs={{0,16},{1,17},{2,18},{3,19},{4,20},{5,21},{6,22},{7,23},{8,24},{9,... | collective-permute-start | bytes 1179656 | tf_op jit(solution)/shard_map/ppermute | solution.py:54
  72.1 21.2 %collective-permute-start.15 = (bf16[1536,128]{1,0:T(8,128)(2,1)S(1)}, bf16[1536,128]{1,0:T(8,128)(2,1)S(1)}, u32[]{:S(2)}, u32[]{:S(2)}) collective-permute-start(bf16[1536,128]{1,0:T(8,128)(2,1)S(1)} %get-tuple-element.72), channel_id=1, source_target_pairs={{0,16},{1,17},{2,18},{3,19},{4,20},{5,21},{6,22},{7,23},{8,24},{9,... | collective-permute-start | bytes 1179656 | tf_op jit(solution)/shard_map/ppermute | solution.py:54
  73.7 23.7 %collective-permute-start.24 = (bf16[1536,128]{1,0:T(8,128)(2,1)S(1)}, bf16[1536,128]{1,0:T(8,128)(2,1)S(1)}, u32[]{:S(2)}, u32[]{:S(2)}) collective-permute-start(bf16[1536,128]{1,0:T(8,128)(2,1)S(1)} %shard_map.65), channel_id=1, source_target_pairs={{0,4},{1,5},{2,6},{3,7},{4,0},{5,1},{6,2},{7,3},{8,12},{9,13},{10,... | collective-permute-start | bytes 1179656 | tf_op jit(solution)/shard_map/ppermute | solution.py:54
  77.6 23.9 %collective-permute-start.18 = (bf16[1536,128]{1,0:T(8,128)(2,1)S(1)}, bf16[1536,128]{1,0:T(8,128)(2,1)S(1)}, u32[]{:S(2)}, u32[]{:S(2)}) collective-permute-start(bf16[1536,128]{1,0:T(8,128)(2,1)S(1)} %get-tuple-element.75), channel_id=1, source_target_pairs={{0,7},{1,6},{2,1},{3,0},{4,3},{5,2},{6,5},{7,4},{8,15},{9,14},{10,... | collective-permute-start | bytes 1179656 | tf_op jit(solution)/shard_map/ppermute | solution.py:54
  85.3 16.0 %collective-permute-start.19 = (bf16[1536,128]{1,0:T(8,128)(2,1)S(1)}, bf16[1536,128]{1,0:T(8,128)(2,1)S(1)}, u32[]{:S(2)}, u32[]{:S(2)}) collective-permute-start(bf16[1536,128]{1,0:T(8,128)(2,1)S(1)} %get-tuple-element.77), channel_id=1, source_target_pairs={{0,16},{1,17},{2,18},{3,19},{4,20},{5,21},{6,22},{7,23},{8,24},{9,... | collective-permute-start | bytes 1179656 | tf_op jit(solution)/shard_map/ppermute | solution.py:54
  93.4 24.9 %collective-permute-start.16 = (bf16[1536,128]{1,0:T(8,128)(2,1)S(1)}, bf16[1536,128]{1,0:T(8,128)(2,1)S(1)}, u32[]{:S(2)}, u32[]{:S(2)}) collective-permute-start(bf16[1536,128]{1,0:T(8,128)(2,1)S(1)} %shard_map.61), channel_id=1, source_target_pairs={{0,6},{1,7},{2,0},{3,1},{4,2},{5,3},{6,4},{7,5},{8,14},{9,15},{10,... | collective-permute-start | bytes 1179656 | tf_op jit(solution)/shard_map/ppermute | solution.py:54
  97.5 41.8 %collective-permute-start.25 = (bf16[1536,128]{1,0:T(8,128)(2,1)S(1)}, bf16[1536,128]{1,0:T(8,128)(2,1)S(1)}, u32[]{:S(2)}, u32[]{:S(2)}) collective-permute-start(bf16[1536,128]{1,0:T(8,128)(2,1)S(1)} %collective-permute-done.23.refs_0_), channel_id=1, source_target_pairs={{0,16},{1,17},{2,18},{3,19},{4,20},{5,21},{6,22},{7,23},{8,24},{9,... | collective-permute-start | bytes 1179656 | tf_op jit(solution)/shard_map/ppermute | solution.py:54
  99.0 19.2 %collective-permute-start.12 = (bf16[1536,128]{1,0:T(8,128)(2,1)S(1)}, bf16[1536,128]{1,0:T(8,128)(2,1)S(1)}, u32[]{:S(2)}, u32[]{:S(2)}) collective-permute-start(bf16[1536,128]{1,0:T(8,128)(2,1)S(1)} %get-tuple-element.67), channel_id=1, source_target_pairs={{0,16},{1,17},{2,18},{3,19},{4,20},{5,21},{6,22},{7,23},{8,24},{9,... | collective-permute-start | bytes 1179656 | tf_op jit(solution)/shard_map/ppermute | solution.py:54
  101.4 41.9 %collective-permute-start.26 = (bf16[1536,128]{1,0:T(8,128)(2,1)S(1)}, bf16[1536,128]{1,0:T(8,128)(2,1)S(1)}, u32[]{:S(2)}, u32[]{:S(2)}) collective-permute-start(bf16[1536,128]{1,0:T(8,128)(2,1)S(1)} %shard_map.67), channel_id=1, source_target_pairs={{0,5},{1,4},{2,7},{3,6},{4,1},{5,0},{6,3},{7,2},{8,13},{9,12},{10,... | collective-permute-start | bytes 1179656 | tf_op jit(solution)/shard_map/ppermute | solution.py:54
  101.5 46.5 %collective-permute-start.20 = (bf16[1536,128]{1,0:T(8,128)(2,1)S(1)}, bf16[1536,128]{1,0:T(8,128)(2,1)S(1)}, u32[]{:S(2)}, u32[]{:S(2)}) collective-permute-start(bf16[1536,128]{1,0:T(8,128)(2,1)S(1)} %collective-permute-done.18.refs_0_), channel_id=1, source_target_pairs={{0,16},{1,17},{2,18},{3,19},{4,20},{5,21},{6,22},{7,23},{8,24},{9,... | collective-permute-start | bytes 1179656 | tf_op jit(solution)/shard_map/ppermute | solution.py:54
  118.3 35.3 %collective-permute-start.17 = (bf16[1536,128]{1,0:T(8,128)(2,1)S(1)}, bf16[1536,128]{1,0:T(8,128)(2,1)S(1)}, u32[]{:S(2)}, u32[]{:S(2)}) collective-permute-start(bf16[1536,128]{1,0:T(8,128)(2,1)S(1)} %shard_map.59), channel_id=1, source_target_pairs={{0,2},{1,3},{2,4},{3,5},{4,6},{5,7},{6,0},{7,1},{8,10},{9,11},{10,... | collective-permute-start | bytes 1179656 | tf_op jit(solution)/shard_map/ppermute | solution.py:54
  153.6 14.4 %collective-permute-start.21 = (bf16[1536,128]{1,0:T(8,128)(2,1)S(1)}, bf16[1536,128]{1,0:T(8,128)(2,1)S(1)}, u32[]{:S(2)}, u32[]{:S(2)}) collective-permute-start(bf16[1536,128]{1,0:T(8,128)(2,1)S(1)} %get-tuple-element.79), channel_id=1, source_target_pairs={{0,16},{1,17},{2,18},{3,19},{4,20},{5,21},{6,22},{7,23},{8,24},{9,... | collective-permute-start | bytes 1179656 | tf_op jit(solution)/shard_map/ppermute | solution.py:54
  154.3 17.2 %collective-permute-start.28 = (bf16[1536,128]{1,0:T(8,128)(2,1)S(1)}, bf16[1536,128]{1,0:T(8,128)(2,1)S(1)}, u32[]{:S(2)}, u32[]{:S(2)}) collective-permute-start(bf16[1536,128]{1,0:T(8,128)(2,1)S(1)} %shard_map.68), channel_id=1, source_target_pairs={{0,7},{1,6},{2,1},{3,0},{4,3},{5,2},{6,5},{7,4},{8,15},{9,14},{10,... | collective-permute-start | bytes 1179656 | tf_op jit(solution)/shard_map/ppermute | solution.py:54
  168.1 16.3 %collective-permute-start.22 = (bf16[1536,128]{1,0:T(8,128)(2,1)S(1)}, bf16[1536,128]{1,0:T(8,128)(2,1)S(1)}, u32[]{:S(2)}, u32[]{:S(2)}) collective-permute-start(bf16[1536,128]{1,0:T(8,128)(2,1)S(1)} %shard_map.63), channel_id=1, source_target_pairs={{0,1},{1,0},{2,3},{3,2},{4,5},{5,4},{6,7},{7,6},{8,9},{9,8},{10,11... | collective-permute-start | bytes 1179656 | tf_op jit(solution)/shard_map/ppermute | solution.py:54
  (11 other events, 134.5 us)

commit v4 on v3

--- a/solution.py
+++ b/solution.py
@@ -27,10 +27,10 @@
           ('out', 5),
           ('back', 5),
           ('out', 3),
+          ('out', 7),
           ('back', 6),
-          ('out', 7),
+          ('back', 7),
           ('back', 3),
-          ('back', 7),
           ('back', 1),
           ('back', 0)],
  'ties': {'dn': (('out', 0), ('z', 1), ('z', 4)),
@@ -38,6 +38,7 @@
           ('back', 0): (('r', 3),),
           ('back', 1): (('r', 6),),
           ('back', 3): (('r', 5),),
+          ('back', 4): ('dn',),
           ('back', 7): (('r', 2),),
           ('out', 3): (('r', 4),),
           ('z', 3): (('r', 7),)},

time: 187 us -> 176 us (0.941)
  starting transfers between devices: 75 us -> 42.1 us
  waiting for transfers between devices: 66.5 us -> 89.5 us
    ppermute x32, starting transfers between devices: 75 us -> 42.1 us  [sent_to(): return lax.ppermute(array, AXES, pairs)]
    ppermute x32, waiting for transfers between devices: 66.5 us -> 89.5 us  [sent_to(): return lax.ppermute(array, AXES, pairs)]
    unnamed x11 -> x7, local copies, waits for them, and re-layouts: 3.8 us -> 3.77 us
  transfers between devices with their start and end apart: 32 -> 32, of which waited for: 13 -> 21; matrix products, arithmetic and copies ran while one was open for 2% -> 2% of each run, Pallas kernels for 19% -> 20%
where the time goes in v4:
time: 176 us
  waiting for transfers between devices  89.5 us (51%)
  starting transfers between devices  42.1 us (24%)
  Pallas kernels  38.9 us (22%)
  local copies, waits for them, and re-layouts  3.79 us (2%)
    ppermute x32, waiting for transfers between devices, sent_to(): return lax.ppermute(array, AXES, pairs)  89.5 us
    ppermute x32, starting transfers between devices, sent_to(): return lax.ppermute(array, AXES, pairs)  42.1 us
    pallas_call x19, Pallas kernels, call_kernel(): pl.pallas_call(body, out_shape=out_shapes, in_specs=[pl.BlockSpec(memory_...  38.9 us
    unnamed x7, local copies, waits for them, and re-layouts  3.77 us
  transfers between devices with their start and end apart: 32, of which 21 were waited for; matrix products, arithmetic and copies ran while one was open for 2% of the time, Pallas kernels for 20%

profile of v4, /device:TPU:0, one launch (start us, length us, event | category | flops | bytes accessed | tf_op | source)
XLA Modules:
  0.0 175.8 jit_solution(434683056170219589)
XLA Ops:
  4.6 3.0 %collective-permute-start.2 = (bf16[1536,128]{1,0:T(8,128)(2,1)S(1)}, bf16[1536,128]{1,0:T(8,128)(2,1)S(1)}, u32[]{:S(2)}, u32[]{:S(2)}) collective-permute-start(bf16[1536,128]{1,0:T(8,128)(2,1)S(1)} %get-tuple-element.52.refs_0_), channel_id=1, source_target_pairs={{0,16},{1,17},{2,18},{3,19},{4,20},{5,21},{6,22},{7,23},{8,24},{9,... | collective-permute-start | bytes 1179656 | tf_op jit(solution)/shard_map/ppermute | solution.py:55
  16.7 10.8 %collective-permute-done.3.refs_0_ = bf16[1536,128]{1,0:T(8,128)(2,1)S(1)} collective-permute-done((bf16[1536,128]{1,0:T(8,128)(2,1)S(1)}, bf16[1536,128]{1,0:T(8,128)(2,1)S(1)}, u32[]{:S(2)}, u32[]{:S(2)}) %collective-permute-start.3) | collective-permute-done | bytes 393248 | tf_op jit(solution)/shard_map/ppermute | solution.py:55
  30.7 9.3 %collective-permute-done.7.refs_1_ = bf16[1536,128]{1,0:T(8,128)(2,1)S(1)} collective-permute-done((bf16[1536,128]{1,0:T(8,128)(2,1)S(1)}, bf16[1536,128]{1,0:T(8,128)(2,1)S(1)}, u32[]{:S(2)}, u32[]{:S(2)}) %collective-permute-start.7) | collective-permute-done | bytes 393248 | tf_op jit(solution)/shard_map/ppermute | solution.py:55
  40.5 4.1 %shard_map.58 = (f32[1536,128]{1,0:T(8,128)S(1)}, bf16[1536,128]{1,0:T(8,128)(2,1)S(1)}) custom-call(bf16[1536,128]{1,0:T(8,128)(2,1)S(1)} %collective-permute-done.3.refs_0_, bf16[1536,128]{1,0:T(8,128)(2,1)S(1)} %collective-permute-done.7.refs_1_, bf16[2,360,2880]{2,1,0:T(8,128)(2,1)S(1)} %bitcast.13, ...), custom_call_target="tpu_custom_call" | custom-call | flops 1791590400 | bytes 14407680 | tf_op jit(solution)/shard_map/pallas_call | solution.py:98
  48.0 3.5 %collective-permute-start.6 = (bf16[1536,128]{1,0:T(8,128)(2,1)S(1)}, bf16[1536,128]{1,0:T(8,128)(2,1)S(1)}, u32[]{:S(2)}, u32[]{:S(2)}) collective-permute-start(bf16[1536,128]{1,0:T(8,128)(2,1)S(1)} %get-tuple-element.59), channel_id=1, source_target_pairs={{0,6},{1,7},{2,0},{3,1},{4,2},{5,3},{6,4},{7,5},{8,14},{9,15},{10,... | collective-permute-start | bytes 1179656 | tf_op jit(solution)/shard_map/ppermute | solution.py:55
  53.0 7.5 %collective-permute-done.9.refs_0_ = bf16[1536,128]{1,0:T(8,128)(2,1)S(1)} collective-permute-done((bf16[1536,128]{1,0:T(8,128)(2,1)S(1)}, bf16[1536,128]{1,0:T(8,128)(2,1)S(1)}, u32[]{:S(2)}, u32[]{:S(2)}) %collective-permute-start.9) | collective-permute-done | bytes 393248 | tf_op jit(solution)/shard_map/ppermute | solution.py:55
  61.1 5.1 %collective-permute-done.6.refs_0_ = bf16[1536,128]{1,0:T(8,128)(2,1)S(1)} collective-permute-done((bf16[1536,128]{1,0:T(8,128)(2,1)S(1)}, bf16[1536,128]{1,0:T(8,128)(2,1)S(1)}, u32[]{:S(2)}, u32[]{:S(2)}) %collective-permute-start.6) | collective-permute-done | bytes 393248 | tf_op jit(solution)/shard_map/ppermute | solution.py:55
  67.7 3.7 %collective-permute-start.25 = (bf16[1536,128]{1,0:T(8,128)(2,1)S(1)}, bf16[1536,128]{1,0:T(8,128)(2,1)S(1)}, u32[]{:S(2)}, u32[]{:S(2)}) collective-permute-start(bf16[1536,128]{1,0:T(8,128)(2,1)S(1)} %get-tuple-element.88), channel_id=1, source_target_pairs={{0,7},{1,6},{2,1},{3,0},{4,3},{5,2},{6,5},{7,4},{8,15},{9,14},{10,... | collective-permute-start | bytes 1179656 | tf_op jit(solution)/shard_map/ppermute | solution.py:55
  71.4 4.1 %shard_map.61 = (f32[1536,128]{1,0:T(8,128)S(1)}, bf16[1536,128]{1,0:T(8,128)(2,1)S(1)}) custom-call(bf16[1536,128]{1,0:T(8,128)(2,1)S(1)} %collective-permute-done.14.refs_0_, bf16[1536,128]{1,0:T(8,128)(2,1)S(1)} %collective-permute-done.15.refs_1_, bf16[2,360,2880]{2,1,0:T(8,128)(2,1)S(1)} %bitcast.14, ...), custom_call_target="tpu_custom_call" | custom-call | flops 1791590400 | bytes 14407680 | tf_op jit(solution)/shard_map/pallas_call | solution.py:98
  77.0 4.1 %shard_map.59 = (f32[1536,128]{1,0:T(8,128)S(1)}, bf16[1536,128]{1,0:T(8,128)(2,1)S(1)}) custom-call(bf16[1536,128]{1,0:T(8,128)(2,1)S(1)} %collective-permute-done.9.refs_0_, bf16[1536,128]{1,0:T(8,128)(2,1)S(1)} %collective-permute-done.11.refs_1_, bf16[2,360,2880]{2,1,0:T(8,128)(2,1)S(1)} %bitcast.15, ...), custom_call_target="tpu_custom_call" | custom-call | flops 1791590400 | bytes 14407680 | tf_op jit(solution)/shard_map/pallas_call | solution.py:98
  81.0 3.8 %collective-permute-done.8.refs_1_ = bf16[1536,128]{1,0:T(8,128)(2,1)S(1)} collective-permute-done((bf16[1536,128]{1,0:T(8,128)(2,1)S(1)}, bf16[1536,128]{1,0:T(8,128)(2,1)S(1)}, u32[]{:S(2)}, u32[]{:S(2)}) %collective-permute-start.8) | collective-permute-done | bytes 393248 | tf_op jit(solution)/shard_map/ppermute | solution.py:55
  86.9 4.2 %collective-permute-done.21.refs_0_ = bf16[1536,128]{1,0:T(8,128)(2,1)S(1)} collective-permute-done((bf16[1536,128]{1,0:T(8,128)(2,1)S(1)}, bf16[1536,128]{1,0:T(8,128)(2,1)S(1)}, u32[]{:S(2)}, u32[]{:S(2)}) %collective-permute-start.21) | collective-permute-done | bytes 393248 | tf_op jit(solution)/shard_map/ppermute | solution.py:55
  93.3 11.7 %collective-permute-done.22.refs_0_ = bf16[1536,128]{1,0:T(8,128)(2,1)S(1)} collective-permute-done((bf16[1536,128]{1,0:T(8,128)(2,1)S(1)}, bf16[1536,128]{1,0:T(8,128)(2,1)S(1)}, u32[]{:S(2)}, u32[]{:S(2)}) %collective-permute-start.22) | collective-permute-done | bytes 393248 | tf_op jit(solution)/shard_map/ppermute | solution.py:55
  106.7 4.1 %shard_map.57 = (f32[1536,128]{1,0:T(8,128)S(1)}, bf16[1536,128]{1,0:T(8,128)(2,1)S(1)}) custom-call(bf16[1536,128]{1,0:T(8,128)(2,1)S(1)} %collective-permute-done.6.refs_0_, bf16[1536,128]{1,0:T(8,128)(2,1)S(1)} %collective-permute-done.8.refs_1_, bf16[2,360,2880]{2,1,0:T(8,128)(2,1)S(1)} %bitcast.16, ...), custom_call_target="tpu_custom_call" | custom-call | flops 1791590400 | bytes 14407680 | tf_op jit(solution)/shard_map/pallas_call | solution.py:98
  111.4 3.2 %collective-permute-start.17 = (bf16[1536,128]{1,0:T(8,128)(2,1)S(1)}, bf16[1536,128]{1,0:T(8,128)(2,1)S(1)}, u32[]{:S(2)}, u32[]{:S(2)}) collective-permute-start(bf16[1536,128]{1,0:T(8,128)(2,1)S(1)} %shard_map.62), channel_id=1, source_target_pairs={{0,6},{1,7},{2,0},{3,1},{4,2},{5,3},{6,4},{7,5},{8,14},{9,15},{10,... | collective-permute-start | bytes 1179656 | tf_op jit(solution)/shard_map/ppermute | solution.py:55
  114.7 3.7 %collective-permute-done.23.refs_1_ = bf16[1536,128]{1,0:T(8,128)(2,1)S(1)} collective-permute-done((bf16[1536,128]{1,0:T(8,128)(2,1)S(1)}, bf16[1536,128]{1,0:T(8,128)(2,1)S(1)}, u32[]{:S(2)}, u32[]{:S(2)}) %collective-permute-start.23) | collective-permute-done | bytes 393248 | tf_op jit(solution)/shard_map/ppermute | solution.py:55
  118.4 4.1 %shard_map.66 = (f32[1536,128]{1,0:T(8,128)S(1)}, bf16[1536,128]{1,0:T(8,128)(2,1)S(1)}) custom-call(bf16[1536,128]{1,0:T(8,128)(2,1)S(1)} %collective-permute-done.21.refs_0_, bf16[1536,128]{1,0:T(8,128)(2,1)S(1)} %collective-permute-done.23.refs_1_, bf16[2,360,2880]{2,1,0:T(8,128)(2,1)S(1)} %bitcast.17, ...), custom_call_target="tpu_custom_call" | custom-call | flops 1791590400 | bytes 14407680 | tf_op jit(solution)/shard_map/pallas_call | solution.py:98
  122.4 5.1 %collective-permute-done.24.refs_2_ = bf16[1536,128]{1,0:T(8,128)(2,1)S(1)} collective-permute-done((bf16[1536,128]{1,0:T(8,128)(2,1)S(1)}, bf16[1536,128]{1,0:T(8,128)(2,1)S(1)}, u32[]{:S(2)}, u32[]{:S(2)}) %collective-permute-start.24) | collective-permute-done | bytes 393248 | tf_op jit(solution)/shard_map/ppermute | solution.py:55
  130.6 4.4 %collective-permute-start.18 = (bf16[1536,128]{1,0:T(8,128)(2,1)S(1)}, bf16[1536,128]{1,0:T(8,128)(2,1)S(1)}, u32[]{:S(2)}, u32[]{:S(2)}) collective-permute-start(bf16[1536,128]{1,0:T(8,128)(2,1)S(1)} %shard_map.60), channel_id=1, source_target_pairs={{0,2},{1,3},{2,4},{3,5},{4,6},{5,7},{6,0},{7,1},{8,10},{9,11},{10,... | collective-permute-start | bytes 1179656 | tf_op jit(solution)/shard_map/ppermute | solution.py:55
  134.9 4.1 %shard_map.56 = (f32[1536,128]{1,0:T(8,128)S(1)}, bf16[1536,128]{1,0:T(8,128)(2,1)S(1)}) custom-call(bf16[1536,128]{1,0:T(8,128)(2,1)S(1)} %collective-permute-done.refs_0_, bf16[1536,128]{1,0:T(8,128)(2,1)S(1)} %collective-permute-done.1.refs_1_, bf16[2,360,2880]{2,1,0:T(8,128)(2,1)S(1)} %bitcast.18, ...), custom_call_target="tpu_custom_call" | custom-call | flops 1791590400 | bytes 14407680 | tf_op jit(solution)/shard_map/pallas_call | solution.py:98
  139.0 4.1 %shard_map.69 = (f32[1536,128]{1,0:T(8,128)S(1)}, bf16[1536,128]{1,0:T(8,128)(2,1)S(1)}) custom-call(bf16[1536,128]{1,0:T(8,128)(2,1)S(1)} %collective-permute-done.25.refs_0_, bf16[1536,128]{1,0:T(8,128)(2,1)S(1)} %collective-permute-done.26.refs_1_, bf16[2,360,2880]{2,1,0:T(8,128)(2,1)S(1)} %bitcast.19, ...), custom_call_target="tpu_custom_call" | custom-call | flops 1791590400 | bytes 14407680 | tf_op jit(solution)/shard_map/pallas_call | solution.py:98
  149.4 4.1 %shard_map.64 = (f32[1536,128]{1,0:T(8,128)S(1)}, bf16[1536,128]{1,0:T(8,128)(2,1)S(1)}) custom-call(bf16[1536,128]{1,0:T(8,128)(2,1)S(1)} %get-tuple-element.52.refs_0_, bf16[1536,128]{1,0:T(8,128)(2,1)S(1)} %collective-permute-done.2.refs_1_, bf16[2,360,2880]{2,1,0:T(8,128)(2,1)S(1)} %bitcast.20, bf16[2,360,2880]{2,1,0:T(8,128)(2,1)S(1)} %collective-permute-done.4.refs_3_, ...), custom_call_target="tpu_custom_call" | custom-call | flops 1791590400 | bytes 14407680 | tf_op jit(solution)/shard_map/pallas_call | solution.py:98
  158.7 5.0 %collective-permute-done.19.refs_1_ = bf16[1536,128]{1,0:T(8,128)(2,1)S(1)} collective-permute-done((bf16[1536,128]{1,0:T(8,128)(2,1)S(1)}, bf16[1536,128]{1,0:T(8,128)(2,1)S(1)}, u32[]{:S(2)}, u32[]{:S(2)}) %collective-permute-start.19) | collective-permute-done | bytes 393248 | tf_op jit(solution)/shard_map/ppermute | solution.py:55
  169.7 4.5 %collective-permute-done.20.refs_0_ = bf16[1536,128]{1,0:T(8,128)(2,1)S(1)} collective-permute-done((bf16[1536,128]{1,0:T(8,128)(2,1)S(1)}, bf16[1536,128]{1,0:T(8,128)(2,1)S(1)}, u32[]{:S(2)}, u32[]{:S(2)}) %collective-permute-start.20) | collective-permute-done | bytes 393248 | tf_op jit(solution)/shard_map/ppermute | solution.py:55
  (78 shorter events, 54.5 us)
Async XLA Ops:
  7.6 19.9 %collective-permute-start.3 = (bf16[1536,128]{1,0:T(8,128)(2,1)S(1)}, bf16[1536,128]{1,0:T(8,128)(2,1)S(1)}, u32[]{:S(2)}, u32[]{:S(2)}) collective-permute-start(bf16[1536,128]{1,0:T(8,128)(2,1)S(1)} %get-tuple-element.53), channel_id=1, source_target_pairs={{0,4},{1,5},{2,6},{3,7},{4,0},{5,1},{6,2},{7,3},{8,12},{9,13},{10,... | collective-permute-start | bytes 1179656 | tf_op jit(solution)/shard_map/ppermute | solution.py:55
  10.2 17.3 %collective-permute-start = (bf16[1536,128]{1,0:T(8,128)(2,1)S(1)}, bf16[1536,128]{1,0:T(8,128)(2,1)S(1)}, u32[]{:S(2)}, u32[]{:S(2)}) collective-permute-start(bf16[1536,128]{1,0:T(8,128)(2,1)S(1)} %get-tuple-element.51), channel_id=1, source_target_pairs={{0,1},{1,0},{2,3},{3,2},{4,5},{5,4},{6,7},{7,6},{8,9},{9,8},{10,11... | collective-permute-start | bytes 1179656 | tf_op jit(solution)/shard_map/ppermute | solution.py:55
  27.5 13.0 %collective-permute-start.4 = (bf16[2,360,2880]{2,1,0:T(8,128)(2,1)S(1)}, bf16[2,360,2880]{2,1,0:T(8,128)(2,1)S(1)}, u32[]{:S(2)}, u32[]{:S(2)}) collective-permute-start(bf16[2,360,2880]{2,1,0:T(8,128)(2,1)S(1)} %bitcast.12), channel_id=1, source_target_pairs={{0,8},{1,9},{2,10},{3,11},{4,12},{5,13},{6,14},{7,15},{8,0},{9,1},... | collective-permute-start | bytes 12441608 | tf_op jit(solution)/shard_map/ppermute | solution.py:55
  28.5 19.0 %collective-permute-start.1 = (bf16[1536,128]{1,0:T(8,128)(2,1)S(1)}, bf16[1536,128]{1,0:T(8,128)(2,1)S(1)}, u32[]{:S(2)}, u32[]{:S(2)}) collective-permute-start(bf16[1536,128]{1,0:T(8,128)(2,1)S(1)} %collective-permute-done.refs_0_), channel_id=1, source_target_pairs={{0,16},{1,17},{2,18},{3,19},{4,20},{5,21},{6,22},{7,23},{8,24},{9,... | collective-permute-start | bytes 1179656 | tf_op jit(solution)/shard_map/ppermute | solution.py:55
  30.0 21.5 %collective-permute-start.14 = (bf16[1536,128]{1,0:T(8,128)(2,1)S(1)}, bf16[1536,128]{1,0:T(8,128)(2,1)S(1)}, u32[]{:S(2)}, u32[]{:S(2)}) collective-permute-start(bf16[1536,128]{1,0:T(8,128)(2,1)S(1)} %get-tuple-element.70), channel_id=1, source_target_pairs={{0,2},{1,3},{2,4},{3,5},{4,6},{5,7},{6,0},{7,1},{8,10},{9,11},{10,... | collective-permute-start | bytes 1179656 | tf_op jit(solution)/shard_map/ppermute | solution.py:55
  40.0 20.5 %collective-permute-start.9 = (bf16[1536,128]{1,0:T(8,128)(2,1)S(1)}, bf16[1536,128]{1,0:T(8,128)(2,1)S(1)}, u32[]{:S(2)}, u32[]{:S(2)}) collective-permute-start(bf16[1536,128]{1,0:T(8,128)(2,1)S(1)} %get-tuple-element.63), channel_id=1, source_target_pairs={{0,5},{1,4},{2,7},{3,6},{4,1},{5,0},{6,3},{7,2},{8,13},{9,12},{10,... | collective-permute-start | bytes 1179656 | tf_op jit(solution)/shard_map/ppermute | solution.py:55
  47.5 13.0 %collective-permute-start.10 = (bf16[1536,128]{1,0:T(8,128)(2,1)S(1)}, bf16[1536,128]{1,0:T(8,128)(2,1)S(1)}, u32[]{:S(2)}, u32[]{:S(2)}) collective-permute-start(bf16[1536,128]{1,0:T(8,128)(2,1)S(1)} %get-tuple-element.65), channel_id=1, source_target_pairs={{0,16},{1,17},{2,18},{3,19},{4,20},{5,21},{6,22},{7,23},{8,24},{9,... | collective-permute-start | bytes 1179656 | tf_op jit(solution)/shard_map/ppermute | solution.py:55
  48.0 18.2 %collective-permute-start.6 = (bf16[1536,128]{1,0:T(8,128)(2,1)S(1)}, bf16[1536,128]{1,0:T(8,128)(2,1)S(1)}, u32[]{:S(2)}, u32[]{:S(2)}) collective-permute-start(bf16[1536,128]{1,0:T(8,128)(2,1)S(1)} %get-tuple-element.59), channel_id=1, source_target_pairs={{0,6},{1,7},{2,0},{3,1},{4,2},{5,3},{6,4},{7,5},{8,14},{9,15},{10,... | collective-permute-start | bytes 1179656 | tf_op jit(solution)/shard_map/ppermute | solution.py:55
  51.6 19.9 %collective-permute-start.15 = (bf16[1536,128]{1,0:T(8,128)(2,1)S(1)}, bf16[1536,128]{1,0:T(8,128)(2,1)S(1)}, u32[]{:S(2)}, u32[]{:S(2)}) collective-permute-start(bf16[1536,128]{1,0:T(8,128)(2,1)S(1)} %collective-permute-done.14.refs_0_), channel_id=1, source_target_pairs={{0,16},{1,17},{2,18},{3,19},{4,20},{5,21},{6,22},{7,23},{8,24},{9,... | collective-permute-start | bytes 1179656 | tf_op jit(solution)/shard_map/ppermute | solution.py:55
  60.5 15.9 %collective-permute-start.11 = (bf16[1536,128]{1,0:T(8,128)(2,1)S(1)}, bf16[1536,128]{1,0:T(8,128)(2,1)S(1)}, u32[]{:S(2)}, u32[]{:S(2)}) collective-permute-start(bf16[1536,128]{1,0:T(8,128)(2,1)S(1)} %collective-permute-done.9.refs_0_), channel_id=1, source_target_pairs={{0,16},{1,17},{2,18},{3,19},{4,20},{5,21},{6,22},{7,23},{8,24},{9,... | collective-permute-start | bytes 1179656 | tf_op jit(solution)/shard_map/ppermute | solution.py:55
  66.2 18.7 %collective-permute-start.8 = (bf16[1536,128]{1,0:T(8,128)(2,1)S(1)}, bf16[1536,128]{1,0:T(8,128)(2,1)S(1)}, u32[]{:S(2)}, u32[]{:S(2)}) collective-permute-start(bf16[1536,128]{1,0:T(8,128)(2,1)S(1)} %collective-permute-done.6.refs_0_), channel_id=1, source_target_pairs={{0,16},{1,17},{2,18},{3,19},{4,20},{5,21},{6,22},{7,23},{8,24},{9,... | collective-permute-start | bytes 1179656 | tf_op jit(solution)/shard_map/ppermute | solution.py:55
  67.7 17.6 %collective-permute-start.25 = (bf16[1536,128]{1,0:T(8,128)(2,1)S(1)}, bf16[1536,128]{1,0:T(8,128)(2,1)S(1)}, u32[]{:S(2)}, u32[]{:S(2)}) collective-permute-start(bf16[1536,128]{1,0:T(8,128)(2,1)S(1)} %get-tuple-element.88), channel_id=1, source_target_pairs={{0,7},{1,6},{2,1},{3,0},{4,3},{5,2},{6,5},{7,4},{8,15},{9,14},{10,... | collective-permute-start | bytes 1179656 | tf_op jit(solution)/shard_map/ppermute | solution.py:55
  71.4 19.7 %collective-permute-start.21 = (bf16[1536,128]{1,0:T(8,128)(2,1)S(1)}, bf16[1536,128]{1,0:T(8,128)(2,1)S(1)}, u32[]{:S(2)}, u32[]{:S(2)}) collective-permute-start(bf16[1536,128]{1,0:T(8,128)(2,1)S(1)} %get-tuple-element.80), channel_id=1, source_target_pairs={{0,3},{1,2},{2,5},{3,4},{4,7},{5,6},{6,1},{7,0},{8,11},{9,10},{10,... | collective-permute-start | bytes 1179656 | tf_op jit(solution)/shard_map/ppermute | solution.py:55
  75.5 17.8 %collective-permute-start.16 = (bf16[1536,128]{1,0:T(8,128)(2,1)S(1)}, bf16[1536,128]{1,0:T(8,128)(2,1)S(1)}, u32[]{:S(2)}, u32[]{:S(2)}) collective-permute-start(bf16[1536,128]{1,0:T(8,128)(2,1)S(1)} %get-tuple-element.74), channel_id=1, source_target_pairs={{0,16},{1,17},{2,18},{3,19},{4,20},{5,21},{6,22},{7,23},{8,24},{9,... | collective-permute-start | bytes 1179656 | tf_op jit(solution)/shard_map/ppermute | solution.py:55
  76.4 28.6 %collective-permute-start.22 = (bf16[1536,128]{1,0:T(8,128)(2,1)S(1)}, bf16[1536,128]{1,0:T(8,128)(2,1)S(1)}, u32[]{:S(2)}, u32[]{:S(2)}) collective-permute-start(bf16[1536,128]{1,0:T(8,128)(2,1)S(1)} %shard_map.65), channel_id=1, source_target_pairs={{0,4},{1,5},{2,6},{3,7},{4,0},{5,1},{6,2},{7,3},{8,12},{9,13},{10,... | collective-permute-start | bytes 1179656 | tf_op jit(solution)/shard_map/ppermute | solution.py:55
  84.9 21.6 %collective-permute-start.12 = (bf16[1536,128]{1,0:T(8,128)(2,1)S(1)}, bf16[1536,128]{1,0:T(8,128)(2,1)S(1)}, u32[]{:S(2)}, u32[]{:S(2)}) collective-permute-start(bf16[1536,128]{1,0:T(8,128)(2,1)S(1)} %get-tuple-element.68), channel_id=1, source_target_pairs={{0,16},{1,17},{2,18},{3,19},{4,20},{5,21},{6,22},{7,23},{8,24},{9,... | collective-permute-start | bytes 1179656 | tf_op jit(solution)/shard_map/ppermute | solution.py:55
  85.3 37.1 %collective-permute-start.26 = (bf16[1536,128]{1,0:T(8,128)(2,1)S(1)}, bf16[1536,128]{1,0:T(8,128)(2,1)S(1)}, u32[]{:S(2)}, u32[]{:S(2)}) collective-permute-start(bf16[1536,128]{1,0:T(8,128)(2,1)S(1)} %collective-permute-done.25.refs_0_), channel_id=1, source_target_pairs={{0,16},{1,17},{2,18},{3,19},{4,20},{5,21},{6,22},{7,23},{8,24},{9,... | collective-permute-start | bytes 1179656 | tf_op jit(solution)/shard_map/ppermute | solution.py:55
  105.0 13.3 %collective-permute-start.23 = (bf16[1536,128]{1,0:T(8,128)(2,1)S(1)}, bf16[1536,128]{1,0:T(8,128)(2,1)S(1)}, u32[]{:S(2)}, u32[]{:S(2)}) collective-permute-start(bf16[1536,128]{1,0:T(8,128)(2,1)S(1)} %collective-permute-done.21.refs_0_), channel_id=1, source_target_pairs={{0,16},{1,17},{2,18},{3,19},{4,20},{5,21},{6,22},{7,23},{8,24},{9,... | collective-permute-start | bytes 1179656 | tf_op jit(solution)/shard_map/ppermute | solution.py:55
  106.6 20.9 %collective-permute-start.24 = (bf16[1536,128]{1,0:T(8,128)(2,1)S(1)}, bf16[1536,128]{1,0:T(8,128)(2,1)S(1)}, u32[]{:S(2)}, u32[]{:S(2)}) collective-permute-start(bf16[1536,128]{1,0:T(8,128)(2,1)S(1)} %shard_map.67), channel_id=1, source_target_pairs={{0,5},{1,4},{2,7},{3,6},{4,1},{5,0},{6,3},{7,2},{8,13},{9,12},{10,... | collective-permute-start | bytes 1179656 | tf_op jit(solution)/shard_map/ppermute | solution.py:55
  110.8 17.1 %collective-permute-start.13 = (bf16[1536,128]{1,0:T(8,128)(2,1)S(1)}, bf16[1536,128]{1,0:T(8,128)(2,1)S(1)}, u32[]{:S(2)}, u32[]{:S(2)}) collective-permute-start(bf16[1536,128]{1,0:T(8,128)(2,1)S(1)} %get-tuple-element.69), channel_id=1, source_target_pairs={{0,16},{1,17},{2,18},{3,19},{4,20},{5,21},{6,22},{7,23},{8,24},{9,... | collective-permute-start | bytes 1179656 | tf_op jit(solution)/shard_map/ppermute | solution.py:55
  111.4 19.1 %collective-permute-start.17 = (bf16[1536,128]{1,0:T(8,128)(2,1)S(1)}, bf16[1536,128]{1,0:T(8,128)(2,1)S(1)}, u32[]{:S(2)}, u32[]{:S(2)}) collective-permute-start(bf16[1536,128]{1,0:T(8,128)(2,1)S(1)} %shard_map.62), channel_id=1, source_target_pairs={{0,6},{1,7},{2,0},{3,1},{4,2},{5,3},{6,4},{7,5},{8,14},{9,15},{10,... | collective-permute-start | bytes 1179656 | tf_op jit(solution)/shard_map/ppermute | solution.py:55
  127.5 16.7 %collective-permute-start.27 = (bf16[1536,128]{1,0:T(8,128)(2,1)S(1)}, bf16[1536,128]{1,0:T(8,128)(2,1)S(1)}, u32[]{:S(2)}, u32[]{:S(2)}) collective-permute-start(bf16[1536,128]{1,0:T(8,128)(2,1)S(1)} %get-tuple-element.90), channel_id=1, source_target_pairs={{0,16},{1,17},{2,18},{3,19},{4,20},{5,21},{6,22},{7,23},{8,24},{9,... | collective-permute-start | bytes 1179656 | tf_op jit(solution)/shard_map/ppermute | solution.py:55
  130.6 15.4 %collective-permute-start.18 = (bf16[1536,128]{1,0:T(8,128)(2,1)S(1)}, bf16[1536,128]{1,0:T(8,128)(2,1)S(1)}, u32[]{:S(2)}, u32[]{:S(2)}) collective-permute-start(bf16[1536,128]{1,0:T(8,128)(2,1)S(1)} %shard_map.60), channel_id=1, source_target_pairs={{0,2},{1,3},{2,4},{3,5},{4,6},{5,7},{6,0},{7,1},{8,10},{9,11},{10,... | collective-permute-start | bytes 1179656 | tf_op jit(solution)/shard_map/ppermute | solution.py:55
  148.0 15.7 %collective-permute-start.19 = (bf16[1536,128]{1,0:T(8,128)(2,1)S(1)}, bf16[1536,128]{1,0:T(8,128)(2,1)S(1)}, u32[]{:S(2)}, u32[]{:S(2)}) collective-permute-start(bf16[1536,128]{1,0:T(8,128)(2,1)S(1)} %get-tuple-element.76), channel_id=1, source_target_pairs={{0,16},{1,17},{2,18},{3,19},{4,20},{5,21},{6,22},{7,23},{8,24},{9,... | collective-permute-start | bytes 1179656 | tf_op jit(solution)/shard_map/ppermute | solution.py:55
  (11 other events, 120.5 us)

commit v5 on v3

--- a/solution.py
+++ b/solution.py
@@ -9,39 +9,41 @@
 
 clamp_limit = 7.0
 AXES = ("dp", "expert")
-VMEM_LIMIT = 12 * 1024 * 1024
+VMEM_LIMIT = 20 * 1024 * 1024
 F32, BF16 = jnp.float32, jnp.bfloat16
-PARAMS = {'far': [4, 2, 5, 6, 3, 7],
- 'far_in': 3,
- 'far_out': 2,
- 'kcost': 6,
+PARAMS = {'far': [2, 6, 4, 3, 5, 7],
+ 'far_in': 2,
+ 'far_out': 3,
+ 'first': [0, 1, 2],
+ 'kcost': 0,
  'late': 2,
  'near_in': 1,
  'plan': [('out', 0),
           ('out', 1),
-          ('out', 4),
           ('out', 2),
-          ('back', 4),
           ('out', 6),
           ('back', 2),
+          ('out', 4),
+          ('back', 6),
+          ('out', 3),
+          ('back', 4),
           ('out', 5),
+          ('back', 3),
+          ('out', 7),
           ('back', 5),
-          ('out', 3),
-          ('back', 6),
-          ('out', 7),
-          ('back', 3),
           ('back', 7),
           ('back', 1),
           ('back', 0)],
- 'ties': {'dn': (('out', 0), ('z', 1), ('z', 4)),
-          'gu': (('out', 0), ('z', 1), ('z', 4)),
-          ('back', 0): (('r', 3),),
-          ('back', 1): (('r', 6),),
-          ('back', 3): (('r', 5),),
-          ('back', 7): (('r', 2),),
-          ('out', 3): (('r', 4),),
-          ('z', 3): (('r', 7),)},
- 'xdepth': 3}
+ 'ties': {'copy': (('out', 0),),
+          'dn': (('out', 0), ('z', 1), ('z', 2)),
+          'gu': (('out', 0), ('z', 1), ('z', 2)),
+          ('back', 1): (('r', 3),),
+          ('back', 2): (('r', 1),),
+          ('back', 5): (('r', 6),),
+          ('back', 7): (('r', 4),),
+          ('out', 5): (('r', 2),),
+          ('out', 7): (('r', 7),)},
+ 'xdepth': 2}
 
 
 def sent_to(array, target):
@@ -221,14 +223,19 @@
     slot_range = jnp.arange(slots, dtype=jnp.int32)
     chosen = rank.T[:, None, :] == slot_range[None, :, None]
     table = jnp.where(rank.T[:, :, None] == slot_range, weight.T[:, :, None], 0.0).astype(BF16)
-    outgoing = call_kernel(
-        functools.partial(pick_kernel, capacity),
-        [jax.ShapeDtypeStruct(packed, BF16)] * groups,
-        (chosen.astype(BF16), hidden_states.T),
-        2 * groups * slots * tok_rows * width,
-        [packed_scratch],
-    )
-
+    outgoing = [None] * groups
+    first = PARAMS["first"] if known else list(range(groups))
+    for blocks in (first, [k for k in range(groups) if k not in first]):
+        if blocks:
+            picked = call_kernel(
+                functools.partial(pick_kernel, capacity),
+                [jax.ShapeDtypeStruct(packed, BF16)] * len(blocks),
+                (jnp.stack([chosen[k] for k in blocks]).astype(BF16), hidden_states.T),
+                2 * len(blocks) * slots * tok_rows * width,
+                [packed_scratch],
+            )
+            for k, block in zip(blocks, picked):
+                outgoing[k] = block
     between_chips, far_in = Line(PARAMS["xdepth"] * (chips - 1)), Line(PARAMS["far_in"])
     near_in, far_out, near_out = Line(PARAMS["near_in"]), Line(PARAMS["far_out"]), Line(1)
     done, rows = {}, [outgoing[0]] + [None] * (groups - 1)

time: 187 us -> 168 us (0.90)
  starting transfers between devices: 75 us -> 42.6 us
  waiting for transfers between devices: 66.5 us -> 80.5 us
    ppermute x32, starting transfers between devices: 75 us -> 42.6 us  [sent_to(): return lax.ppermute(array, AXES, pairs)]
    ppermute x32, waiting for transfers between devices: 66.5 us -> 80.5 us  [sent_to(): return lax.ppermute(array, AXES, pairs)]
    pallas_call x19 -> x20, Pallas kernels: 39.1 us -> 39 us  [call_kernel(): pl.pallas_call(body, out_shape=out_shapes, in_specs=[pl.BlockSpec(memory_...]
    unnamed x11 -> x14, local copies, waits for them, and re-layouts: 3.8 us -> 3.81 us
  transfers between devices with their start and end apart: 32 -> 32, of which waited for: 13 -> 18; matrix products, arithmetic and copies ran while one was open for 2% -> 2% of each run, Pallas kernels for 19% -> 22%
where the time goes in v5:
time: 168 us; the launch traced here: 167 us
  waiting for transfers between devices  80.5 us (48%)
  starting transfers between devices  42.6 us (25%)
  Pallas kernels  39 us (23%)
  local copies, waits for them, and re-layouts  3.82 us (2%)
    ppermute x32, waiting for transfers between devices, sent_to(): return lax.ppermute(array, AXES, pairs)  80.5 us
    ppermute x32, starting transfers between devices, sent_to(): return lax.ppermute(array, AXES, pairs)  42.6 us
    pallas_call x20, Pallas kernels, call_kernel(): pl.pallas_call(body, out_shape=out_shapes, in_specs=[pl.BlockSpec(memory_...  39 us
    unnamed x14, local copies, waits for them, and re-layouts  3.81 us
  transfers between devices with their start and end apart: 32, of which 18 were waited for; matrix products, arithmetic and copies ran while one was open for 2% of the time, Pallas kernels for 22%

profile of v5, /device:TPU:0, one launch (start us, length us, event | category | flops | bytes accessed | tf_op | source)
XLA Modules:
  0.0 167.4 jit_solution(4774301001345574539)
XLA Ops:
  3.2 3.0 %collective-permute-start.2 = (bf16[1536,128]{1,0:T(8,128)(2,1)S(1)}, bf16[1536,128]{1,0:T(8,128)(2,1)S(1)}, u32[]{:S(2)}, u32[]{:S(2)}) collective-permute-start(bf16[1536,128]{1,0:T(8,128)(2,1)S(1)} %get-tuple-element.54.refs_0_), channel_id=1, source_target_pairs={{0,16},{1,17},{2,18},{3,19},{4,20},{5,21},{6,22},{7,23},{8,24},{9,... | collective-permute-start | bytes 1179656 | tf_op jit(solution)/shard_map/ppermute | solution.py:56
  11.9 3.4 %collective-permute-done.2.refs_1_ = bf16[1536,128]{1,0:T(8,128)(2,1)S(1)} collective-permute-done((bf16[1536,128]{1,0:T(8,128)(2,1)S(1)}, bf16[1536,128]{1,0:T(8,128)(2,1)S(1)}, u32[]{:S(2)}, u32[]{:S(2)}) %collective-permute-start.2) | collective-permute-done | bytes 393248 | tf_op jit(solution)/shard_map/ppermute | solution.py:56
  15.3 3.3 %collective-permute-done.3.refs_0_ = bf16[1536,128]{1,0:T(8,128)(2,1)S(1)} collective-permute-done((bf16[1536,128]{1,0:T(8,128)(2,1)S(1)}, bf16[1536,128]{1,0:T(8,128)(2,1)S(1)}, u32[]{:S(2)}, u32[]{:S(2)}) %collective-permute-start.3) | collective-permute-done | bytes 393248 | tf_op jit(solution)/shard_map/ppermute | solution.py:56
  24.6 7.3 %collective-permute-done.6.refs_0_ = bf16[1536,128]{1,0:T(8,128)(2,1)S(1)} collective-permute-done((bf16[1536,128]{1,0:T(8,128)(2,1)S(1)}, bf16[1536,128]{1,0:T(8,128)(2,1)S(1)}, u32[]{:S(2)}, u32[]{:S(2)}) %collective-permute-start.6) | collective-permute-done | bytes 393248 | tf_op jit(solution)/shard_map/ppermute | solution.py:56
  35.1 7.9 %collective-permute-done.12.refs_1_ = bf16[1536,128]{1,0:T(8,128)(2,1)S(1)} collective-permute-done((bf16[1536,128]{1,0:T(8,128)(2,1)S(1)}, bf16[1536,128]{1,0:T(8,128)(2,1)S(1)}, u32[]{:S(2)}, u32[]{:S(2)}) %collective-permute-start.12) | collective-permute-done | bytes 393248 | tf_op jit(solution)/shard_map/ppermute | solution.py:56
  43.0 4.1 %shard_map.61 = (f32[1536,128]{1,0:T(8,128)S(1)}, bf16[1536,128]{1,0:T(8,128)(2,1)S(1)}) custom-call(bf16[1536,128]{1,0:T(8,128)(2,1)S(1)} %collective-permute-done.3.refs_0_, bf16[1536,128]{1,0:T(8,128)(2,1)S(1)} %collective-permute-done.12.refs_1_, bf16[2,360,2880]{2,1,0:T(8,128)(2,1)S(1)} %bitcast.12, ...), custom_call_target="tpu_custom_call" | custom-call | bytes 14407680 | tf_op jit(solution)/shard_map/pallas_call | solution.py:99
  48.9 11.0 %collective-permute-done.8.refs_0_ = bf16[1536,128]{1,0:T(8,128)(2,1)S(1)} collective-permute-done((bf16[1536,128]{1,0:T(8,128)(2,1)S(1)}, bf16[1536,128]{1,0:T(8,128)(2,1)S(1)}, u32[]{:S(2)}, u32[]{:S(2)}) %collective-permute-start.8) | collective-permute-done | bytes 393248 | tf_op jit(solution)/shard_map/ppermute | solution.py:56
  59.9 4.1 %shard_map.60 = (f32[1536,128]{1,0:T(8,128)S(1)}, bf16[1536,128]{1,0:T(8,128)(2,1)S(1)}) custom-call(bf16[1536,128]{1,0:T(8,128)(2,1)S(1)} %collective-permute-done.6.refs_0_, bf16[1536,128]{1,0:T(8,128)(2,1)S(1)} %collective-permute-done.9.refs_1_, bf16[2,360,2880]{2,1,0:T(8,128)(2,1)S(1)} %bitcast.13, ...), custom_call_target="tpu_custom_call" | custom-call | bytes 14407680 | tf_op jit(solution)/shard_map/pallas_call | solution.py:99
  66.6 5.4 %collective-permute-done.10.refs_1_ = bf16[1536,128]{1,0:T(8,128)(2,1)S(1)} collective-permute-done((bf16[1536,128]{1,0:T(8,128)(2,1)S(1)}, bf16[1536,128]{1,0:T(8,128)(2,1)S(1)}, u32[]{:S(2)}, u32[]{:S(2)}) %collective-permute-start.10) | collective-permute-done | bytes 393248 | tf_op jit(solution)/shard_map/ppermute | solution.py:56
  72.3 4.1 %shard_map.59 = (f32[1536,128]{1,0:T(8,128)S(1)}, bf16[1536,128]{1,0:T(8,128)(2,1)S(1)}) custom-call(bf16[1536,128]{1,0:T(8,128)(2,1)S(1)} %collective-permute-done.8.refs_0_, bf16[1536,128]{1,0:T(8,128)(2,1)S(1)} %collective-permute-done.10.refs_1_, bf16[2,360,2880]{2,1,0:T(8,128)(2,1)S(1)} %bitcast.14, ...), custom_call_target="tpu_custom_call" | custom-call | bytes 14407680 | tf_op jit(solution)/shard_map/pallas_call | solution.py:99
  76.4 4.0 %collective-permute-done.14.refs_1_ = bf16[1536,128]{1,0:T(8,128)(2,1)S(1)} collective-permute-done((bf16[1536,128]{1,0:T(8,128)(2,1)S(1)}, bf16[1536,128]{1,0:T(8,128)(2,1)S(1)}, u32[]{:S(2)}, u32[]{:S(2)}) %collective-permute-start.14) | collective-permute-done | bytes 393248 | tf_op jit(solution)/shard_map/ppermute | solution.py:56
  80.4 8.4 %collective-permute-done.11.refs_1_ = bf16[1536,128]{1,0:T(8,128)(2,1)S(1)} collective-permute-done((bf16[1536,128]{1,0:T(8,128)(2,1)S(1)}, bf16[1536,128]{1,0:T(8,128)(2,1)S(1)}, u32[]{:S(2)}, u32[]{:S(2)}) %collective-permute-start.11) | collective-permute-done | bytes 393248 | tf_op jit(solution)/shard_map/ppermute | solution.py:56
  88.8 4.1 %shard_map.58 = (f32[1536,128]{1,0:T(8,128)S(1)}, bf16[1536,128]{1,0:T(8,128)(2,1)S(1)}) custom-call(bf16[1536,128]{1,0:T(8,128)(2,1)S(1)} %collective-permute-done.7.refs_0_, bf16[1536,128]{1,0:T(8,128)(2,1)S(1)} %collective-permute-done.11.refs_1_, bf16[2,360,2880]{2,1,0:T(8,128)(2,1)S(1)} %bitcast.15, ...), custom_call_target="tpu_custom_call" | custom-call | bytes 14407680 | tf_op jit(solution)/shard_map/pallas_call | solution.py:99
  93.1 11.3 %collective-permute-start.21 = (bf16[1536,128]{1,0:T(8,128)(2,1)S(1)}, bf16[1536,128]{1,0:T(8,128)(2,1)S(1)}, u32[]{:S(2)}, u32[]{:S(2)}) collective-permute-start(bf16[1536,128]{1,0:T(8,128)(2,1)S(1)} %shard_map.65), channel_id=1, source_target_pairs={{0,2},{1,3},{2,4},{3,5},{4,6},{5,7},{6,0},{7,1},{8,10},{9,11},{10,... | collective-permute-start | bytes 1179656 | tf_op jit(solution)/shard_map/ppermute | solution.py:56
  107.0 4.1 %shard_map.64 = (f32[1536,128]{1,0:T(8,128)S(1)}, bf16[1536,128]{1,0:T(8,128)(2,1)S(1)}) custom-call(bf16[1536,128]{1,0:T(8,128)(2,1)S(1)} %collective-permute-done.19.refs_0_, bf16[1536,128]{1,0:T(8,128)(2,1)S(1)} %collective-permute-done.20.refs_1_, bf16[2,360,2880]{2,1,0:T(8,128)(2,1)S(1)} %bitcast.16, ...), custom_call_target="tpu_custom_call" | custom-call | bytes 14407680 | tf_op jit(solution)/shard_map/pallas_call | solution.py:99
  111.3 5.1 %collective-permute-done.16.refs_1_ = bf16[1536,128]{1,0:T(8,128)(2,1)S(1)} collective-permute-done((bf16[1536,128]{1,0:T(8,128)(2,1)S(1)}, bf16[1536,128]{1,0:T(8,128)(2,1)S(1)}, u32[]{:S(2)}, u32[]{:S(2)}) %collective-permute-start.16) | collective-permute-done | bytes 393248 | tf_op jit(solution)/shard_map/ppermute | solution.py:56
  117.1 8.0 %collective-permute-start.18 = (bf16[1536,128]{1,0:T(8,128)(2,1)S(1)}, bf16[1536,128]{1,0:T(8,128)(2,1)S(1)}, u32[]{:S(2)}, u32[]{:S(2)}) collective-permute-start(bf16[1536,128]{1,0:T(8,128)(2,1)S(1)} %shard_map.62), channel_id=1, source_target_pairs={{0,7},{1,6},{2,1},{3,0},{4,3},{5,2},{6,5},{7,4},{8,15},{9,14},{10,... | collective-permute-start | bytes 1179656 | tf_op jit(solution)/shard_map/ppermute | solution.py:56
  125.1 4.1 %shard_map.56 = (f32[1536,128]{1,0:T(8,128)S(1)}, bf16[1536,128]{1,0:T(8,128)(2,1)S(1)}) custom-call(bf16[1536,128]{1,0:T(8,128)(2,1)S(1)} %collective-permute-done.refs_0_, bf16[1536,128]{1,0:T(8,128)(2,1)S(1)} %collective-permute-done.1.refs_1_, bf16[2,360,2880]{2,1,0:T(8,128)(2,1)S(1)} %bitcast.17, ...), custom_call_target="tpu_custom_call" | custom-call | bytes 14407680 | tf_op jit(solution)/shard_map/pallas_call | solution.py:99
  129.1 4.1 %shard_map.68 = (f32[1536,128]{1,0:T(8,128)S(1)}, bf16[1536,128]{1,0:T(8,128)(2,1)S(1)}) custom-call(bf16[1536,128]{1,0:T(8,128)(2,1)S(1)} %collective-permute-done.25.refs_0_, bf16[1536,128]{1,0:T(8,128)(2,1)S(1)} %collective-permute-done.26.refs_1_, bf16[2,360,2880]{2,1,0:T(8,128)(2,1)S(1)} %bitcast.18, ...), custom_call_target="tpu_custom_call" | custom-call | bytes 14407680 | tf_op jit(solution)/shard_map/pallas_call | solution.py:99
  135.3 4.1 %shard_map.67 = (f32[1536,128]{1,0:T(8,128)S(1)}, bf16[1536,128]{1,0:T(8,128)(2,1)S(1)}) custom-call(bf16[1536,128]{1,0:T(8,128)(2,1)S(1)} %get-tuple-element.54.refs_0_, bf16[1536,128]{1,0:T(8,128)(2,1)S(1)} %collective-permute-done.2.refs_1_, bf16[2,360,2880]{2,1,0:T(8,128)(2,1)S(1)} %bitcast.19, bf16[2,360,2880]{2,1,0:T(8,128)(2,1)S(1)} %collective-permute-done.4.refs_3_, ...), custom_call_target="tpu_custom_call" | custom-call | bytes 14407680 | tf_op jit(solution)/shard_map/pallas_call | solution.py:99
  139.4 5.3 %collective-permute-done.28.refs_1_ = bf16[1536,128]{1,0:T(8,128)(2,1)S(1)} collective-permute-done((bf16[1536,128]{1,0:T(8,128)(2,1)S(1)}, bf16[1536,128]{1,0:T(8,128)(2,1)S(1)}, u32[]{:S(2)}, u32[]{:S(2)}) %collective-permute-start.28) | collective-permute-done | bytes 393248 | tf_op jit(solution)/shard_map/ppermute | solution.py:56
  145.1 4.4 %collective-permute-done.23.refs_1_ = bf16[1536,128]{1,0:T(8,128)(2,1)S(1)} collective-permute-done((bf16[1536,128]{1,0:T(8,128)(2,1)S(1)}, bf16[1536,128]{1,0:T(8,128)(2,1)S(1)}, u32[]{:S(2)}, u32[]{:S(2)}) %collective-permute-start.23) | collective-permute-done | bytes 393248 | tf_op jit(solution)/shard_map/ppermute | solution.py:56
  150.5 3.1 %collective-permute-done.29.refs_1_ = bf16[1536,128]{1,0:T(8,128)(2,1)S(1)} collective-permute-done((bf16[1536,128]{1,0:T(8,128)(2,1)S(1)}, bf16[1536,128]{1,0:T(8,128)(2,1)S(1)}, u32[]{:S(2)}, u32[]{:S(2)}) %collective-permute-start.29) | collective-permute-done | bytes 393248 | tf_op jit(solution)/shard_map/ppermute | solution.py:56
  155.5 7.6 %collective-permute-done.30.refs_4_ = bf16[1536,128]{1,0:T(8,128)(2,1)S(1)} collective-permute-done((bf16[1536,128]{1,0:T(8,128)(2,1)S(1)}, bf16[1536,128]{1,0:T(8,128)(2,1)S(1)}, u32[]{:S(2)}, u32[]{:S(2)}) %collective-permute-start.30) | collective-permute-done | bytes 393248 | tf_op jit(solution)/shard_map/ppermute | solution.py:56
  (86 shorter events, 36.0 us)
Async XLA Ops:
  3.2 12.1 %collective-permute-start.2 = (bf16[1536,128]{1,0:T(8,128)(2,1)S(1)}, bf16[1536,128]{1,0:T(8,128)(2,1)S(1)}, u32[]{:S(2)}, u32[]{:S(2)}) collective-permute-start(bf16[1536,128]{1,0:T(8,128)(2,1)S(1)} %get-tuple-element.54.refs_0_), channel_id=1, source_target_pairs={{0,16},{1,17},{2,18},{3,19},{4,20},{5,21},{6,22},{7,23},{8,24},{9,... | collective-permute-start | bytes 1179656 | tf_op jit(solution)/shard_map/ppermute | solution.py:56
  6.2 12.4 %collective-permute-start.3 = (bf16[1536,128]{1,0:T(8,128)(2,1)S(1)}, bf16[1536,128]{1,0:T(8,128)(2,1)S(1)}, u32[]{:S(2)}, u32[]{:S(2)}) collective-permute-start(bf16[1536,128]{1,0:T(8,128)(2,1)S(1)} %get-tuple-element.56), channel_id=1, source_target_pairs={{0,2},{1,3},{2,4},{3,5},{4,6},{5,7},{6,0},{7,1},{8,10},{9,11},{10,... | collective-permute-start | bytes 1179656 | tf_op jit(solution)/shard_map/ppermute | solution.py:56
  18.6 24.4 %collective-permute-start.4 = (bf16[2,360,2880]{2,1,0:T(8,128)(2,1)S(1)}, bf16[2,360,2880]{2,1,0:T(8,128)(2,1)S(1)}, u32[]{:S(2)}, u32[]{:S(2)}) collective-permute-start(bf16[2,360,2880]{2,1,0:T(8,128)(2,1)S(1)} %bitcast.11), channel_id=1, source_target_pairs={{0,8},{1,9},{2,10},{3,11},{4,12},{5,13},{6,14},{7,15},{8,0},{9,1},... | collective-permute-start | bytes 12441608 | tf_op jit(solution)/shard_map/ppermute | solution.py:56
  18.6 24.4 %collective-permute-start.5 = (bf16[360,2880]{1,0:T(8,128)(2,1)S(1)}, bf16[360,2880]{1,0:T(8,128)(2,1)S(1)}, u32[]{:S(2)}, u32[]{:S(2)}) collective-permute-start(bf16[360,2880]{1,0:T(8,128)(2,1)S(1)} %bitcast.20), channel_id=1, source_target_pairs={{0,8},{1,9},{2,10},{3,11},{4,12},{5,13},{6,14},{7,15},{8,0},{9,1},... | collective-permute-start | bytes 6220808 | tf_op jit(solution)/shard_map/ppermute | solution.py:56
  23.1 19.9 %collective-permute-start.12 = (bf16[1536,128]{1,0:T(8,128)(2,1)S(1)}, bf16[1536,128]{1,0:T(8,128)(2,1)S(1)}, u32[]{:S(2)}, u32[]{:S(2)}) collective-permute-start(bf16[1536,128]{1,0:T(8,128)(2,1)S(1)} %collective-permute-done.3.refs_0_), channel_id=1, source_target_pairs={{0,16},{1,17},{2,18},{3,19},{4,20},{5,21},{6,22},{7,23},{8,24},{9,... | collective-permute-start | bytes 1179656 | tf_op jit(solution)/shard_map/ppermute | solution.py:56
  31.9 28.0 %collective-permute-start.8 = (bf16[1536,128]{1,0:T(8,128)(2,1)S(1)}, bf16[1536,128]{1,0:T(8,128)(2,1)S(1)}, u32[]{:S(2)}, u32[]{:S(2)}) collective-permute-start(bf16[1536,128]{1,0:T(8,128)(2,1)S(1)} %get-tuple-element.65), channel_id=1, source_target_pairs={{0,4},{1,5},{2,6},{3,7},{4,0},{5,1},{6,2},{7,3},{8,12},{9,13},{10,... | collective-permute-start | bytes 1179656 | tf_op jit(solution)/shard_map/ppermute | solution.py:56
  34.6 25.3 %collective-permute-start.9 = (bf16[1536,128]{1,0:T(8,128)(2,1)S(1)}, bf16[1536,128]{1,0:T(8,128)(2,1)S(1)}, u32[]{:S(2)}, u32[]{:S(2)}) collective-permute-start(bf16[1536,128]{1,0:T(8,128)(2,1)S(1)} %collective-permute-done.6.refs_0_), channel_id=1, source_target_pairs={{0,16},{1,17},{2,18},{3,19},{4,20},{5,21},{6,22},{7,23},{8,24},{9,... | collective-permute-start | bytes 1179656 | tf_op jit(solution)/shard_map/ppermute | solution.py:56
  47.1 16.9 %collective-permute-start.13 = (bf16[1536,128]{1,0:T(8,128)(2,1)S(1)}, bf16[1536,128]{1,0:T(8,128)(2,1)S(1)}, u32[]{:S(2)}, u32[]{:S(2)}) collective-permute-start(bf16[1536,128]{1,0:T(8,128)(2,1)S(1)} %get-tuple-element.75), channel_id=1, source_target_pairs={{0,16},{1,17},{2,18},{3,19},{4,20},{5,21},{6,22},{7,23},{8,24},{9,... | collective-permute-start | bytes 1179656 | tf_op jit(solution)/shard_map/ppermute | solution.py:56
  47.7 18.9 %collective-permute-start.7 = (bf16[1536,128]{1,0:T(8,128)(2,1)S(1)}, bf16[1536,128]{1,0:T(8,128)(2,1)S(1)}, u32[]{:S(2)}, u32[]{:S(2)}) collective-permute-start(bf16[1536,128]{1,0:T(8,128)(2,1)S(1)} %get-tuple-element.63), channel_id=1, source_target_pairs={{0,3},{1,2},{2,5},{3,4},{4,7},{5,6},{6,1},{7,0},{8,11},{9,10},{10,... | collective-permute-start | bytes 1179656 | tf_op jit(solution)/shard_map/ppermute | solution.py:56
  64.0 16.4 %collective-permute-start.14 = (bf16[1536,128]{1,0:T(8,128)(2,1)S(1)}, bf16[1536,128]{1,0:T(8,128)(2,1)S(1)}, u32[]{:S(2)}, u32[]{:S(2)}) collective-permute-start(bf16[1536,128]{1,0:T(8,128)(2,1)S(1)} %get-tuple-element.76), channel_id=1, source_target_pairs={{0,16},{1,17},{2,18},{3,19},{4,20},{5,21},{6,22},{7,23},{8,24},{9,... | collective-permute-start | bytes 1179656 | tf_op jit(solution)/shard_map/ppermute | solution.py:56
  66.1 26.8 %collective-permute-start.19 = (bf16[1536,128]{1,0:T(8,128)(2,1)S(1)}, bf16[1536,128]{1,0:T(8,128)(2,1)S(1)}, u32[]{:S(2)}, u32[]{:S(2)}) collective-permute-start(bf16[1536,128]{1,0:T(8,128)(2,1)S(1)} %get-tuple-element.82), channel_id=1, source_target_pairs={{0,5},{1,4},{2,7},{3,6},{4,1},{5,0},{6,3},{7,2},{8,13},{9,12},{10,... | collective-permute-start | bytes 1179656 | tf_op jit(solution)/shard_map/ppermute | solution.py:56
  72.0 16.9 %collective-permute-start.11 = (bf16[1536,128]{1,0:T(8,128)(2,1)S(1)}, bf16[1536,128]{1,0:T(8,128)(2,1)S(1)}, u32[]{:S(2)}, u32[]{:S(2)}) collective-permute-start(bf16[1536,128]{1,0:T(8,128)(2,1)S(1)} %collective-permute-done.7.refs_0_), channel_id=1, source_target_pairs={{0,16},{1,17},{2,18},{3,19},{4,20},{5,21},{6,22},{7,23},{8,24},{9,... | collective-permute-start | bytes 1179656 | tf_op jit(solution)/shard_map/ppermute | solution.py:56
  72.1 20.9 %collective-permute-start.17 = (bf16[1536,128]{1,0:T(8,128)(2,1)S(1)}, bf16[1536,128]{1,0:T(8,128)(2,1)S(1)}, u32[]{:S(2)}, u32[]{:S(2)}) collective-permute-start(bf16[1536,128]{1,0:T(8,128)(2,1)S(1)} %shard_map.63), channel_id=1, source_target_pairs={{0,6},{1,7},{2,0},{3,1},{4,2},{5,3},{6,4},{7,5},{8,14},{9,15},{10,... | collective-permute-start | bytes 1179656 | tf_op jit(solution)/shard_map/ppermute | solution.py:56
  80.4 23.9 %collective-permute-start.15 = (bf16[1536,128]{1,0:T(8,128)(2,1)S(1)}, bf16[1536,128]{1,0:T(8,128)(2,1)S(1)}, u32[]{:S(2)}, u32[]{:S(2)}) collective-permute-start(bf16[1536,128]{1,0:T(8,128)(2,1)S(1)} %get-tuple-element.77), channel_id=1, source_target_pairs={{0,16},{1,17},{2,18},{3,19},{4,20},{5,21},{6,22},{7,23},{8,24},{9,... | collective-permute-start | bytes 1179656 | tf_op jit(solution)/shard_map/ppermute | solution.py:56
  80.4 25.0 %collective-permute-start.25 = (bf16[1536,128]{1,0:T(8,128)(2,1)S(1)}, bf16[1536,128]{1,0:T(8,128)(2,1)S(1)}, u32[]{:S(2)}, u32[]{:S(2)}) collective-permute-start(bf16[1536,128]{1,0:T(8,128)(2,1)S(1)} %get-tuple-element.91), channel_id=1, source_target_pairs={{0,7},{1,6},{2,1},{3,0},{4,3},{5,2},{6,5},{7,4},{8,15},{9,14},{10,... | collective-permute-start | bytes 1179656 | tf_op jit(solution)/shard_map/ppermute | solution.py:56
  92.9 12.8 %collective-permute-start.20 = (bf16[1536,128]{1,0:T(8,128)(2,1)S(1)}, bf16[1536,128]{1,0:T(8,128)(2,1)S(1)}, u32[]{:S(2)}, u32[]{:S(2)}) collective-permute-start(bf16[1536,128]{1,0:T(8,128)(2,1)S(1)} %collective-permute-done.19.refs_0_), channel_id=1, source_target_pairs={{0,16},{1,17},{2,18},{3,19},{4,20},{5,21},{6,22},{7,23},{8,24},{9,... | collective-permute-start | bytes 1179656 | tf_op jit(solution)/shard_map/ppermute | solution.py:56
  93.1 18.2 %collective-permute-start.21 = (bf16[1536,128]{1,0:T(8,128)(2,1)S(1)}, bf16[1536,128]{1,0:T(8,128)(2,1)S(1)}, u32[]{:S(2)}, u32[]{:S(2)}) collective-permute-start(bf16[1536,128]{1,0:T(8,128)(2,1)S(1)} %shard_map.65), channel_id=1, source_target_pairs={{0,2},{1,3},{2,4},{3,5},{4,6},{5,7},{6,0},{7,1},{8,10},{9,11},{10,... | collective-permute-start | bytes 1179656 | tf_op jit(solution)/shard_map/ppermute | solution.py:56
  105.4 27.9 %collective-permute-start.27 = (bf16[1536,128]{1,0:T(8,128)(2,1)S(1)}, bf16[1536,128]{1,0:T(8,128)(2,1)S(1)}, u32[]{:S(2)}, u32[]{:S(2)}) collective-permute-start(bf16[1536,128]{1,0:T(8,128)(2,1)S(1)} %shard_map.69), channel_id=1, source_target_pairs={{0,4},{1,5},{2,6},{3,7},{4,0},{5,1},{6,2},{7,3},{8,12},{9,13},{10,... | collective-permute-start | bytes 1179656 | tf_op jit(solution)/shard_map/ppermute | solution.py:56
  105.7 23.5 %collective-permute-start.26 = (bf16[1536,128]{1,0:T(8,128)(2,1)S(1)}, bf16[1536,128]{1,0:T(8,128)(2,1)S(1)}, u32[]{:S(2)}, u32[]{:S(2)}) collective-permute-start(bf16[1536,128]{1,0:T(8,128)(2,1)S(1)} %collective-permute-done.25.refs_0_), channel_id=1, source_target_pairs={{0,16},{1,17},{2,18},{3,19},{4,20},{5,21},{6,22},{7,23},{8,24},{9,... | collective-permute-start | bytes 1179656 | tf_op jit(solution)/shard_map/ppermute | solution.py:56
  116.4 17.4 %collective-permute-start.22 = (bf16[1536,128]{1,0:T(8,128)(2,1)S(1)}, bf16[1536,128]{1,0:T(8,128)(2,1)S(1)}, u32[]{:S(2)}, u32[]{:S(2)}) collective-permute-start(bf16[1536,128]{1,0:T(8,128)(2,1)S(1)} %get-tuple-element.86), channel_id=1, source_target_pairs={{0,16},{1,17},{2,18},{3,19},{4,20},{5,21},{6,22},{7,23},{8,24},{9,... | collective-permute-start | bytes 1179656 | tf_op jit(solution)/shard_map/ppermute | solution.py:56
  117.1 16.8 %collective-permute-start.18 = (bf16[1536,128]{1,0:T(8,128)(2,1)S(1)}, bf16[1536,128]{1,0:T(8,128)(2,1)S(1)}, u32[]{:S(2)}, u32[]{:S(2)}) collective-permute-start(bf16[1536,128]{1,0:T(8,128)(2,1)S(1)} %shard_map.62), channel_id=1, source_target_pairs={{0,7},{1,6},{2,1},{3,0},{4,3},{5,2},{6,5},{7,4},{8,15},{9,14},{10,... | collective-permute-start | bytes 1179656 | tf_op jit(solution)/shard_map/ppermute | solution.py:56
  133.8 15.7 %collective-permute-start.23 = (bf16[1536,128]{1,0:T(8,128)(2,1)S(1)}, bf16[1536,128]{1,0:T(8,128)(2,1)S(1)}, u32[]{:S(2)}, u32[]{:S(2)}) collective-permute-start(bf16[1536,128]{1,0:T(8,128)(2,1)S(1)} %get-tuple-element.87), channel_id=1, source_target_pairs={{0,16},{1,17},{2,18},{3,19},{4,20},{5,21},{6,22},{7,23},{8,24},{9,... | collective-permute-start | bytes 1179656 | tf_op jit(solution)/shard_map/ppermute | solution.py:56
  144.9 18.2 %collective-permute-start.30 = (bf16[1536,128]{1,0:T(8,128)(2,1)S(1)}, bf16[1536,128]{1,0:T(8,128)(2,1)S(1)}, u32[]{:S(2)}, u32[]{:S(2)}) collective-permute-start(bf16[1536,128]{1,0:T(8,128)(2,1)S(1)} %shard_map.71), channel_id=1, source_target_pairs={{0,5},{1,4},{2,7},{3,6},{4,1},{5,0},{6,3},{7,2},{8,13},{9,12},{10,... | collective-permute-start | bytes 1179656 | tf_op jit(solution)/shard_map/ppermute | solution.py:56
  149.5 16.4 %collective-permute-start.24 = (bf16[1536,128]{1,0:T(8,128)(2,1)S(1)}, bf16[1536,128]{1,0:T(8,128)(2,1)S(1)}, u32[]{:S(2)}, u32[]{:S(2)}) collective-permute-start(bf16[1536,128]{1,0:T(8,128)(2,1)S(1)} %shard_map.66), channel_id=1, source_target_pairs={{0,1},{1,0},{2,3},{3,2},{4,5},{5,4},{6,7},{7,6},{8,9},{9,8},{10,11... | collective-permute-start | bytes 1179656 | tf_op jit(solution)/shard_map/ppermute | solution.py:56
  (12 other events, 136.8 us)

commit v6 on v5

--- a/solution.py
+++ b/solution.py
@@ -39,8 +39,10 @@
           'gu': (('out', 0), ('z', 1), ('z', 2)),
           ('back', 1): (('r', 3),),
           ('back', 2): (('r', 1),),
-          ('back', 5): (('r', 6),),
+          ('back', 4): (('z', 6),),
+          ('back', 5): (('r', 6), ('z', 7)),
           ('back', 7): (('r', 4),),
+          ('out', 1): (('r', 7),),
           ('out', 5): (('r', 2),),
           ('out', 7): (('r', 7),)},
  'xdepth': 2}

time: 168 us -> 168 us (level)
  no operation moved by 1% of the time
where the time goes in v6:
time: 168 us; the launch traced here: 167 us
  waiting for transfers between devices  80.5 us (48%)
  starting transfers between devices  42.6 us (25%)
  Pallas kernels  39 us (23%)
  local copies, waits for them, and re-layouts  3.82 us (2%)
    ppermute x32, waiting for transfers between devices, sent_to(): return lax.ppermute(array, AXES, pairs)  80.5 us
    ppermute x32, starting transfers between devices, sent_to(): return lax.ppermute(array, AXES, pairs)  42.6 us
    pallas_call x20, Pallas kernels, call_kernel(): pl.pallas_call(body, out_shape=out_shapes, in_specs=[pl.BlockSpec(memory_...  39 us
    unnamed x14, local copies, waits for them, and re-layouts  3.81 us
  transfers between devices with their start and end apart: 32, of which 18 were waited for; matrix products, arithmetic and copies ran while one was open for 2% of the time, Pallas kernels for 22%

profile of v6, /device:TPU:0, one launch (start us, length us, event | category | flops | bytes accessed | tf_op | source)
XLA Modules:
  0.0 167.4 jit_solution(4774301001345574539)
XLA Ops:
  3.2 3.0 %collective-permute-start.2 = (bf16[1536,128]{1,0:T(8,128)(2,1)S(1)}, bf16[1536,128]{1,0:T(8,128)(2,1)S(1)}, u32[]{:S(2)}, u32[]{:S(2)}) collective-permute-start(bf16[1536,128]{1,0:T(8,128)(2,1)S(1)} %get-tuple-element.54.refs_0_), channel_id=1, source_target_pairs={{0,16},{1,17},{2,18},{3,19},{4,20},{5,21},{6,22},{7,23},{8,24},{9,... | collective-permute-start | bytes 1179656 | tf_op jit(solution)/shard_map/ppermute | solution.py:58
  11.9 3.4 %collective-permute-done.2.refs_1_ = bf16[1536,128]{1,0:T(8,128)(2,1)S(1)} collective-permute-done((bf16[1536,128]{1,0:T(8,128)(2,1)S(1)}, bf16[1536,128]{1,0:T(8,128)(2,1)S(1)}, u32[]{:S(2)}, u32[]{:S(2)}) %collective-permute-start.2) | collective-permute-done | bytes 393248 | tf_op jit(solution)/shard_map/ppermute | solution.py:58
  15.3 3.3 %collective-permute-done.3.refs_0_ = bf16[1536,128]{1,0:T(8,128)(2,1)S(1)} collective-permute-done((bf16[1536,128]{1,0:T(8,128)(2,1)S(1)}, bf16[1536,128]{1,0:T(8,128)(2,1)S(1)}, u32[]{:S(2)}, u32[]{:S(2)}) %collective-permute-start.3) | collective-permute-done | bytes 393248 | tf_op jit(solution)/shard_map/ppermute | solution.py:58
  24.6 7.3 %collective-permute-done.6.refs_0_ = bf16[1536,128]{1,0:T(8,128)(2,1)S(1)} collective-permute-done((bf16[1536,128]{1,0:T(8,128)(2,1)S(1)}, bf16[1536,128]{1,0:T(8,128)(2,1)S(1)}, u32[]{:S(2)}, u32[]{:S(2)}) %collective-permute-start.6) | collective-permute-done | bytes 393248 | tf_op jit(solution)/shard_map/ppermute | solution.py:58
  35.1 7.9 %collective-permute-done.12.refs_1_ = bf16[1536,128]{1,0:T(8,128)(2,1)S(1)} collective-permute-done((bf16[1536,128]{1,0:T(8,128)(2,1)S(1)}, bf16[1536,128]{1,0:T(8,128)(2,1)S(1)}, u32[]{:S(2)}, u32[]{:S(2)}) %collective-permute-start.12) | collective-permute-done | bytes 393248 | tf_op jit(solution)/shard_map/ppermute | solution.py:58
  43.0 4.1 %shard_map.61 = (f32[1536,128]{1,0:T(8,128)S(1)}, bf16[1536,128]{1,0:T(8,128)(2,1)S(1)}) custom-call(bf16[1536,128]{1,0:T(8,128)(2,1)S(1)} %collective-permute-done.3.refs_0_, bf16[1536,128]{1,0:T(8,128)(2,1)S(1)} %collective-permute-done.12.refs_1_, bf16[2,360,2880]{2,1,0:T(8,128)(2,1)S(1)} %bitcast.12, ...), custom_call_target="tpu_custom_call" | custom-call | bytes 14407680 | tf_op jit(solution)/shard_map/pallas_call | solution.py:101
  48.9 11.0 %collective-permute-done.8.refs_0_ = bf16[1536,128]{1,0:T(8,128)(2,1)S(1)} collective-permute-done((bf16[1536,128]{1,0:T(8,128)(2,1)S(1)}, bf16[1536,128]{1,0:T(8,128)(2,1)S(1)}, u32[]{:S(2)}, u32[]{:S(2)}) %collective-permute-start.8) | collective-permute-done | bytes 393248 | tf_op jit(solution)/shard_map/ppermute | solution.py:58
  59.9 4.1 %shard_map.60 = (f32[1536,128]{1,0:T(8,128)S(1)}, bf16[1536,128]{1,0:T(8,128)(2,1)S(1)}) custom-call(bf16[1536,128]{1,0:T(8,128)(2,1)S(1)} %collective-permute-done.6.refs_0_, bf16[1536,128]{1,0:T(8,128)(2,1)S(1)} %collective-permute-done.9.refs_1_, bf16[2,360,2880]{2,1,0:T(8,128)(2,1)S(1)} %bitcast.13, ...), custom_call_target="tpu_custom_call" | custom-call | bytes 14407680 | tf_op jit(solution)/shard_map/pallas_call | solution.py:101
  66.6 5.4 %collective-permute-done.10.refs_1_ = bf16[1536,128]{1,0:T(8,128)(2,1)S(1)} collective-permute-done((bf16[1536,128]{1,0:T(8,128)(2,1)S(1)}, bf16[1536,128]{1,0:T(8,128)(2,1)S(1)}, u32[]{:S(2)}, u32[]{:S(2)}) %collective-permute-start.10) | collective-permute-done | bytes 393248 | tf_op jit(solution)/shard_map/ppermute | solution.py:58
  72.3 4.1 %shard_map.59 = (f32[1536,128]{1,0:T(8,128)S(1)}, bf16[1536,128]{1,0:T(8,128)(2,1)S(1)}) custom-call(bf16[1536,128]{1,0:T(8,128)(2,1)S(1)} %collective-permute-done.8.refs_0_, bf16[1536,128]{1,0:T(8,128)(2,1)S(1)} %collective-permute-done.10.refs_1_, bf16[2,360,2880]{2,1,0:T(8,128)(2,1)S(1)} %bitcast.14, ...), custom_call_target="tpu_custom_call" | custom-call | bytes 14407680 | tf_op jit(solution)/shard_map/pallas_call | solution.py:101
  76.4 4.0 %collective-permute-done.14.refs_1_ = bf16[1536,128]{1,0:T(8,128)(2,1)S(1)} collective-permute-done((bf16[1536,128]{1,0:T(8,128)(2,1)S(1)}, bf16[1536,128]{1,0:T(8,128)(2,1)S(1)}, u32[]{:S(2)}, u32[]{:S(2)}) %collective-permute-start.14) | collective-permute-done | bytes 393248 | tf_op jit(solution)/shard_map/ppermute | solution.py:58
  80.4 8.4 %collective-permute-done.11.refs_1_ = bf16[1536,128]{1,0:T(8,128)(2,1)S(1)} collective-permute-done((bf16[1536,128]{1,0:T(8,128)(2,1)S(1)}, bf16[1536,128]{1,0:T(8,128)(2,1)S(1)}, u32[]{:S(2)}, u32[]{:S(2)}) %collective-permute-start.11) | collective-permute-done | bytes 393248 | tf_op jit(solution)/shard_map/ppermute | solution.py:58
  88.8 4.1 %shard_map.58 = (f32[1536,128]{1,0:T(8,128)S(1)}, bf16[1536,128]{1,0:T(8,128)(2,1)S(1)}) custom-call(bf16[1536,128]{1,0:T(8,128)(2,1)S(1)} %collective-permute-done.7.refs_0_, bf16[1536,128]{1,0:T(8,128)(2,1)S(1)} %collective-permute-done.11.refs_1_, bf16[2,360,2880]{2,1,0:T(8,128)(2,1)S(1)} %bitcast.15, ...), custom_call_target="tpu_custom_call" | custom-call | bytes 14407680 | tf_op jit(solution)/shard_map/pallas_call | solution.py:101
  93.1 11.3 %collective-permute-start.21 = (bf16[1536,128]{1,0:T(8,128)(2,1)S(1)}, bf16[1536,128]{1,0:T(8,128)(2,1)S(1)}, u32[]{:S(2)}, u32[]{:S(2)}) collective-permute-start(bf16[1536,128]{1,0:T(8,128)(2,1)S(1)} %shard_map.65), channel_id=1, source_target_pairs={{0,2},{1,3},{2,4},{3,5},{4,6},{5,7},{6,0},{7,1},{8,10},{9,11},{10,... | collective-permute-start | bytes 1179656 | tf_op jit(solution)/shard_map/ppermute | solution.py:58
  107.0 4.1 %shard_map.64 = (f32[1536,128]{1,0:T(8,128)S(1)}, bf16[1536,128]{1,0:T(8,128)(2,1)S(1)}) custom-call(bf16[1536,128]{1,0:T(8,128)(2,1)S(1)} %collective-permute-done.19.refs_0_, bf16[1536,128]{1,0:T(8,128)(2,1)S(1)} %collective-permute-done.20.refs_1_, bf16[2,360,2880]{2,1,0:T(8,128)(2,1)S(1)} %bitcast.16, ...), custom_call_target="tpu_custom_call" | custom-call | bytes 14407680 | tf_op jit(solution)/shard_map/pallas_call | solution.py:101
  111.3 5.1 %collective-permute-done.16.refs_1_ = bf16[1536,128]{1,0:T(8,128)(2,1)S(1)} collective-permute-done((bf16[1536,128]{1,0:T(8,128)(2,1)S(1)}, bf16[1536,128]{1,0:T(8,128)(2,1)S(1)}, u32[]{:S(2)}, u32[]{:S(2)}) %collective-permute-start.16) | collective-permute-done | bytes 393248 | tf_op jit(solution)/shard_map/ppermute | solution.py:58
  117.1 8.0 %collective-permute-start.18 = (bf16[1536,128]{1,0:T(8,128)(2,1)S(1)}, bf16[1536,128]{1,0:T(8,128)(2,1)S(1)}, u32[]{:S(2)}, u32[]{:S(2)}) collective-permute-start(bf16[1536,128]{1,0:T(8,128)(2,1)S(1)} %shard_map.62), channel_id=1, source_target_pairs={{0,7},{1,6},{2,1},{3,0},{4,3},{5,2},{6,5},{7,4},{8,15},{9,14},{10,... | collective-permute-start | bytes 1179656 | tf_op jit(solution)/shard_map/ppermute | solution.py:58
  125.1 4.1 %shard_map.56 = (f32[1536,128]{1,0:T(8,128)S(1)}, bf16[1536,128]{1,0:T(8,128)(2,1)S(1)}) custom-call(bf16[1536,128]{1,0:T(8,128)(2,1)S(1)} %collective-permute-done.refs_0_, bf16[1536,128]{1,0:T(8,128)(2,1)S(1)} %collective-permute-done.1.refs_1_, bf16[2,360,2880]{2,1,0:T(8,128)(2,1)S(1)} %bitcast.17, ...), custom_call_target="tpu_custom_call" | custom-call | bytes 14407680 | tf_op jit(solution)/shard_map/pallas_call | solution.py:101
  129.1 4.1 %shard_map.68 = (f32[1536,128]{1,0:T(8,128)S(1)}, bf16[1536,128]{1,0:T(8,128)(2,1)S(1)}) custom-call(bf16[1536,128]{1,0:T(8,128)(2,1)S(1)} %collective-permute-done.22.refs_0_, bf16[1536,128]{1,0:T(8,128)(2,1)S(1)} %collective-permute-done.26.refs_1_, bf16[2,360,2880]{2,1,0:T(8,128)(2,1)S(1)} %bitcast.18, ...), custom_call_target="tpu_custom_call" | custom-call | bytes 14407680 | tf_op jit(solution)/shard_map/pallas_call | solution.py:101
  135.3 4.1 %shard_map.67 = (f32[1536,128]{1,0:T(8,128)S(1)}, bf16[1536,128]{1,0:T(8,128)(2,1)S(1)}) custom-call(bf16[1536,128]{1,0:T(8,128)(2,1)S(1)} %get-tuple-element.54.refs_0_, bf16[1536,128]{1,0:T(8,128)(2,1)S(1)} %collective-permute-done.2.refs_1_, bf16[2,360,2880]{2,1,0:T(8,128)(2,1)S(1)} %bitcast.19, bf16[2,360,2880]{2,1,0:T(8,128)(2,1)S(1)} %collective-permute-done.4.refs_3_, ...), custom_call_target="tpu_custom_call" | custom-call | bytes 14407680 | tf_op jit(solution)/shard_map/pallas_call | solution.py:101
  139.4 5.3 %collective-permute-done.28.refs_1_ = bf16[1536,128]{1,0:T(8,128)(2,1)S(1)} collective-permute-done((bf16[1536,128]{1,0:T(8,128)(2,1)S(1)}, bf16[1536,128]{1,0:T(8,128)(2,1)S(1)}, u32[]{:S(2)}, u32[]{:S(2)}) %collective-permute-start.28) | collective-permute-done | bytes 393248 | tf_op jit(solution)/shard_map/ppermute | solution.py:58
  145.1 4.4 %collective-permute-done.24.refs_1_ = bf16[1536,128]{1,0:T(8,128)(2,1)S(1)} collective-permute-done((bf16[1536,128]{1,0:T(8,128)(2,1)S(1)}, bf16[1536,128]{1,0:T(8,128)(2,1)S(1)}, u32[]{:S(2)}, u32[]{:S(2)}) %collective-permute-start.24) | collective-permute-done | bytes 393248 | tf_op jit(solution)/shard_map/ppermute | solution.py:58
  150.5 3.1 %collective-permute-done.29.refs_1_ = bf16[1536,128]{1,0:T(8,128)(2,1)S(1)} collective-permute-done((bf16[1536,128]{1,0:T(8,128)(2,1)S(1)}, bf16[1536,128]{1,0:T(8,128)(2,1)S(1)}, u32[]{:S(2)}, u32[]{:S(2)}) %collective-permute-start.29) | collective-permute-done | bytes 393248 | tf_op jit(solution)/shard_map/ppermute | solution.py:58
  155.5 7.6 %collective-permute-done.30.refs_4_ = bf16[1536,128]{1,0:T(8,128)(2,1)S(1)} collective-permute-done((bf16[1536,128]{1,0:T(8,128)(2,1)S(1)}, bf16[1536,128]{1,0:T(8,128)(2,1)S(1)}, u32[]{:S(2)}, u32[]{:S(2)}) %collective-permute-start.30) | collective-permute-done | bytes 393248 | tf_op jit(solution)/shard_map/ppermute | solution.py:58
  (86 shorter events, 36.0 us)
Async XLA Ops:
  3.2 12.1 %collective-permute-start.2 = (bf16[1536,128]{1,0:T(8,128)(2,1)S(1)}, bf16[1536,128]{1,0:T(8,128)(2,1)S(1)}, u32[]{:S(2)}, u32[]{:S(2)}) collective-permute-start(bf16[1536,128]{1,0:T(8,128)(2,1)S(1)} %get-tuple-element.54.refs_0_), channel_id=1, source_target_pairs={{0,16},{1,17},{2,18},{3,19},{4,20},{5,21},{6,22},{7,23},{8,24},{9,... | collective-permute-start | bytes 1179656 | tf_op jit(solution)/shard_map/ppermute | solution.py:58
  6.2 12.4 %collective-permute-start.3 = (bf16[1536,128]{1,0:T(8,128)(2,1)S(1)}, bf16[1536,128]{1,0:T(8,128)(2,1)S(1)}, u32[]{:S(2)}, u32[]{:S(2)}) collective-permute-start(bf16[1536,128]{1,0:T(8,128)(2,1)S(1)} %get-tuple-element.56), channel_id=1, source_target_pairs={{0,2},{1,3},{2,4},{3,5},{4,6},{5,7},{6,0},{7,1},{8,10},{9,11},{10,... | collective-permute-start | bytes 1179656 | tf_op jit(solution)/shard_map/ppermute | solution.py:58
  18.6 24.4 %collective-permute-start.4 = (bf16[2,360,2880]{2,1,0:T(8,128)(2,1)S(1)}, bf16[2,360,2880]{2,1,0:T(8,128)(2,1)S(1)}, u32[]{:S(2)}, u32[]{:S(2)}) collective-permute-start(bf16[2,360,2880]{2,1,0:T(8,128)(2,1)S(1)} %bitcast.11), channel_id=1, source_target_pairs={{0,8},{1,9},{2,10},{3,11},{4,12},{5,13},{6,14},{7,15},{8,0},{9,1},... | collective-permute-start | bytes 12441608 | tf_op jit(solution)/shard_map/ppermute | solution.py:58
  18.6 24.4 %collective-permute-start.5 = (bf16[360,2880]{1,0:T(8,128)(2,1)S(1)}, bf16[360,2880]{1,0:T(8,128)(2,1)S(1)}, u32[]{:S(2)}, u32[]{:S(2)}) collective-permute-start(bf16[360,2880]{1,0:T(8,128)(2,1)S(1)} %bitcast.20), channel_id=1, source_target_pairs={{0,8},{1,9},{2,10},{3,11},{4,12},{5,13},{6,14},{7,15},{8,0},{9,1},... | collective-permute-start | bytes 6220808 | tf_op jit(solution)/shard_map/ppermute | solution.py:58
  23.1 19.9 %collective-permute-start.12 = (bf16[1536,128]{1,0:T(8,128)(2,1)S(1)}, bf16[1536,128]{1,0:T(8,128)(2,1)S(1)}, u32[]{:S(2)}, u32[]{:S(2)}) collective-permute-start(bf16[1536,128]{1,0:T(8,128)(2,1)S(1)} %collective-permute-done.3.refs_0_), channel_id=1, source_target_pairs={{0,16},{1,17},{2,18},{3,19},{4,20},{5,21},{6,22},{7,23},{8,24},{9,... | collective-permute-start | bytes 1179656 | tf_op jit(solution)/shard_map/ppermute | solution.py:58
  31.9 28.0 %collective-permute-start.8 = (bf16[1536,128]{1,0:T(8,128)(2,1)S(1)}, bf16[1536,128]{1,0:T(8,128)(2,1)S(1)}, u32[]{:S(2)}, u32[]{:S(2)}) collective-permute-start(bf16[1536,128]{1,0:T(8,128)(2,1)S(1)} %get-tuple-element.65), channel_id=1, source_target_pairs={{0,4},{1,5},{2,6},{3,7},{4,0},{5,1},{6,2},{7,3},{8,12},{9,13},{10,... | collective-permute-start | bytes 1179656 | tf_op jit(solution)/shard_map/ppermute | solution.py:58
  34.6 25.3 %collective-permute-start.9 = (bf16[1536,128]{1,0:T(8,128)(2,1)S(1)}, bf16[1536,128]{1,0:T(8,128)(2,1)S(1)}, u32[]{:S(2)}, u32[]{:S(2)}) collective-permute-start(bf16[1536,128]{1,0:T(8,128)(2,1)S(1)} %collective-permute-done.6.refs_0_), channel_id=1, source_target_pairs={{0,16},{1,17},{2,18},{3,19},{4,20},{5,21},{6,22},{7,23},{8,24},{9,... | collective-permute-start | bytes 1179656 | tf_op jit(solution)/shard_map/ppermute | solution.py:58
  47.1 16.9 %collective-permute-start.13 = (bf16[1536,128]{1,0:T(8,128)(2,1)S(1)}, bf16[1536,128]{1,0:T(8,128)(2,1)S(1)}, u32[]{:S(2)}, u32[]{:S(2)}) collective-permute-start(bf16[1536,128]{1,0:T(8,128)(2,1)S(1)} %get-tuple-element.75), channel_id=1, source_target_pairs={{0,16},{1,17},{2,18},{3,19},{4,20},{5,21},{6,22},{7,23},{8,24},{9,... | collective-permute-start | bytes 1179656 | tf_op jit(solution)/shard_map/ppermute | solution.py:58
  47.7 18.9 %collective-permute-start.7 = (bf16[1536,128]{1,0:T(8,128)(2,1)S(1)}, bf16[1536,128]{1,0:T(8,128)(2,1)S(1)}, u32[]{:S(2)}, u32[]{:S(2)}) collective-permute-start(bf16[1536,128]{1,0:T(8,128)(2,1)S(1)} %get-tuple-element.63), channel_id=1, source_target_pairs={{0,3},{1,2},{2,5},{3,4},{4,7},{5,6},{6,1},{7,0},{8,11},{9,10},{10,... | collective-permute-start | bytes 1179656 | tf_op jit(solution)/shard_map/ppermute | solution.py:58
  64.0 16.4 %collective-permute-start.14 = (bf16[1536,128]{1,0:T(8,128)(2,1)S(1)}, bf16[1536,128]{1,0:T(8,128)(2,1)S(1)}, u32[]{:S(2)}, u32[]{:S(2)}) collective-permute-start(bf16[1536,128]{1,0:T(8,128)(2,1)S(1)} %get-tuple-element.76), channel_id=1, source_target_pairs={{0,16},{1,17},{2,18},{3,19},{4,20},{5,21},{6,22},{7,23},{8,24},{9,... | collective-permute-start | bytes 1179656 | tf_op jit(solution)/shard_map/ppermute | solution.py:58
  66.1 26.8 %collective-permute-start.19 = (bf16[1536,128]{1,0:T(8,128)(2,1)S(1)}, bf16[1536,128]{1,0:T(8,128)(2,1)S(1)}, u32[]{:S(2)}, u32[]{:S(2)}) collective-permute-start(bf16[1536,128]{1,0:T(8,128)(2,1)S(1)} %get-tuple-element.82), channel_id=1, source_target_pairs={{0,5},{1,4},{2,7},{3,6},{4,1},{5,0},{6,3},{7,2},{8,13},{9,12},{10,... | collective-permute-start | bytes 1179656 | tf_op jit(solution)/shard_map/ppermute | solution.py:58
  72.0 16.9 %collective-permute-start.11 = (bf16[1536,128]{1,0:T(8,128)(2,1)S(1)}, bf16[1536,128]{1,0:T(8,128)(2,1)S(1)}, u32[]{:S(2)}, u32[]{:S(2)}) collective-permute-start(bf16[1536,128]{1,0:T(8,128)(2,1)S(1)} %collective-permute-done.7.refs_0_), channel_id=1, source_target_pairs={{0,16},{1,17},{2,18},{3,19},{4,20},{5,21},{6,22},{7,23},{8,24},{9,... | collective-permute-start | bytes 1179656 | tf_op jit(solution)/shard_map/ppermute | solution.py:58
  72.1 20.9 %collective-permute-start.17 = (bf16[1536,128]{1,0:T(8,128)(2,1)S(1)}, bf16[1536,128]{1,0:T(8,128)(2,1)S(1)}, u32[]{:S(2)}, u32[]{:S(2)}) collective-permute-start(bf16[1536,128]{1,0:T(8,128)(2,1)S(1)} %shard_map.63), channel_id=1, source_target_pairs={{0,6},{1,7},{2,0},{3,1},{4,2},{5,3},{6,4},{7,5},{8,14},{9,15},{10,... | collective-permute-start | bytes 1179656 | tf_op jit(solution)/shard_map/ppermute | solution.py:58
  80.4 23.9 %collective-permute-start.15 = (bf16[1536,128]{1,0:T(8,128)(2,1)S(1)}, bf16[1536,128]{1,0:T(8,128)(2,1)S(1)}, u32[]{:S(2)}, u32[]{:S(2)}) collective-permute-start(bf16[1536,128]{1,0:T(8,128)(2,1)S(1)} %get-tuple-element.77), channel_id=1, source_target_pairs={{0,16},{1,17},{2,18},{3,19},{4,20},{5,21},{6,22},{7,23},{8,24},{9,... | collective-permute-start | bytes 1179656 | tf_op jit(solution)/shard_map/ppermute | solution.py:58
  80.4 25.0 %collective-permute-start.22 = (bf16[1536,128]{1,0:T(8,128)(2,1)S(1)}, bf16[1536,128]{1,0:T(8,128)(2,1)S(1)}, u32[]{:S(2)}, u32[]{:S(2)}) collective-permute-start(bf16[1536,128]{1,0:T(8,128)(2,1)S(1)} %get-tuple-element.87), channel_id=1, source_target_pairs={{0,7},{1,6},{2,1},{3,0},{4,3},{5,2},{6,5},{7,4},{8,15},{9,14},{10,... | collective-permute-start | bytes 1179656 | tf_op jit(solution)/shard_map/ppermute | solution.py:58
  92.9 12.8 %collective-permute-start.20 = (bf16[1536,128]{1,0:T(8,128)(2,1)S(1)}, bf16[1536,128]{1,0:T(8,128)(2,1)S(1)}, u32[]{:S(2)}, u32[]{:S(2)}) collective-permute-start(bf16[1536,128]{1,0:T(8,128)(2,1)S(1)} %collective-permute-done.19.refs_0_), channel_id=1, source_target_pairs={{0,16},{1,17},{2,18},{3,19},{4,20},{5,21},{6,22},{7,23},{8,24},{9,... | collective-permute-start | bytes 1179656 | tf_op jit(solution)/shard_map/ppermute | solution.py:58
  93.1 18.2 %collective-permute-start.21 = (bf16[1536,128]{1,0:T(8,128)(2,1)S(1)}, bf16[1536,128]{1,0:T(8,128)(2,1)S(1)}, u32[]{:S(2)}, u32[]{:S(2)}) collective-permute-start(bf16[1536,128]{1,0:T(8,128)(2,1)S(1)} %shard_map.65), channel_id=1, source_target_pairs={{0,2},{1,3},{2,4},{3,5},{4,6},{5,7},{6,0},{7,1},{8,10},{9,11},{10,... | collective-permute-start | bytes 1179656 | tf_op jit(solution)/shard_map/ppermute | solution.py:58
  105.4 27.9 %collective-permute-start.27 = (bf16[1536,128]{1,0:T(8,128)(2,1)S(1)}, bf16[1536,128]{1,0:T(8,128)(2,1)S(1)}, u32[]{:S(2)}, u32[]{:S(2)}) collective-permute-start(bf16[1536,128]{1,0:T(8,128)(2,1)S(1)} %shard_map.69), channel_id=1, source_target_pairs={{0,4},{1,5},{2,6},{3,7},{4,0},{5,1},{6,2},{7,3},{8,12},{9,13},{10,... | collective-permute-start | bytes 1179656 | tf_op jit(solution)/shard_map/ppermute | solution.py:58
  105.7 23.5 %collective-permute-start.26 = (bf16[1536,128]{1,0:T(8,128)(2,1)S(1)}, bf16[1536,128]{1,0:T(8,128)(2,1)S(1)}, u32[]{:S(2)}, u32[]{:S(2)}) collective-permute-start(bf16[1536,128]{1,0:T(8,128)(2,1)S(1)} %collective-permute-done.22.refs_0_), channel_id=1, source_target_pairs={{0,16},{1,17},{2,18},{3,19},{4,20},{5,21},{6,22},{7,23},{8,24},{9,... | collective-permute-start | bytes 1179656 | tf_op jit(solution)/shard_map/ppermute | solution.py:58
  116.4 17.4 %collective-permute-start.23 = (bf16[1536,128]{1,0:T(8,128)(2,1)S(1)}, bf16[1536,128]{1,0:T(8,128)(2,1)S(1)}, u32[]{:S(2)}, u32[]{:S(2)}) collective-permute-start(bf16[1536,128]{1,0:T(8,128)(2,1)S(1)} %get-tuple-element.88), channel_id=1, source_target_pairs={{0,16},{1,17},{2,18},{3,19},{4,20},{5,21},{6,22},{7,23},{8,24},{9,... | collective-permute-start | bytes 1179656 | tf_op jit(solution)/shard_map/ppermute | solution.py:58
  117.1 16.8 %collective-permute-start.18 = (bf16[1536,128]{1,0:T(8,128)(2,1)S(1)}, bf16[1536,128]{1,0:T(8,128)(2,1)S(1)}, u32[]{:S(2)}, u32[]{:S(2)}) collective-permute-start(bf16[1536,128]{1,0:T(8,128)(2,1)S(1)} %shard_map.62), channel_id=1, source_target_pairs={{0,7},{1,6},{2,1},{3,0},{4,3},{5,2},{6,5},{7,4},{8,15},{9,14},{10,... | collective-permute-start | bytes 1179656 | tf_op jit(solution)/shard_map/ppermute | solution.py:58
  133.8 15.7 %collective-permute-start.24 = (bf16[1536,128]{1,0:T(8,128)(2,1)S(1)}, bf16[1536,128]{1,0:T(8,128)(2,1)S(1)}, u32[]{:S(2)}, u32[]{:S(2)}) collective-permute-start(bf16[1536,128]{1,0:T(8,128)(2,1)S(1)} %get-tuple-element.89), channel_id=1, source_target_pairs={{0,16},{1,17},{2,18},{3,19},{4,20},{5,21},{6,22},{7,23},{8,24},{9,... | collective-permute-start | bytes 1179656 | tf_op jit(solution)/shard_map/ppermute | solution.py:58
  144.9 18.2 %collective-permute-start.30 = (bf16[1536,128]{1,0:T(8,128)(2,1)S(1)}, bf16[1536,128]{1,0:T(8,128)(2,1)S(1)}, u32[]{:S(2)}, u32[]{:S(2)}) collective-permute-start(bf16[1536,128]{1,0:T(8,128)(2,1)S(1)} %shard_map.71), channel_id=1, source_target_pairs={{0,5},{1,4},{2,7},{3,6},{4,1},{5,0},{6,3},{7,2},{8,13},{9,12},{10,... | collective-permute-start | bytes 1179656 | tf_op jit(solution)/shard_map/ppermute | solution.py:58
  149.5 16.4 %collective-permute-start.25 = (bf16[1536,128]{1,0:T(8,128)(2,1)S(1)}, bf16[1536,128]{1,0:T(8,128)(2,1)S(1)}, u32[]{:S(2)}, u32[]{:S(2)}) collective-permute-start(bf16[1536,128]{1,0:T(8,128)(2,1)S(1)} %shard_map.66), channel_id=1, source_target_pairs={{0,1},{1,0},{2,3},{3,2},{4,5},{5,4},{6,7},{7,6},{8,9},{9,8},{10,11... | collective-permute-start | bytes 1179656 | tf_op jit(solution)/shard_map/ppermute | solution.py:58
  (12 other events, 136.8 us)

commit v7 on v6

--- a/solution.py
+++ b/solution.py
@@ -9,7 +9,7 @@
 
 clamp_limit = 7.0
 AXES = ("dp", "expert")
-VMEM_LIMIT = 20 * 1024 * 1024
+VMEM_LIMIT = 14 * 1024 * 1024
 F32, BF16 = jnp.float32, jnp.bfloat16
 PARAMS = {'far': [2, 6, 4, 3, 5, 7],
  'far_in': 2,

time: 168 us -> 168 us (level)
  no operation moved by 1% of the time
where the time goes in v7:
time: 168 us; the launch traced here: 167 us
  waiting for transfers between devices  80.5 us (48%)
  starting transfers between devices  42.6 us (25%)
  Pallas kernels  39 us (23%)
  local copies, waits for them, and re-layouts  3.82 us (2%)
    ppermute x32, waiting for transfers between devices, sent_to(): return lax.ppermute(array, AXES, pairs)  80.5 us
    ppermute x32, starting transfers between devices, sent_to(): return lax.ppermute(array, AXES, pairs)  42.6 us
    pallas_call x20, Pallas kernels, call_kernel(): pl.pallas_call(body, out_shape=out_shapes, in_specs=[pl.BlockSpec(memory_...  39 us
    unnamed x14, local copies, waits for them, and re-layouts  3.81 us
  transfers between devices with their start and end apart: 32, of which 18 were waited for; matrix products, arithmetic and copies ran while one was open for 2% of the time, Pallas kernels for 22%

profile of v7, /device:TPU:0, one launch (start us, length us, event | category | flops | bytes accessed | tf_op | source)
XLA Modules:
  0.0 167.4 jit_solution(16219121154460864452)
XLA Ops:
  3.2 3.0 %collective-permute-start.2 = (bf16[1536,128]{1,0:T(8,128)(2,1)S(1)}, bf16[1536,128]{1,0:T(8,128)(2,1)S(1)}, u32[]{:S(2)}, u32[]{:S(2)}) collective-permute-start(bf16[1536,128]{1,0:T(8,128)(2,1)S(1)} %get-tuple-element.54.refs_0_), channel_id=1, source_target_pairs={{0,16},{1,17},{2,18},{3,19},{4,20},{5,21},{6,22},{7,23},{8,24},{9,... | collective-permute-start | bytes 1179656 | tf_op jit(solution)/shard_map/ppermute | solution.py:58
  11.9 3.4 %collective-permute-done.2.refs_1_ = bf16[1536,128]{1,0:T(8,128)(2,1)S(1)} collective-permute-done((bf16[1536,128]{1,0:T(8,128)(2,1)S(1)}, bf16[1536,128]{1,0:T(8,128)(2,1)S(1)}, u32[]{:S(2)}, u32[]{:S(2)}) %collective-permute-start.2) | collective-permute-done | bytes 393248 | tf_op jit(solution)/shard_map/ppermute | solution.py:58
  15.3 3.3 %collective-permute-done.3.refs_0_ = bf16[1536,128]{1,0:T(8,128)(2,1)S(1)} collective-permute-done((bf16[1536,128]{1,0:T(8,128)(2,1)S(1)}, bf16[1536,128]{1,0:T(8,128)(2,1)S(1)}, u32[]{:S(2)}, u32[]{:S(2)}) %collective-permute-start.3) | collective-permute-done | bytes 393248 | tf_op jit(solution)/shard_map/ppermute | solution.py:58
  24.6 7.3 %collective-permute-done.6.refs_0_ = bf16[1536,128]{1,0:T(8,128)(2,1)S(1)} collective-permute-done((bf16[1536,128]{1,0:T(8,128)(2,1)S(1)}, bf16[1536,128]{1,0:T(8,128)(2,1)S(1)}, u32[]{:S(2)}, u32[]{:S(2)}) %collective-permute-start.6) | collective-permute-done | bytes 393248 | tf_op jit(solution)/shard_map/ppermute | solution.py:58
  35.1 7.9 %collective-permute-done.12.refs_1_ = bf16[1536,128]{1,0:T(8,128)(2,1)S(1)} collective-permute-done((bf16[1536,128]{1,0:T(8,128)(2,1)S(1)}, bf16[1536,128]{1,0:T(8,128)(2,1)S(1)}, u32[]{:S(2)}, u32[]{:S(2)}) %collective-permute-start.12) | collective-permute-done | bytes 393248 | tf_op jit(solution)/shard_map/ppermute | solution.py:58
  43.0 4.1 %shard_map.61 = (f32[1536,128]{1,0:T(8,128)S(1)}, bf16[1536,128]{1,0:T(8,128)(2,1)S(1)}) custom-call(bf16[1536,128]{1,0:T(8,128)(2,1)S(1)} %collective-permute-done.3.refs_0_, bf16[1536,128]{1,0:T(8,128)(2,1)S(1)} %collective-permute-done.12.refs_1_, bf16[2,360,2880]{2,1,0:T(8,128)(2,1)S(1)} %bitcast.12, ...), custom_call_target="tpu_custom_call" | custom-call | bytes 14407680 | tf_op jit(solution)/shard_map/pallas_call | solution.py:101
  48.9 11.0 %collective-permute-done.8.refs_0_ = bf16[1536,128]{1,0:T(8,128)(2,1)S(1)} collective-permute-done((bf16[1536,128]{1,0:T(8,128)(2,1)S(1)}, bf16[1536,128]{1,0:T(8,128)(2,1)S(1)}, u32[]{:S(2)}, u32[]{:S(2)}) %collective-permute-start.8) | collective-permute-done | bytes 393248 | tf_op jit(solution)/shard_map/ppermute | solution.py:58
  59.9 4.1 %shard_map.60 = (f32[1536,128]{1,0:T(8,128)S(1)}, bf16[1536,128]{1,0:T(8,128)(2,1)S(1)}) custom-call(bf16[1536,128]{1,0:T(8,128)(2,1)S(1)} %collective-permute-done.6.refs_0_, bf16[1536,128]{1,0:T(8,128)(2,1)S(1)} %collective-permute-done.9.refs_1_, bf16[2,360,2880]{2,1,0:T(8,128)(2,1)S(1)} %bitcast.13, ...), custom_call_target="tpu_custom_call" | custom-call | bytes 14407680 | tf_op jit(solution)/shard_map/pallas_call | solution.py:101
  66.6 5.4 %collective-permute-done.10.refs_1_ = bf16[1536,128]{1,0:T(8,128)(2,1)S(1)} collective-permute-done((bf16[1536,128]{1,0:T(8,128)(2,1)S(1)}, bf16[1536,128]{1,0:T(8,128)(2,1)S(1)}, u32[]{:S(2)}, u32[]{:S(2)}) %collective-permute-start.10) | collective-permute-done | bytes 393248 | tf_op jit(solution)/shard_map/ppermute | solution.py:58
  72.3 4.1 %shard_map.59 = (f32[1536,128]{1,0:T(8,128)S(1)}, bf16[1536,128]{1,0:T(8,128)(2,1)S(1)}) custom-call(bf16[1536,128]{1,0:T(8,128)(2,1)S(1)} %collective-permute-done.8.refs_0_, bf16[1536,128]{1,0:T(8,128)(2,1)S(1)} %collective-permute-done.10.refs_1_, bf16[2,360,2880]{2,1,0:T(8,128)(2,1)S(1)} %bitcast.14, ...), custom_call_target="tpu_custom_call" | custom-call | bytes 14407680 | tf_op jit(solution)/shard_map/pallas_call | solution.py:101
  76.4 4.0 %collective-permute-done.14.refs_1_ = bf16[1536,128]{1,0:T(8,128)(2,1)S(1)} collective-permute-done((bf16[1536,128]{1,0:T(8,128)(2,1)S(1)}, bf16[1536,128]{1,0:T(8,128)(2,1)S(1)}, u32[]{:S(2)}, u32[]{:S(2)}) %collective-permute-start.14) | collective-permute-done | bytes 393248 | tf_op jit(solution)/shard_map/ppermute | solution.py:58
  80.4 8.4 %collective-permute-done.11.refs_1_ = bf16[1536,128]{1,0:T(8,128)(2,1)S(1)} collective-permute-done((bf16[1536,128]{1,0:T(8,128)(2,1)S(1)}, bf16[1536,128]{1,0:T(8,128)(2,1)S(1)}, u32[]{:S(2)}, u32[]{:S(2)}) %collective-permute-start.11) | collective-permute-done | bytes 393248 | tf_op jit(solution)/shard_map/ppermute | solution.py:58
  88.8 4.1 %shard_map.58 = (f32[1536,128]{1,0:T(8,128)S(1)}, bf16[1536,128]{1,0:T(8,128)(2,1)S(1)}) custom-call(bf16[1536,128]{1,0:T(8,128)(2,1)S(1)} %collective-permute-done.7.refs_0_, bf16[1536,128]{1,0:T(8,128)(2,1)S(1)} %collective-permute-done.11.refs_1_, bf16[2,360,2880]{2,1,0:T(8,128)(2,1)S(1)} %bitcast.15, ...), custom_call_target="tpu_custom_call" | custom-call | bytes 14407680 | tf_op jit(solution)/shard_map/pallas_call | solution.py:101
  93.1 11.3 %collective-permute-start.21 = (bf16[1536,128]{1,0:T(8,128)(2,1)S(1)}, bf16[1536,128]{1,0:T(8,128)(2,1)S(1)}, u32[]{:S(2)}, u32[]{:S(2)}) collective-permute-start(bf16[1536,128]{1,0:T(8,128)(2,1)S(1)} %shard_map.65), channel_id=1, source_target_pairs={{0,2},{1,3},{2,4},{3,5},{4,6},{5,7},{6,0},{7,1},{8,10},{9,11},{10,... | collective-permute-start | bytes 1179656 | tf_op jit(solution)/shard_map/ppermute | solution.py:58
  107.0 4.1 %shard_map.64 = (f32[1536,128]{1,0:T(8,128)S(1)}, bf16[1536,128]{1,0:T(8,128)(2,1)S(1)}) custom-call(bf16[1536,128]{1,0:T(8,128)(2,1)S(1)} %collective-permute-done.19.refs_0_, bf16[1536,128]{1,0:T(8,128)(2,1)S(1)} %collective-permute-done.20.refs_1_, bf16[2,360,2880]{2,1,0:T(8,128)(2,1)S(1)} %bitcast.16, ...), custom_call_target="tpu_custom_call" | custom-call | bytes 14407680 | tf_op jit(solution)/shard_map/pallas_call | solution.py:101
  111.3 5.1 %collective-permute-done.16.refs_1_ = bf16[1536,128]{1,0:T(8,128)(2,1)S(1)} collective-permute-done((bf16[1536,128]{1,0:T(8,128)(2,1)S(1)}, bf16[1536,128]{1,0:T(8,128)(2,1)S(1)}, u32[]{:S(2)}, u32[]{:S(2)}) %collective-permute-start.16) | collective-permute-done | bytes 393248 | tf_op jit(solution)/shard_map/ppermute | solution.py:58
  117.1 8.0 %collective-permute-start.18 = (bf16[1536,128]{1,0:T(8,128)(2,1)S(1)}, bf16[1536,128]{1,0:T(8,128)(2,1)S(1)}, u32[]{:S(2)}, u32[]{:S(2)}) collective-permute-start(bf16[1536,128]{1,0:T(8,128)(2,1)S(1)} %shard_map.62), channel_id=1, source_target_pairs={{0,7},{1,6},{2,1},{3,0},{4,3},{5,2},{6,5},{7,4},{8,15},{9,14},{10,... | collective-permute-start | bytes 1179656 | tf_op jit(solution)/shard_map/ppermute | solution.py:58
  125.1 4.1 %shard_map.56 = (f32[1536,128]{1,0:T(8,128)S(1)}, bf16[1536,128]{1,0:T(8,128)(2,1)S(1)}) custom-call(bf16[1536,128]{1,0:T(8,128)(2,1)S(1)} %collective-permute-done.refs_0_, bf16[1536,128]{1,0:T(8,128)(2,1)S(1)} %collective-permute-done.1.refs_1_, bf16[2,360,2880]{2,1,0:T(8,128)(2,1)S(1)} %bitcast.17, ...), custom_call_target="tpu_custom_call" | custom-call | bytes 14407680 | tf_op jit(solution)/shard_map/pallas_call | solution.py:101
  129.1 4.1 %shard_map.68 = (f32[1536,128]{1,0:T(8,128)S(1)}, bf16[1536,128]{1,0:T(8,128)(2,1)S(1)}) custom-call(bf16[1536,128]{1,0:T(8,128)(2,1)S(1)} %collective-permute-done.22.refs_0_, bf16[1536,128]{1,0:T(8,128)(2,1)S(1)} %collective-permute-done.26.refs_1_, bf16[2,360,2880]{2,1,0:T(8,128)(2,1)S(1)} %bitcast.18, ...), custom_call_target="tpu_custom_call" | custom-call | bytes 14407680 | tf_op jit(solution)/shard_map/pallas_call | solution.py:101
  135.3 4.1 %shard_map.67 = (f32[1536,128]{1,0:T(8,128)S(1)}, bf16[1536,128]{1,0:T(8,128)(2,1)S(1)}) custom-call(bf16[1536,128]{1,0:T(8,128)(2,1)S(1)} %get-tuple-element.54.refs_0_, bf16[1536,128]{1,0:T(8,128)(2,1)S(1)} %collective-permute-done.2.refs_1_, bf16[2,360,2880]{2,1,0:T(8,128)(2,1)S(1)} %bitcast.19, bf16[2,360,2880]{2,1,0:T(8,128)(2,1)S(1)} %collective-permute-done.4.refs_3_, ...), custom_call_target="tpu_custom_call" | custom-call | bytes 14407680 | tf_op jit(solution)/shard_map/pallas_call | solution.py:101
  139.4 5.3 %collective-permute-done.28.refs_1_ = bf16[1536,128]{1,0:T(8,128)(2,1)S(1)} collective-permute-done((bf16[1536,128]{1,0:T(8,128)(2,1)S(1)}, bf16[1536,128]{1,0:T(8,128)(2,1)S(1)}, u32[]{:S(2)}, u32[]{:S(2)}) %collective-permute-start.28) | collective-permute-done | bytes 393248 | tf_op jit(solution)/shard_map/ppermute | solution.py:58
  145.1 4.4 %collective-permute-done.24.refs_1_ = bf16[1536,128]{1,0:T(8,128)(2,1)S(1)} collective-permute-done((bf16[1536,128]{1,0:T(8,128)(2,1)S(1)}, bf16[1536,128]{1,0:T(8,128)(2,1)S(1)}, u32[]{:S(2)}, u32[]{:S(2)}) %collective-permute-start.24) | collective-permute-done | bytes 393248 | tf_op jit(solution)/shard_map/ppermute | solution.py:58
  150.5 3.1 %collective-permute-done.29.refs_1_ = bf16[1536,128]{1,0:T(8,128)(2,1)S(1)} collective-permute-done((bf16[1536,128]{1,0:T(8,128)(2,1)S(1)}, bf16[1536,128]{1,0:T(8,128)(2,1)S(1)}, u32[]{:S(2)}, u32[]{:S(2)}) %collective-permute-start.29) | collective-permute-done | bytes 393248 | tf_op jit(solution)/shard_map/ppermute | solution.py:58
  155.5 7.6 %collective-permute-done.30.refs_4_ = bf16[1536,128]{1,0:T(8,128)(2,1)S(1)} collective-permute-done((bf16[1536,128]{1,0:T(8,128)(2,1)S(1)}, bf16[1536,128]{1,0:T(8,128)(2,1)S(1)}, u32[]{:S(2)}, u32[]{:S(2)}) %collective-permute-start.30) | collective-permute-done | bytes 393248 | tf_op jit(solution)/shard_map/ppermute | solution.py:58
  (86 shorter events, 36.0 us)
Async XLA Ops:
  3.2 12.1 %collective-permute-start.2 = (bf16[1536,128]{1,0:T(8,128)(2,1)S(1)}, bf16[1536,128]{1,0:T(8,128)(2,1)S(1)}, u32[]{:S(2)}, u32[]{:S(2)}) collective-permute-start(bf16[1536,128]{1,0:T(8,128)(2,1)S(1)} %get-tuple-element.54.refs_0_), channel_id=1, source_target_pairs={{0,16},{1,17},{2,18},{3,19},{4,20},{5,21},{6,22},{7,23},{8,24},{9,... | collective-permute-start | bytes 1179656 | tf_op jit(solution)/shard_map/ppermute | solution.py:58
  6.2 12.4 %collective-permute-start.3 = (bf16[1536,128]{1,0:T(8,128)(2,1)S(1)}, bf16[1536,128]{1,0:T(8,128)(2,1)S(1)}, u32[]{:S(2)}, u32[]{:S(2)}) collective-permute-start(bf16[1536,128]{1,0:T(8,128)(2,1)S(1)} %get-tuple-element.56), channel_id=1, source_target_pairs={{0,2},{1,3},{2,4},{3,5},{4,6},{5,7},{6,0},{7,1},{8,10},{9,11},{10,... | collective-permute-start | bytes 1179656 | tf_op jit(solution)/shard_map/ppermute | solution.py:58
  18.6 24.4 %collective-permute-start.4 = (bf16[2,360,2880]{2,1,0:T(8,128)(2,1)S(1)}, bf16[2,360,2880]{2,1,0:T(8,128)(2,1)S(1)}, u32[]{:S(2)}, u32[]{:S(2)}) collective-permute-start(bf16[2,360,2880]{2,1,0:T(8,128)(2,1)S(1)} %bitcast.11), channel_id=1, source_target_pairs={{0,8},{1,9},{2,10},{3,11},{4,12},{5,13},{6,14},{7,15},{8,0},{9,1},... | collective-permute-start | bytes 12441608 | tf_op jit(solution)/shard_map/ppermute | solution.py:58
  18.6 24.4 %collective-permute-start.5 = (bf16[360,2880]{1,0:T(8,128)(2,1)S(1)}, bf16[360,2880]{1,0:T(8,128)(2,1)S(1)}, u32[]{:S(2)}, u32[]{:S(2)}) collective-permute-start(bf16[360,2880]{1,0:T(8,128)(2,1)S(1)} %bitcast.20), channel_id=1, source_target_pairs={{0,8},{1,9},{2,10},{3,11},{4,12},{5,13},{6,14},{7,15},{8,0},{9,1},... | collective-permute-start | bytes 6220808 | tf_op jit(solution)/shard_map/ppermute | solution.py:58
  23.1 19.9 %collective-permute-start.12 = (bf16[1536,128]{1,0:T(8,128)(2,1)S(1)}, bf16[1536,128]{1,0:T(8,128)(2,1)S(1)}, u32[]{:S(2)}, u32[]{:S(2)}) collective-permute-start(bf16[1536,128]{1,0:T(8,128)(2,1)S(1)} %collective-permute-done.3.refs_0_), channel_id=1, source_target_pairs={{0,16},{1,17},{2,18},{3,19},{4,20},{5,21},{6,22},{7,23},{8,24},{9,... | collective-permute-start | bytes 1179656 | tf_op jit(solution)/shard_map/ppermute | solution.py:58
  31.9 28.0 %collective-permute-start.8 = (bf16[1536,128]{1,0:T(8,128)(2,1)S(1)}, bf16[1536,128]{1,0:T(8,128)(2,1)S(1)}, u32[]{:S(2)}, u32[]{:S(2)}) collective-permute-start(bf16[1536,128]{1,0:T(8,128)(2,1)S(1)} %get-tuple-element.65), channel_id=1, source_target_pairs={{0,4},{1,5},{2,6},{3,7},{4,0},{5,1},{6,2},{7,3},{8,12},{9,13},{10,... | collective-permute-start | bytes 1179656 | tf_op jit(solution)/shard_map/ppermute | solution.py:58
  34.6 25.3 %collective-permute-start.9 = (bf16[1536,128]{1,0:T(8,128)(2,1)S(1)}, bf16[1536,128]{1,0:T(8,128)(2,1)S(1)}, u32[]{:S(2)}, u32[]{:S(2)}) collective-permute-start(bf16[1536,128]{1,0:T(8,128)(2,1)S(1)} %collective-permute-done.6.refs_0_), channel_id=1, source_target_pairs={{0,16},{1,17},{2,18},{3,19},{4,20},{5,21},{6,22},{7,23},{8,24},{9,... | collective-permute-start | bytes 1179656 | tf_op jit(solution)/shard_map/ppermute | solution.py:58
  47.1 16.9 %collective-permute-start.13 = (bf16[1536,128]{1,0:T(8,128)(2,1)S(1)}, bf16[1536,128]{1,0:T(8,128)(2,1)S(1)}, u32[]{:S(2)}, u32[]{:S(2)}) collective-permute-start(bf16[1536,128]{1,0:T(8,128)(2,1)S(1)} %get-tuple-element.75), channel_id=1, source_target_pairs={{0,16},{1,17},{2,18},{3,19},{4,20},{5,21},{6,22},{7,23},{8,24},{9,... | collective-permute-start | bytes 1179656 | tf_op jit(solution)/shard_map/ppermute | solution.py:58
  47.7 18.9 %collective-permute-start.7 = (bf16[1536,128]{1,0:T(8,128)(2,1)S(1)}, bf16[1536,128]{1,0:T(8,128)(2,1)S(1)}, u32[]{:S(2)}, u32[]{:S(2)}) collective-permute-start(bf16[1536,128]{1,0:T(8,128)(2,1)S(1)} %get-tuple-element.63), channel_id=1, source_target_pairs={{0,3},{1,2},{2,5},{3,4},{4,7},{5,6},{6,1},{7,0},{8,11},{9,10},{10,... | collective-permute-start | bytes 1179656 | tf_op jit(solution)/shard_map/ppermute | solution.py:58
  64.0 16.4 %collective-permute-start.14 = (bf16[1536,128]{1,0:T(8,128)(2,1)S(1)}, bf16[1536,128]{1,0:T(8,128)(2,1)S(1)}, u32[]{:S(2)}, u32[]{:S(2)}) collective-permute-start(bf16[1536,128]{1,0:T(8,128)(2,1)S(1)} %get-tuple-element.76), channel_id=1, source_target_pairs={{0,16},{1,17},{2,18},{3,19},{4,20},{5,21},{6,22},{7,23},{8,24},{9,... | collective-permute-start | bytes 1179656 | tf_op jit(solution)/shard_map/ppermute | solution.py:58
  66.1 26.8 %collective-permute-start.19 = (bf16[1536,128]{1,0:T(8,128)(2,1)S(1)}, bf16[1536,128]{1,0:T(8,128)(2,1)S(1)}, u32[]{:S(2)}, u32[]{:S(2)}) collective-permute-start(bf16[1536,128]{1,0:T(8,128)(2,1)S(1)} %get-tuple-element.82), channel_id=1, source_target_pairs={{0,5},{1,4},{2,7},{3,6},{4,1},{5,0},{6,3},{7,2},{8,13},{9,12},{10,... | collective-permute-start | bytes 1179656 | tf_op jit(solution)/shard_map/ppermute | solution.py:58
  72.0 16.9 %collective-permute-start.11 = (bf16[1536,128]{1,0:T(8,128)(2,1)S(1)}, bf16[1536,128]{1,0:T(8,128)(2,1)S(1)}, u32[]{:S(2)}, u32[]{:S(2)}) collective-permute-start(bf16[1536,128]{1,0:T(8,128)(2,1)S(1)} %collective-permute-done.7.refs_0_), channel_id=1, source_target_pairs={{0,16},{1,17},{2,18},{3,19},{4,20},{5,21},{6,22},{7,23},{8,24},{9,... | collective-permute-start | bytes 1179656 | tf_op jit(solution)/shard_map/ppermute | solution.py:58
  72.1 20.9 %collective-permute-start.17 = (bf16[1536,128]{1,0:T(8,128)(2,1)S(1)}, bf16[1536,128]{1,0:T(8,128)(2,1)S(1)}, u32[]{:S(2)}, u32[]{:S(2)}) collective-permute-start(bf16[1536,128]{1,0:T(8,128)(2,1)S(1)} %shard_map.63), channel_id=1, source_target_pairs={{0,6},{1,7},{2,0},{3,1},{4,2},{5,3},{6,4},{7,5},{8,14},{9,15},{10,... | collective-permute-start | bytes 1179656 | tf_op jit(solution)/shard_map/ppermute | solution.py:58
  80.4 23.9 %collective-permute-start.15 = (bf16[1536,128]{1,0:T(8,128)(2,1)S(1)}, bf16[1536,128]{1,0:T(8,128)(2,1)S(1)}, u32[]{:S(2)}, u32[]{:S(2)}) collective-permute-start(bf16[1536,128]{1,0:T(8,128)(2,1)S(1)} %get-tuple-element.77), channel_id=1, source_target_pairs={{0,16},{1,17},{2,18},{3,19},{4,20},{5,21},{6,22},{7,23},{8,24},{9,... | collective-permute-start | bytes 1179656 | tf_op jit(solution)/shard_map/ppermute | solution.py:58
  80.4 25.0 %collective-permute-start.22 = (bf16[1536,128]{1,0:T(8,128)(2,1)S(1)}, bf16[1536,128]{1,0:T(8,128)(2,1)S(1)}, u32[]{:S(2)}, u32[]{:S(2)}) collective-permute-start(bf16[1536,128]{1,0:T(8,128)(2,1)S(1)} %get-tuple-element.87), channel_id=1, source_target_pairs={{0,7},{1,6},{2,1},{3,0},{4,3},{5,2},{6,5},{7,4},{8,15},{9,14},{10,... | collective-permute-start | bytes 1179656 | tf_op jit(solution)/shard_map/ppermute | solution.py:58
  92.9 12.8 %collective-permute-start.20 = (bf16[1536,128]{1,0:T(8,128)(2,1)S(1)}, bf16[1536,128]{1,0:T(8,128)(2,1)S(1)}, u32[]{:S(2)}, u32[]{:S(2)}) collective-permute-start(bf16[1536,128]{1,0:T(8,128)(2,1)S(1)} %collective-permute-done.19.refs_0_), channel_id=1, source_target_pairs={{0,16},{1,17},{2,18},{3,19},{4,20},{5,21},{6,22},{7,23},{8,24},{9,... | collective-permute-start | bytes 1179656 | tf_op jit(solution)/shard_map/ppermute | solution.py:58
  93.1 18.2 %collective-permute-start.21 = (bf16[1536,128]{1,0:T(8,128)(2,1)S(1)}, bf16[1536,128]{1,0:T(8,128)(2,1)S(1)}, u32[]{:S(2)}, u32[]{:S(2)}) collective-permute-start(bf16[1536,128]{1,0:T(8,128)(2,1)S(1)} %shard_map.65), channel_id=1, source_target_pairs={{0,2},{1,3},{2,4},{3,5},{4,6},{5,7},{6,0},{7,1},{8,10},{9,11},{10,... | collective-permute-start | bytes 1179656 | tf_op jit(solution)/shard_map/ppermute | solution.py:58
  105.4 27.9 %collective-permute-start.27 = (bf16[1536,128]{1,0:T(8,128)(2,1)S(1)}, bf16[1536,128]{1,0:T(8,128)(2,1)S(1)}, u32[]{:S(2)}, u32[]{:S(2)}) collective-permute-start(bf16[1536,128]{1,0:T(8,128)(2,1)S(1)} %shard_map.69), channel_id=1, source_target_pairs={{0,4},{1,5},{2,6},{3,7},{4,0},{5,1},{6,2},{7,3},{8,12},{9,13},{10,... | collective-permute-start | bytes 1179656 | tf_op jit(solution)/shard_map/ppermute | solution.py:58
  105.7 23.5 %collective-permute-start.26 = (bf16[1536,128]{1,0:T(8,128)(2,1)S(1)}, bf16[1536,128]{1,0:T(8,128)(2,1)S(1)}, u32[]{:S(2)}, u32[]{:S(2)}) collective-permute-start(bf16[1536,128]{1,0:T(8,128)(2,1)S(1)} %collective-permute-done.22.refs_0_), channel_id=1, source_target_pairs={{0,16},{1,17},{2,18},{3,19},{4,20},{5,21},{6,22},{7,23},{8,24},{9,... | collective-permute-start | bytes 1179656 | tf_op jit(solution)/shard_map/ppermute | solution.py:58
  116.4 17.4 %collective-permute-start.23 = (bf16[1536,128]{1,0:T(8,128)(2,1)S(1)}, bf16[1536,128]{1,0:T(8,128)(2,1)S(1)}, u32[]{:S(2)}, u32[]{:S(2)}) collective-permute-start(bf16[1536,128]{1,0:T(8,128)(2,1)S(1)} %get-tuple-element.88), channel_id=1, source_target_pairs={{0,16},{1,17},{2,18},{3,19},{4,20},{5,21},{6,22},{7,23},{8,24},{9,... | collective-permute-start | bytes 1179656 | tf_op jit(solution)/shard_map/ppermute | solution.py:58
  117.1 16.8 %collective-permute-start.18 = (bf16[1536,128]{1,0:T(8,128)(2,1)S(1)}, bf16[1536,128]{1,0:T(8,128)(2,1)S(1)}, u32[]{:S(2)}, u32[]{:S(2)}) collective-permute-start(bf16[1536,128]{1,0:T(8,128)(2,1)S(1)} %shard_map.62), channel_id=1, source_target_pairs={{0,7},{1,6},{2,1},{3,0},{4,3},{5,2},{6,5},{7,4},{8,15},{9,14},{10,... | collective-permute-start | bytes 1179656 | tf_op jit(solution)/shard_map/ppermute | solution.py:58
  133.8 15.7 %collective-permute-start.24 = (bf16[1536,128]{1,0:T(8,128)(2,1)S(1)}, bf16[1536,128]{1,0:T(8,128)(2,1)S(1)}, u32[]{:S(2)}, u32[]{:S(2)}) collective-permute-start(bf16[1536,128]{1,0:T(8,128)(2,1)S(1)} %get-tuple-element.89), channel_id=1, source_target_pairs={{0,16},{1,17},{2,18},{3,19},{4,20},{5,21},{6,22},{7,23},{8,24},{9,... | collective-permute-start | bytes 1179656 | tf_op jit(solution)/shard_map/ppermute | solution.py:58
  144.9 18.2 %collective-permute-start.30 = (bf16[1536,128]{1,0:T(8,128)(2,1)S(1)}, bf16[1536,128]{1,0:T(8,128)(2,1)S(1)}, u32[]{:S(2)}, u32[]{:S(2)}) collective-permute-start(bf16[1536,128]{1,0:T(8,128)(2,1)S(1)} %shard_map.71), channel_id=1, source_target_pairs={{0,5},{1,4},{2,7},{3,6},{4,1},{5,0},{6,3},{7,2},{8,13},{9,12},{10,... | collective-permute-start | bytes 1179656 | tf_op jit(solution)/shard_map/ppermute | solution.py:58
  149.5 16.4 %collective-permute-start.25 = (bf16[1536,128]{1,0:T(8,128)(2,1)S(1)}, bf16[1536,128]{1,0:T(8,128)(2,1)S(1)}, u32[]{:S(2)}, u32[]{:S(2)}) collective-permute-start(bf16[1536,128]{1,0:T(8,128)(2,1)S(1)} %shard_map.66), channel_id=1, source_target_pairs={{0,1},{1,0},{2,3},{3,2},{4,5},{5,4},{6,7},{7,6},{8,9},{9,8},{10,11... | collective-permute-start | bytes 1179656 | tf_op jit(solution)/shard_map/ppermute | solution.py:58
  (12 other events, 136.8 us)
